TPU v7x, 32 devices: a whole 2x2x4 slice. The times are simulated.
32 devices in a mesh: grp: 8 (over z, core), tm: 4 (over y, x).
Axes of the slice: x: 2, y: 2, z: 4, core: 2. Of those that a mesh axis runs over, the one named last changes fastest.
Arguments:
- features: bfloat16 [32, 1024, 1024], P('grp', 'tm'), may hold values from -40 to 40
- frame_counts: int32 [32], P('grp'), may hold values from 256 to 1024
- pool_query: bfloat16 [8, 1024], replicated, may hold values from -4 to 4
- w_proj: bfloat16 [1024, 512], replicated, may hold values from -0.1875 to 0.1875
- doc_embed: bfloat16 [512, 512], P(('grp', 'tm')), may hold values from -0.25 to 0.25
- doc_index: int32 [32], replicated, may hold values from 0 to 511
Outputs:
- loss: float32 [32], P('grp')
- speech_grad: float32 [32, 512], P('grp')
- doc_grad: float32 [512, 512], P(('grp', 'tm'))
All inputs are finite; a program needn't handle non-finite values.
Results may differ from a plain program's by a relative error of at most 0.0044.
Values may be sent and summed in bfloat16 or wider, within the bound.
No kernel may reach another device: no remote copies, remote signals or barrier semaphores. Data moves between devices by JAX's collectives and lax.ppermute only.
A program may use at most 64 MiB of HBM per device.

v0:
```python
import math

import jax
import jax.numpy as jnp
from jax import lax
from jax.sharding import PartitionSpec as P

logit_scale = 10.0
logit_shift = -8.0
norm_eps = 1e-06


def passed_along(value, axis, steps):
    count = lax.axis_size(axis)
    pairs = [(source, (source + steps) % count) for source in range(count)]
    return lax.ppermute(value, axis, pairs)


def pair_tile(speech_rows, rec_start, doc_rows, doc_start, doc_index):
    row_count = speech_rows.shape[0]
    logits = (
        logit_scale * jnp.dot(speech_rows, doc_rows.T, preferred_element_type=jnp.float32)
        + logit_shift
    )
    targets = lax.dynamic_slice_in_dim(doc_index, rec_start, row_count)
    doc_ids = doc_start + jnp.arange(doc_rows.shape[0], dtype=jnp.int32)
    labels = jnp.where(targets[:, None] == doc_ids[None, :], 1.0, -1.0)
    losses = jnp.sum(jax.nn.softplus(-labels * logits), axis=1)
    grad_b = (-labels * jax.nn.sigmoid(-labels * logits)).astype(jnp.bfloat16)
    speech_part = logit_scale * jnp.dot(grad_b, doc_rows, preferred_element_type=jnp.float32)
    doc_part = logit_scale * jnp.dot(grad_b.T, speech_rows, preferred_element_type=jnp.float32)
    return (losses, speech_part, doc_part)


def body(features, frame_counts, pool_query, w_proj, doc_embed, doc_index):
    rec_count, frame_dev, channels = features.shape
    width = w_proj.shape[1]
    heads = pool_query.shape[0]
    doc_dev = doc_embed.shape[0]
    values = jnp.dot(
        features.reshape(rec_count * frame_dev, channels),
        w_proj,
        preferred_element_type=jnp.float32,
    ).astype(jnp.bfloat16)
    values = values.reshape(rec_count, frame_dev, heads, width // heads)
    scores = jnp.einsum(
        "rfc,hc->rhf", features, pool_query, preferred_element_type=jnp.float32
    ) / math.sqrt(channels)
    positions = lax.axis_index("tm") * frame_dev + jnp.arange(frame_dev, dtype=jnp.int32)
    valid = (positions[None, :] < frame_counts[:, None])[:, None, :]
    masked = jnp.where(valid, scores, -1e30)
    peak_score = lax.pmax(jnp.max(masked, axis=2), "tm")
    weights = jnp.where(valid, jnp.exp(masked - peak_score[:, :, None]), 0.0)
    totals = jnp.sum(weights, axis=2)
    numerator = jnp.einsum(
        "rhf,rfhd->rhd", weights.astype(jnp.bfloat16), values, preferred_element_type=jnp.float32
    )
    numerator, totals = lax.psum((numerator, totals), "tm")
    pooled = (numerator / totals[:, :, None]).reshape(rec_count, width)
    speech = (
        pooled * lax.rsqrt(jnp.sum(pooled * pooled, axis=1, keepdims=True) + norm_eps)
    ).astype(jnp.bfloat16)
    group = lax.axis_index("grp")
    column = lax.axis_index("tm")
    group_count = lax.axis_size("grp")
    column_count = lax.axis_size("tm")
    loss_zero = jnp.zeros((rec_count,), jnp.float32)
    speech_zero = jnp.zeros((rec_count, width), jnp.float32)
    doc_zero = jnp.zeros((doc_dev, width), jnp.float32)

    def advance_docs(turn, state_tuple):
        blocks, grads, losses, speech_acc = state_tuple
        source = (group - turn) % group_count
        loss_rows, speech_part, doc_part = pair_tile(
            speech, group * rec_count, blocks, (source * column_count + column) * doc_dev, doc_index
        )
        blocks = passed_along(blocks, "grp", 1)
        grads = passed_along(grads + doc_part, "grp", 1)
        return (blocks, grads, losses + loss_rows, speech_acc + speech_part)

    final_state = lax.fori_loop(
        0, group_count, advance_docs, (doc_embed, doc_zero, loss_zero, speech_zero)
    )
    doc_grad = final_state[1]
    loss_part = final_state[2]
    speech_part_sum = final_state[3]
    speech_grad, loss = lax.psum((speech_part_sum, loss_part), "tm")
    return (loss, speech_grad, doc_grad)


def solution(mesh):
    placed = (P("grp", "tm", None), P("grp"), P(), P(), P(("grp", "tm"), None), P())
    return jax.shard_map(
        body,
        mesh=mesh,
        in_specs=placed,
        out_specs=(P("grp"), P("grp", None), P(("grp", "tm"), None)),
        check_vma=False,
    )
```

profile of v0, /device:TPU:0, one launch (start us, length us, event | category | flops | bytes accessed | tf_op | source)
XLA Modules:
  0.0 92.5 jit_solution(10944215307295022520)
XLA Ops:
  0.6 0.0 copy-start
  0.7 0.9 broadcast_compare_fusion
  1.5 0.7 copy-done
  2.2 1.4 %fusion.18 = (f32[4,8]{1,0:T(4,128)S(1)}, f32[4,8,256]{2,1,0:T(8,128)S(1)}) fusion(bf16[4,256,1024]{2,1,0:T(8,128)(2,1)S(1)} %copy-done, bf16[8,1024]{1,0:T(8,128)(2,1)} %param.10, pred[4,256]{1,0:T(4,128)(4,1)S(1)} %broadcast_compare_fusion), kind=kOutput, calls=%fused_computation.33 | convolution fusion | flops 16801760 | bytes 2147456 | tf_op jit(solution)/shard_map/rfc,hc->rhf/dot_general | solution.py:46
  3.7 11.3 %pmax.7 = f32[4,8]{1,0:T(4,128)S(1)} all-reduce(f32[4,8]{1,0:T(4,128)S(1)} %get-tuple-element.294), channel_id=1, replica_groups=mesh['grp'=8,'tm'=4] {'tm'}, use_global_device_ids=true, to_apply=%region_1.2 | all-reduce | flops 32 | bytes 256 | tf_op jit(solution)/shard_map/pmax | solution.py:52
  15.0 0.2 fusion.14
  15.2 2.5 %convolution_convert_fusion = bf16[1024,512]{1,0:T(8,128)(2,1)S(1)} fusion(bf16[1024,1024]{1,0:T(8,128)(2,1)S(1)} %bitcast.27, bf16[1024,512]{1,0:T(8,128)(2,1)} %param.11), kind=kOutput, calls=%fused_computation.17 | convolution fusion | flops 1074266112 | bytes 4194304 | tf_op jit(solution)/shard_map/dot_general | solution.py:40
  17.7 0.0 copy-start.2
  17.7 0.0 copy-start.1
  17.7 2.1 %reshape.61 = bf16[4,256,8,64]{3,2,1,0:T(8,128)(2,1)} reshape(bf16[1024,512]{1,0:T(8,128)(2,1)S(1)} %convolution_convert_fusion) | data formatting | bytes 2097152 | tf_op jit(solution)/shard_map/reshape | solution.py:45
  19.8 2.0 %fusion.9 = f32[4,8,1,64]{3,2,1,0:T(1,128)S(1)} fusion(bf16[4,256,8,64]{3,2,1,0:T(8,128)(2,1)} %reshape.61, bf16[4,8,256,1]{2,1,0,3:T(8,128)(2,1)S(1)} %get-tuple-element.293), kind=kOutput, calls=%fused_computation.15 | convolution fusion | flops 1048576 | bytes 1073152 | tf_op jit(solution)/shard_map/rhf,rfhd->rhd/dot_general | solution.py:55
  21.8 14.4 %all-reduce.1 = (f32[4,8,64]{2,1,0:T(8,128)S(1)}, f32[4,8]{1,0:T(4,128)S(1)}) all-reduce(f32[4,8,64]{2,1,0:T(8,128)S(1)} %bitcast.28, f32[4,8]{1,0:T(4,128)S(1)} %get-tuple-element.292), channel_id=1, replica_groups=mesh['grp'=8,'tm'=4] {'tm'}, use_global_device_ids=true, to_apply=%region_2.3 | all-reduce | flops 2080 | bytes 16640 | tf_op jit(solution)/shard_map/psum | solution.py:58
  36.1 0.2 multiply_reduce_fusion
  36.3 0.1 reshape.57
  36.4 0.1 multiply_convert_fusion
  36.5 0.1 dynamic_slice.9
  36.6 45.4 %while.22 = (s32[]{:T(128)}, bf16[16,512]{1,0:T(8,128)(2,1)S(1)}, f32[16,512]{1,0:T(8,128)S(1)}, f32[4]{0:T(128)S(1)}, f32[4,512]{1,0:T(4,128)S(1)}, /*index=5*/...) while((s32[]{:T(128)}, bf16[16,512]{1,0:T(8,128)(2,1)S(1)}, ...), condition=%wide.region_8.9_spmd.clone, body=%wide.region_6.8_spmd.clone.sunk | while | flops 221030 | bytes 353785 | solution.py:81
  36.6 0.1 collective-permute-start
  36.7 0.2 fusion.42
  37.0 0.3 fusion.43
  37.2 1.7 %collective-permute-start.1 = (f32[16,512]{1,0:T(8,128)S(1)}, f32[16,512]{1,0:T(8,128)S(1)}, u32[]{:S(2)}, u32[]{:S(2)}) collective-permute-start(f32[16,512]{1,0:T(8,128)S(1)} %fusion.43), channel_id=1, source_target_pairs={{0,4},{4,8},{8,12},{12,16},{16,20},{20,24},{24,28},{28,0},{1,5},{5... | collective-permute-start | bytes 98312 | tf_op jit(solution)/shard_map/while/body/eval_jaxpr/ppermute | solution.py:16
  38.9 0.2 fusion.45
  39.1 2.5 %collective-permute-done = bf16[16,512]{1,0:T(8,128)(2,1)S(1)} collective-permute-done((bf16[16,512]{1,0:T(8,128)(2,1)S(1)}, bf16[16,512]{1,0:T(8,128)(2,1)S(1)}, u32[]{:S(2)}, u32[]{:S(2)}) %collective-permute-start) | collective-permute-done | bytes 16416 | tf_op jit(solution)/shard_map/while/body/eval_jaxpr/ppermute | solution.py:16
  41.6 0.7 collective-permute-done.1
  42.4 0.2 fusion.42
  42.6 0.3 fusion.43
  42.9 0.2 fusion.45
  43.1 4.2 %collective-permute-done = bf16[16,512]{1,0:T(8,128)(2,1)S(1)} collective-permute-done((bf16[16,512]{1,0:T(8,128)(2,1)S(1)}, bf16[16,512]{1,0:T(8,128)(2,1)S(1)}, u32[]{:S(2)}, u32[]{:S(2)}) %collective-permute-start) | collective-permute-done | bytes 16416 | tf_op jit(solution)/shard_map/while/body/eval_jaxpr/ppermute | solution.py:16
  47.3 0.7 collective-permute-done.1
  48.0 0.2 fusion.42
  48.3 0.3 fusion.43
  48.5 0.0 collective-permute-start.1
  48.5 0.2 fusion.45
  48.8 4.2 %collective-permute-done = bf16[16,512]{1,0:T(8,128)(2,1)S(1)} collective-permute-done((bf16[16,512]{1,0:T(8,128)(2,1)S(1)}, bf16[16,512]{1,0:T(8,128)(2,1)S(1)}, u32[]{:S(2)}, u32[]{:S(2)}) %collective-permute-start) | collective-permute-done | bytes 16416 | tf_op jit(solution)/shard_map/while/body/eval_jaxpr/ppermute | solution.py:16
  53.0 0.7 collective-permute-done.1
  53.7 0.0 collective-permute-start
  53.7 0.2 fusion.42
  54.0 0.3 fusion.43
  54.2 0.0 collective-permute-start.1
  54.2 0.2 fusion.45
  54.4 4.2 %collective-permute-done = bf16[16,512]{1,0:T(8,128)(2,1)S(1)} collective-permute-done((bf16[16,512]{1,0:T(8,128)(2,1)S(1)}, bf16[16,512]{1,0:T(8,128)(2,1)S(1)}, u32[]{:S(2)}, u32[]{:S(2)}) %collective-permute-start) | collective-permute-done | bytes 16416 | tf_op jit(solution)/shard_map/while/body/eval_jaxpr/ppermute | solution.py:16
  58.7 0.7 collective-permute-done.1
  59.4 0.2 fusion.42
  59.6 0.3 fusion.43
  59.9 0.2 fusion.45
  60.1 4.2 %collective-permute-done = bf16[16,512]{1,0:T(8,128)(2,1)S(1)} collective-permute-done((bf16[16,512]{1,0:T(8,128)(2,1)S(1)}, bf16[16,512]{1,0:T(8,128)(2,1)S(1)}, u32[]{:S(2)}, u32[]{:S(2)}) %collective-permute-start) | collective-permute-done | bytes 16416 | tf_op jit(solution)/shard_map/while/body/eval_jaxpr/ppermute | solution.py:16
  64.3 0.7 collective-permute-done.1
  65.0 0.2 fusion.42
  65.3 0.3 fusion.43
  65.5 0.2 fusion.45
  65.8 4.2 %collective-permute-done = bf16[16,512]{1,0:T(8,128)(2,1)S(1)} collective-permute-done((bf16[16,512]{1,0:T(8,128)(2,1)S(1)}, bf16[16,512]{1,0:T(8,128)(2,1)S(1)}, u32[]{:S(2)}, u32[]{:S(2)}) %collective-permute-start) | collective-permute-done | bytes 16416 | tf_op jit(solution)/shard_map/while/body/eval_jaxpr/ppermute | solution.py:16
  70.0 0.7 collective-permute-done.1
  70.7 0.2 fusion.42
  71.0 0.3 fusion.43
  71.2 0.2 fusion.45
  71.4 4.2 %collective-permute-done = bf16[16,512]{1,0:T(8,128)(2,1)S(1)} collective-permute-done((bf16[16,512]{1,0:T(8,128)(2,1)S(1)}, bf16[16,512]{1,0:T(8,128)(2,1)S(1)}, u32[]{:S(2)}, u32[]{:S(2)}) %collective-permute-start) | collective-permute-done | bytes 16416 | tf_op jit(solution)/shard_map/while/body/eval_jaxpr/ppermute | solution.py:16
  75.7 0.7 collective-permute-done.1
  76.4 0.2 fusion.42
  76.6 0.3 fusion.43
  76.9 0.2 fusion.45
  77.1 4.2 %collective-permute-done = bf16[16,512]{1,0:T(8,128)(2,1)S(1)} collective-permute-done((bf16[16,512]{1,0:T(8,128)(2,1)S(1)}, bf16[16,512]{1,0:T(8,128)(2,1)S(1)}, u32[]{:S(2)}, u32[]{:S(2)}) %collective-permute-start) | collective-permute-done | bytes 16416 | tf_op jit(solution)/shard_map/while/body/eval_jaxpr/ppermute | solution.py:16
  81.3 0.7 collective-permute-done.1
  82.0 9.8 %all-reduce = (f32[4]{0:T(128)}, f32[4,512]{1,0:T(4,128)}) all-reduce(f32[4]{0:T(128)S(1)} %get-tuple-element.233, f32[4,512]{1,0:T(4,128)S(1)} %get-tuple-element.234), channel_id=1, replica_groups=mesh['grp'=8,'tm'=4] {'tm'}, use_global_device_ids=true, to_apply=%region_9.10 | all-reduce | flops 2052 | bytes 16416 | tf_op jit(solution)/shard_map/psum | solution.py:87
  91.8 0.6 copy.37
  (42 shorter events, 0.2 us)
Async XLA Ops:
  0.6 1.6 %copy-start = (bf16[4,256,1024]{2,1,0:T(8,128)(2,1)S(1)}, bf16[4,256,1024]{2,1,0:T(8,128)(2,1)}, u32[]{:S(2)}) copy-start(bf16[4,256,1024]{2,1,0:T(8,128)(2,1)} %param.8) | copy-start | bytes 6291460
  17.7 18.8 %copy-start.2 = (s32[32]{0:T(128)S(1)}, s32[32]{0:T(128)}, u32[]{:S(2)}) copy-start(s32[32]{0:T(128)} %param.13) | copy-start | bytes 388
  17.7 18.9 %copy-start.1 = (bf16[16,512]{1,0:T(8,128)(2,1)S(1)}, bf16[16,512]{1,0:T(8,128)(2,1)}, u32[]{:S(2)}) copy-start(bf16[16,512]{1,0:T(8,128)(2,1)} %param.12) | copy-start | bytes 49156
  36.6 5.0 %collective-permute-start = (bf16[16,512]{1,0:T(8,128)(2,1)S(1)}, bf16[16,512]{1,0:T(8,128)(2,1)S(1)}, u32[]{:S(2)}, u32[]{:S(2)}) collective-permute-start(bf16[16,512]{1,0:T(8,128)(2,1)S(1)} %copy.25), channel_id=1, source_target_pairs={{0,4},{4,8},{8,12},{12,16},{16,20},{20,24},{24,28},{28,0},{1,5},{5... | collective-permute-start | bytes 49160 | tf_op jit(solution)/shard_map/while/body/eval_jaxpr/ppermute | solution.py:16
  37.2 5.2 %collective-permute-start.1 = (f32[16,512]{1,0:T(8,128)S(1)}, f32[16,512]{1,0:T(8,128)S(1)}, u32[]{:S(2)}, u32[]{:S(2)}) collective-permute-start(f32[16,512]{1,0:T(8,128)S(1)} %fusion.43), channel_id=1, source_target_pairs={{0,4},{4,8},{8,12},{12,16},{16,20},{20,24},{24,28},{28,0},{1,5},{5... | collective-permute-start | bytes 98312 | tf_op jit(solution)/shard_map/while/body/eval_jaxpr/ppermute | solution.py:16
  42.4 5.0 %collective-permute-start = (bf16[16,512]{1,0:T(8,128)(2,1)S(1)}, bf16[16,512]{1,0:T(8,128)(2,1)S(1)}, u32[]{:S(2)}, u32[]{:S(2)}) collective-permute-start(bf16[16,512]{1,0:T(8,128)(2,1)S(1)} %copy.25), channel_id=1, source_target_pairs={{0,4},{4,8},{8,12},{12,16},{16,20},{20,24},{24,28},{28,0},{1,5},{5... | collective-permute-start | bytes 49160 | tf_op jit(solution)/shard_map/while/body/eval_jaxpr/ppermute | solution.py:16
  42.9 5.2 %collective-permute-start.1 = (f32[16,512]{1,0:T(8,128)S(1)}, f32[16,512]{1,0:T(8,128)S(1)}, u32[]{:S(2)}, u32[]{:S(2)}) collective-permute-start(f32[16,512]{1,0:T(8,128)S(1)} %fusion.43), channel_id=1, source_target_pairs={{0,4},{4,8},{8,12},{12,16},{16,20},{20,24},{24,28},{28,0},{1,5},{5... | collective-permute-start | bytes 98312 | tf_op jit(solution)/shard_map/while/body/eval_jaxpr/ppermute | solution.py:16
  48.0 5.0 %collective-permute-start = (bf16[16,512]{1,0:T(8,128)(2,1)S(1)}, bf16[16,512]{1,0:T(8,128)(2,1)S(1)}, u32[]{:S(2)}, u32[]{:S(2)}) collective-permute-start(bf16[16,512]{1,0:T(8,128)(2,1)S(1)} %copy.25), channel_id=1, source_target_pairs={{0,4},{4,8},{8,12},{12,16},{16,20},{20,24},{24,28},{28,0},{1,5},{5... | collective-permute-start | bytes 49160 | tf_op jit(solution)/shard_map/while/body/eval_jaxpr/ppermute | solution.py:16
  48.5 5.2 %collective-permute-start.1 = (f32[16,512]{1,0:T(8,128)S(1)}, f32[16,512]{1,0:T(8,128)S(1)}, u32[]{:S(2)}, u32[]{:S(2)}) collective-permute-start(f32[16,512]{1,0:T(8,128)S(1)} %fusion.43), channel_id=1, source_target_pairs={{0,4},{4,8},{8,12},{12,16},{16,20},{20,24},{24,28},{28,0},{1,5},{5... | collective-permute-start | bytes 98312 | tf_op jit(solution)/shard_map/while/body/eval_jaxpr/ppermute | solution.py:16
  53.7 5.0 %collective-permute-start = (bf16[16,512]{1,0:T(8,128)(2,1)S(1)}, bf16[16,512]{1,0:T(8,128)(2,1)S(1)}, u32[]{:S(2)}, u32[]{:S(2)}) collective-permute-start(bf16[16,512]{1,0:T(8,128)(2,1)S(1)} %copy.25), channel_id=1, source_target_pairs={{0,4},{4,8},{8,12},{12,16},{16,20},{20,24},{24,28},{28,0},{1,5},{5... | collective-permute-start | bytes 49160 | tf_op jit(solution)/shard_map/while/body/eval_jaxpr/ppermute | solution.py:16
  54.2 5.2 %collective-permute-start.1 = (f32[16,512]{1,0:T(8,128)S(1)}, f32[16,512]{1,0:T(8,128)S(1)}, u32[]{:S(2)}, u32[]{:S(2)}) collective-permute-start(f32[16,512]{1,0:T(8,128)S(1)} %fusion.43), channel_id=1, source_target_pairs={{0,4},{4,8},{8,12},{12,16},{16,20},{20,24},{24,28},{28,0},{1,5},{5... | collective-permute-start | bytes 98312 | tf_op jit(solution)/shard_map/while/body/eval_jaxpr/ppermute | solution.py:16
  59.4 5.0 %collective-permute-start = (bf16[16,512]{1,0:T(8,128)(2,1)S(1)}, bf16[16,512]{1,0:T(8,128)(2,1)S(1)}, u32[]{:S(2)}, u32[]{:S(2)}) collective-permute-start(bf16[16,512]{1,0:T(8,128)(2,1)S(1)} %copy.25), channel_id=1, source_target_pairs={{0,4},{4,8},{8,12},{12,16},{16,20},{20,24},{24,28},{28,0},{1,5},{5... | collective-permute-start | bytes 49160 | tf_op jit(solution)/shard_map/while/body/eval_jaxpr/ppermute | solution.py:16
  59.9 5.2 %collective-permute-start.1 = (f32[16,512]{1,0:T(8,128)S(1)}, f32[16,512]{1,0:T(8,128)S(1)}, u32[]{:S(2)}, u32[]{:S(2)}) collective-permute-start(f32[16,512]{1,0:T(8,128)S(1)} %fusion.43), channel_id=1, source_target_pairs={{0,4},{4,8},{8,12},{12,16},{16,20},{20,24},{24,28},{28,0},{1,5},{5... | collective-permute-start | bytes 98312 | tf_op jit(solution)/shard_map/while/body/eval_jaxpr/ppermute | solution.py:16
  65.0 5.0 %collective-permute-start = (bf16[16,512]{1,0:T(8,128)(2,1)S(1)}, bf16[16,512]{1,0:T(8,128)(2,1)S(1)}, u32[]{:S(2)}, u32[]{:S(2)}) collective-permute-start(bf16[16,512]{1,0:T(8,128)(2,1)S(1)} %copy.25), channel_id=1, source_target_pairs={{0,4},{4,8},{8,12},{12,16},{16,20},{20,24},{24,28},{28,0},{1,5},{5... | collective-permute-start | bytes 49160 | tf_op jit(solution)/shard_map/while/body/eval_jaxpr/ppermute | solution.py:16
  65.5 5.2 %collective-permute-start.1 = (f32[16,512]{1,0:T(8,128)S(1)}, f32[16,512]{1,0:T(8,128)S(1)}, u32[]{:S(2)}, u32[]{:S(2)}) collective-permute-start(f32[16,512]{1,0:T(8,128)S(1)} %fusion.43), channel_id=1, source_target_pairs={{0,4},{4,8},{8,12},{12,16},{16,20},{20,24},{24,28},{28,0},{1,5},{5... | collective-permute-start | bytes 98312 | tf_op jit(solution)/shard_map/while/body/eval_jaxpr/ppermute | solution.py:16
  70.7 5.0 %collective-permute-start = (bf16[16,512]{1,0:T(8,128)(2,1)S(1)}, bf16[16,512]{1,0:T(8,128)(2,1)S(1)}, u32[]{:S(2)}, u32[]{:S(2)}) collective-permute-start(bf16[16,512]{1,0:T(8,128)(2,1)S(1)} %copy.25), channel_id=1, source_target_pairs={{0,4},{4,8},{8,12},{12,16},{16,20},{20,24},{24,28},{28,0},{1,5},{5... | collective-permute-start | bytes 49160 | tf_op jit(solution)/shard_map/while/body/eval_jaxpr/ppermute | solution.py:16
  71.2 5.2 %collective-permute-start.1 = (f32[16,512]{1,0:T(8,128)S(1)}, f32[16,512]{1,0:T(8,128)S(1)}, u32[]{:S(2)}, u32[]{:S(2)}) collective-permute-start(f32[16,512]{1,0:T(8,128)S(1)} %fusion.43), channel_id=1, source_target_pairs={{0,4},{4,8},{8,12},{12,16},{16,20},{20,24},{24,28},{28,0},{1,5},{5... | collective-permute-start | bytes 98312 | tf_op jit(solution)/shard_map/while/body/eval_jaxpr/ppermute | solution.py:16
  76.4 5.0 %collective-permute-start = (bf16[16,512]{1,0:T(8,128)(2,1)S(1)}, bf16[16,512]{1,0:T(8,128)(2,1)S(1)}, u32[]{:S(2)}, u32[]{:S(2)}) collective-permute-start(bf16[16,512]{1,0:T(8,128)(2,1)S(1)} %copy.25), channel_id=1, source_target_pairs={{0,4},{4,8},{8,12},{12,16},{16,20},{20,24},{24,28},{28,0},{1,5},{5... | collective-permute-start | bytes 49160 | tf_op jit(solution)/shard_map/while/body/eval_jaxpr/ppermute | solution.py:16
  76.9 5.2 %collective-permute-start.1 = (f32[16,512]{1,0:T(8,128)S(1)}, f32[16,512]{1,0:T(8,128)S(1)}, u32[]{:S(2)}, u32[]{:S(2)}) collective-permute-start(f32[16,512]{1,0:T(8,128)S(1)} %fusion.43), channel_id=1, source_target_pairs={{0,4},{4,8},{8,12},{12,16},{16,20},{20,24},{24,28},{28,0},{1,5},{5... | collective-permute-start | bytes 98312 | tf_op jit(solution)/shard_map/while/body/eval_jaxpr/ppermute | solution.py:16
where the time goes:
time: 92.8 us; the launch traced here: 92.5 us
  waiting for transfers between devices  37.8 us (41%)
  blocking collectives  35.5 us (38%)
  matrix products  11.4 us (12%)
  local copies, waits for them, and re-layouts  3.66 us (4%)
  starting transfers between devices  1.76 us (2%)
  other arithmetic  1.42 us (2%)
    ppermute x16, waiting for transfers between devices, passed_along(): return lax.ppermute(value, axis, pairs)  37.8 us
    psum x1, blocking collectives, body(): numerator, totals = lax.psum((numerator, totals), 'tm')  14.4 us
    pmax x1, blocking collectives, body(): peak_score = lax.pmax(jnp.max(masked, axis=2), 'tm')  11.3 us
    psum x1, blocking collectives, body(): speech_grad, loss = lax.psum((speech_part_sum, loss_part), 'tm')  9.82 us
    dot_general x1, matrix products, body(): jnp.dot(features.reshape(rec_count * frame_dev, channels), w_proj, prefer...  2.47 us
    reshape x1, local copies, waits for them, and re-layouts, body(): values = values.reshape(rec_count, frame_dev, heads, width // heads)  2.14 us
    dot_general x8, matrix products, pair_tile(): jnp.dot(grad_b.T, speech_rows, preferred_element_type=jnp.float32)  2.03 us
    dot_general x1, matrix products, body(): jnp.einsum('rhf,rfhd->rhd', weights.astype(jnp.bfloat16), values, preferr...  1.96 us
  transfers between devices with their start and end apart: 16, of which 16 were waited for; matrix products, arithmetic and copies ran while one was open for 6% of the time, Pallas kernels for 0%

commit v1 on v0

v1 whole, which is shorter than its diff:
```python
import math

import jax
import jax.numpy as jnp
from jax import lax
from jax.sharding import PartitionSpec as P

logit_scale = 10.0
logit_shift = -8.0
norm_eps = 1e-06
direct_limit = 8


def swap_pairs(count, stride, steps):
    return [(source, source ^ (steps * stride)) for source in range(count)]


def gathered(value, axis, stride, extent):
    count = lax.axis_size(axis)
    index = lax.axis_index(axis)
    place = (index // stride) % extent
    if extent <= direct_limit and extent & (extent - 1) == 0:
        parts = [value] + [
            lax.ppermute(value, axis, swap_pairs(count, stride, steps)) for steps in range(1, extent)
        ]
        places = [place ^ steps for steps in range(extent)]
        return parts, places
    groups = [
        [base + stride * step for step in range(extent)]
        for base in range(count)
        if (base // stride) % extent == 0
    ]
    whole = lax.all_gather(value, axis, axis_index_groups=groups)
    return [whole[step] for step in range(extent)], list(range(extent))


def split_two(value):
    high = value.astype(jnp.bfloat16)
    low = (value - high.astype(jnp.float32)).astype(jnp.bfloat16)
    return high, low


def pooled_part(features, frame_counts, pool_query, w_proj):
    rec_count, frame_dev, channels = features.shape
    heads = pool_query.shape[0]
    width = w_proj.shape[1]
    scores = jnp.einsum(
        "hc,rfc->rhf", pool_query, features, preferred_element_type=jnp.float32
    ) / math.sqrt(channels)
    positions = lax.axis_index("tm") * frame_dev + jnp.arange(frame_dev, dtype=jnp.int32)
    valid = (positions[None, :] < frame_counts[:, None])[:, None, :]
    masked = jnp.where(valid, scores, -1e30)
    peak = jnp.max(masked, axis=2).astype(jnp.bfloat16)
    weights = jnp.where(valid, jnp.exp(masked - peak.astype(jnp.float32)[:, :, None]), 0.0)
    totals = jnp.sum(weights, axis=2)
    high, low = split_two(weights)
    both = jnp.concatenate([high, low], axis=1)
    sums = jnp.einsum("rhf,rfc->rhc", both, features, preferred_element_type=jnp.float32)
    sums = (sums[:, :heads] + sums[:, heads:]).reshape(rec_count * heads, channels)
    high, low = split_two(sums)
    wide = jnp.dot(jnp.concatenate([high, low]), w_proj, preferred_element_type=jnp.float32)
    wide = (wide[: rec_count * heads] + wide[rec_count * heads :]).reshape(rec_count, heads, width)
    own = jnp.arange(width)[None, :] // (width // heads) == jnp.arange(heads)[:, None]
    numerator = jnp.sum(jnp.where(own[None], wide, 0.0), axis=1)
    return numerator, peak, totals


def pair_terms(speech, targets, docs, doc_ids):
    logits = (
        logit_scale * jnp.dot(speech, docs.T, preferred_element_type=jnp.float32) + logit_shift
    )
    labels = jnp.where(targets[:, None] == doc_ids[None, :], 1.0, -1.0)
    losses = jnp.sum(jax.nn.softplus(-labels * logits), axis=1)
    grad_b = (-labels * jax.nn.sigmoid(-labels * logits)).astype(jnp.bfloat16)
    return losses, grad_b


def body(features, frame_counts, pool_query, w_proj, doc_embed, doc_index):
    rec_count, frame_dev, channels = features.shape
    heads = pool_query.shape[0]
    width = w_proj.shape[1]
    doc_dev = doc_embed.shape[0]
    group = lax.axis_index("grp")
    column = lax.axis_index("tm")
    group_count = lax.axis_size("grp")
    column_count = lax.axis_size("tm")
    cores = 2 if group_count % 2 == 0 else 1
    layers = group_count // cores
    core = group % cores

    def doc_start(layer, core, column):
        return ((layer * cores + core) * column_count + column) * doc_dev

    doc_parts, doc_layers = gathered(doc_embed, "grp", cores, layers)
    numerator, peak, totals = pooled_part(features, frame_counts, pool_query, w_proj)

    high, low = split_two(numerator)
    total_high, total_low = split_two(totals)
    stats = jnp.concatenate([peak, total_high, total_low], axis=1)
    stats = jnp.pad(stats, ((0, 0), (0, width - 3 * heads)))
    payload = jnp.concatenate(doc_parts + [high, low, stats])
    doc_rows = layers * doc_dev
    parts, columns = gathered(payload, "tm", 1, column_count)

    stats = jnp.stack([part[doc_rows + 2 * rec_count :, : 3 * heads] for part in parts]).astype(jnp.float32)
    peaks = stats[:, :, :heads]
    top = jnp.max(peaks, axis=0)
    shares = jnp.exp(peaks - top[None])
    all_totals = jnp.sum(shares * (stats[:, :, heads : 2 * heads] + stats[:, :, 2 * heads :]), axis=0)
    scale = shares / all_totals[None]
    scale = jnp.repeat(scale, width // heads, axis=2)
    numerators = jnp.stack(
        [
            part[doc_rows : doc_rows + rec_count].astype(jnp.float32)
            + part[doc_rows + rec_count : doc_rows + 2 * rec_count].astype(jnp.float32)
            for part in parts
        ]
    )
    pooled = jnp.sum(numerators * scale, axis=0)
    speech = (
        pooled * lax.rsqrt(jnp.sum(pooled * pooled, axis=1, keepdims=True) + norm_eps)
    ).astype(jnp.bfloat16)

    speech_parts, layer_list = gathered(speech, "grp", cores, layers)
    docs = jnp.concatenate([part[:doc_rows] for part in parts])
    doc_ids = jnp.concatenate(
        [
            doc_start(layer, core, col) + jnp.arange(doc_dev, dtype=jnp.int32)
            for col in columns
            for layer in doc_layers
        ]
    )
    own_targets = lax.dynamic_slice_in_dim(doc_index, group * rec_count, rec_count)
    loss, grad_b = pair_terms(speech, own_targets, docs, doc_ids)
    speech_grad = jnp.dot(grad_b, docs, preferred_element_type=jnp.float32)
    rows = jnp.concatenate(speech_parts)
    rec_ids = jnp.concatenate(
        [
            (layer * cores + core) * rec_count + jnp.arange(rec_count, dtype=jnp.int32)
            for layer in layer_list
        ]
    )
    if cores == 2:
        pairs = swap_pairs(group_count, 1, 1)
        other_docs = lax.ppermute(docs, "grp", pairs)
        other_rows = lax.ppermute(rows, "grp", pairs)
        shift = (1 - 2 * core) * column_count * doc_dev
        other_loss, other_grad = pair_terms(speech, own_targets, other_docs, doc_ids + shift)
        loss = loss + other_loss
        speech_grad = speech_grad + jnp.dot(other_grad, other_docs, preferred_element_type=jnp.float32)
        rows = jnp.concatenate([rows, other_rows])
        rec_ids = jnp.concatenate([rec_ids, rec_ids + (1 - 2 * core) * rec_count])
    speech_grad = logit_scale * speech_grad

    rec_total = group_count * rec_count
    picks = rec_ids[:, None] == jnp.arange(rec_total, dtype=jnp.int32)[None, :]
    targets = jnp.sum(jnp.where(picks, doc_index[None, :], 0), axis=1)
    own_ids = (group * column_count + column) * doc_dev + jnp.arange(doc_dev, dtype=jnp.int32)
    _, grad_b = pair_terms(rows, targets, doc_embed, own_ids)
    doc_grad = logit_scale * jnp.dot(grad_b.T, rows, preferred_element_type=jnp.float32)
    return (loss, speech_grad, doc_grad)


def solution(mesh):
    placed = (P("grp", "tm", None), P("grp"), P(), P(), P(("grp", "tm"), None), P())
    return jax.shard_map(
        body,
        mesh=mesh,
        in_specs=placed,
        out_specs=(P("grp"), P("grp", None), P(("grp", "tm"), None)),
        check_vma=False,
    )
```

time: 92.8 us -> 32.8 us (0.35)
  blocking collectives: 35.5 us -> 0 us
  waiting for transfers between devices: 37.8 us -> 9.89 us
  starting transfers between devices: 1.76 us -> 13.8 us
  matrix products: 11.4 us -> 4.73 us
  local copies, waits for them, and re-layouts: 3.66 us -> 0.79 us
  other arithmetic: 1.42 us -> 2.43 us
    ppermute x16 -> x11, waiting for transfers between devices: 37.8 us -> 9.89 us  [the longest x9 9.03 us: gathered(): lax.ppermute(value, axis, swap_pairs(count, stride, steps))]
    psum x2 -> x0, blocking collectives: 24.2 us -> none  [the longest x1 14.4 us: body(): numerator, totals = lax.psum((numerator, totals), 'tm')]
    ppermute x16 -> x11, starting transfers between devices: 1.76 us -> 13.8 us  [the longest x9 13.6 us: gathered(): lax.ppermute(value, axis, swap_pairs(count, stride, steps))]
    pmax x1 -> x0, blocking collectives: 11.3 us -> none  [body(): peak_score = lax.pmax(jnp.max(masked, axis=2), 'tm')]
    dot_general x27 -> x8, matrix products: 11.4 us -> 4.73 us  [the longest x1 1.53 us: pooled_part(): jnp.einsum('hc,rfc->rhf', pool_query, features, preferred_element_type=jn...]
    reshape x2 -> x0, local copies, waits for them, and re-layouts: 2.21 us -> none  [the longest x1 2.14 us: body(): values = values.reshape(rec_count, frame_dev, heads, width // heads)]
    unnamed x7 -> x14, local copies, waits for them, and re-layouts: 1.34 us -> 0.04 us
  transfers between devices with their start and end apart: 16 -> 11, of which waited for: 16 -> 7; matrix products, arithmetic and copies ran while one was open for 6% -> 17% of each run, Pallas kernels for 0% -> 0%
where the time goes in v1:
time: 32.8 us; the launch traced here: 32.5 us
  starting transfers between devices  13.8 us (42%)
  waiting for transfers between devices  9.89 us (30%)
  matrix products  4.73 us (14%)
  other arithmetic  2.43 us (7%)
  between operations  0.96 us (3%)
  local copies, waits for them, and re-layouts  0.79 us (2%)
    ppermute x9, starting transfers between devices, gathered(): lax.ppermute(value, axis, swap_pairs(count, stride, steps))  13.6 us
    ppermute x9, waiting for transfers between devices, gathered(): lax.ppermute(value, axis, swap_pairs(count, stride, steps))  9.03 us
    dot_general x1, matrix products, pooled_part(): jnp.einsum('hc,rfc->rhf', pool_query, features, preferred_element_type=jn...  1.53 us
    dot_general x1, matrix products, body(): jnp.dot(grad_b.T, rows, preferred_element_type=jnp.float32)  0.94 us
    ppermute x1, waiting for transfers between devices, body(): other_rows = lax.ppermute(rows, 'grp', pairs)  0.86 us
    dot_general x1, matrix products, body(): speech_grad = jnp.dot(grad_b, docs, preferred_element_type=jnp.float32)  0.79 us
    lt x1, other arithmetic, pooled_part(): valid = (positions[None, :] < frame_counts[:, None])[:, None, :]  0.73 us
  transfers between devices with their start and end apart: 11, of which 7 were waited for; matrix products, arithmetic and copies ran while one was open for 17% of the time, Pallas kernels for 0%

profile of v1, /device:TPU:0, one launch (start us, length us, event | category | flops | bytes accessed | tf_op | source)
XLA Modules:
  0.0 32.5 jit_solution(17065356946571720841)
XLA Ops:
  0.6 0.0 copy-start
  0.6 3.1 %collective-permute-start = (bf16[16,512]{1,0:T(8,128)(2,1)}, bf16[16,512]{1,0:T(8,128)(2,1)S(1)}, u32[]{:S(2)}, u32[]{:S(2)}) collective-permute-start(bf16[16,512]{1,0:T(8,128)(2,1)} %param.10), channel_id=1, source_target_pairs={{0,8},{4,12},{8,0},{12,4},{16,24},{20,28},{24,16},{28,20},{1,9},{5... | collective-permute-start | bytes 49160 | tf_op jit(solution)/shard_map/ppermute | solution.py:24
  3.7 2.6 %collective-permute-start.1 = (bf16[16,512]{1,0:T(8,128)(2,1)}, bf16[16,512]{1,0:T(8,128)(2,1)S(1)}, u32[]{:S(2)}, u32[]{:S(2)}) collective-permute-start(bf16[16,512]{1,0:T(8,128)(2,1)} %param.10), channel_id=1, source_target_pairs={{0,16},{4,20},{8,24},{12,28},{16,0},{20,4},{24,8},{28,12},{1,17},{... | collective-permute-start | bytes 49160 | tf_op jit(solution)/shard_map/ppermute | solution.py:24
  6.3 0.0 collective-permute-start.2
  6.3 0.7 %broadcast_compare_fusion = pred[4,256]{1,0:T(4,128)(4,1)S(1)} fusion(s32[256]{0:T(256)S(1)} %iota_add_fusion, s32[4]{0:T(128)} %param.7), kind=kLoop, calls=%fused_computation.99 | loop fusion | flops 1024 | bytes 2064 | tf_op jit(solution)/shard_map/lt | solution.py:51
  7.1 0.0 copy-done
  7.1 0.0 copy-start.1
  7.1 1.5 %fusion.74 = (bf16[4,8]{1,0:T(4,128)(2,1)S(1)}, f32[4,8,256]{2,1,0:T(8,128)S(1)}) fusion(bf16[4,256,1024]{2,1,0:T(8,128)(2,1)S(1)} %copy-done, bf16[8,1024]{1,0:T(8,128)(2,1)} %param.8, pred[4,256]{1,0:T(4,128)(4,1)S(1)} %broadcast_compare_fusion), kind=kOutput, calls=%fused_computation.147 | convolution fusion | flops 16801760 | bytes 2147392 | tf_op jit(solution)/shard_map/hc,rfc->rhf/dot_general | solution.py:47
  8.6 0.2 fusion.29
  8.8 0.0 copy-start.2
  8.8 0.0 copy-start.3
  8.8 0.4 %fusion.25 = f32[4,16,1024]{2,1,0:T(8,128)S(1)} fusion(bf16[4,256,1024]{2,1,0:T(8,128)(2,1)S(1)} %copy-done, bf16[4,8,256]{2,1,0:T(8,128)(2,1)S(1)} %get-tuple-element.10, bf16[4,8,256]{2,1,0:T(8,128)(2,1)S(1)} %get-tuple-element.11), kind=kOutput, calls=%fused_computation.38 | convolution fusion | flops 33619968 | bytes 2392064 | tf_op jit(solution)/shard_map/rhf,rfc->rhc/dot_general | solution.py:58
  9.2 0.0 copy-done.1
  9.2 0.3 fusion.16
  9.6 0.1 reduce_sum.77
  9.7 0.1 pad_maximum_fusion.1
  9.7 0.1 fusion.87
  9.8 0.0 copy-done.2
  9.9 0.1 add_add_fusion
  10.0 0.1 concatenate.46
  10.2 0.1 concatenate.39
  10.3 0.0 copy-done.3
  10.3 0.2 select_reduce_fusion
  10.5 0.1 dynamic_slice.3
  10.6 0.0 collective-permute-done
  10.6 0.0 collective-permute-done.1
  10.6 1.5 %collective-permute-done.2 = bf16[16,512]{1,0:T(8,128)(2,1)S(1)} collective-permute-done((bf16[16,512]{1,0:T(8,128)(2,1)}, bf16[16,512]{1,0:T(8,128)(2,1)S(1)}, u32[]{:S(2)}, u32[]{:S(2)}) %collective-permute-start.2) | collective-permute-done | bytes 16416 | tf_op jit(solution)/shard_map/ppermute | solution.py:24
  12.1 2.5 %collective-permute-start.5 = (bf16[76,512]{1,0:T(8,128)(2,1)S(1)}, bf16[76,512]{1,0:T(8,128)(2,1)S(1)}, u32[]{:S(2)}, u32[]{:S(2)}) collective-permute-start(bf16[76,512]{1,0:T(8,128)(2,1)S(1)} %concatenate.43), channel_id=1, source_target_pairs={{0,3},{1,2},{2,1},{3,0},{4,7},{5,6},{6,5},{7,4},{8,11},{9,10},{10,... | collective-permute-start | bytes 233480 | tf_op jit(solution)/shard_map/ppermute | solution.py:24
  14.6 0.5 %collective-permute-start.4 = (bf16[76,512]{1,0:T(8,128)(2,1)S(1)}, bf16[76,512]{1,0:T(8,128)(2,1)S(1)}, u32[]{:S(2)}, u32[]{:S(2)}) collective-permute-start(bf16[76,512]{1,0:T(8,128)(2,1)S(1)} %concatenate.43), channel_id=1, source_target_pairs={{0,2},{1,3},{2,0},{3,1},{4,6},{5,7},{6,4},{7,5},{8,10},{9,11},{10,... | collective-permute-start | bytes 233480 | tf_op jit(solution)/shard_map/ppermute | solution.py:24
  15.1 0.5 %collective-permute-start.3 = (bf16[76,512]{1,0:T(8,128)(2,1)S(1)}, bf16[76,512]{1,0:T(8,128)(2,1)S(1)}, u32[]{:S(2)}, u32[]{:S(2)}) collective-permute-start(bf16[76,512]{1,0:T(8,128)(2,1)S(1)} %concatenate.43), channel_id=1, source_target_pairs={{0,1},{1,0},{2,3},{3,2},{4,5},{5,4},{6,7},{7,6},{8,9},{9,8},{10,11... | collective-permute-start | bytes 233480 | tf_op jit(solution)/shard_map/ppermute | solution.py:24
  15.7 2.3 %collective-permute-done.5 = bf16[76,512]{1,0:T(8,128)(2,1)S(1)} collective-permute-done((bf16[76,512]{1,0:T(8,128)(2,1)S(1)}, bf16[76,512]{1,0:T(8,128)(2,1)S(1)}, u32[]{:S(2)}, u32[]{:S(2)}) %collective-permute-start.5) | collective-permute-done | bytes 77856 | tf_op jit(solution)/shard_map/ppermute | solution.py:24
  18.0 1.1 %collective-permute-done.4 = bf16[76,512]{1,0:T(8,128)(2,1)S(1)} collective-permute-done((bf16[76,512]{1,0:T(8,128)(2,1)S(1)}, bf16[76,512]{1,0:T(8,128)(2,1)S(1)}, u32[]{:S(2)}, u32[]{:S(2)}) %collective-permute-start.4) | collective-permute-done | bytes 77856 | tf_op jit(solution)/shard_map/ppermute | solution.py:24
  19.1 0.1 stack.30
  19.1 0.1 stack.29
  19.2 0.3 %collective-permute-done.3 = bf16[76,512]{1,0:T(8,128)(2,1)S(1)} collective-permute-done((bf16[76,512]{1,0:T(8,128)(2,1)S(1)}, bf16[76,512]{1,0:T(8,128)(2,1)S(1)}, u32[]{:S(2)}, u32[]{:S(2)}) %collective-permute-start.3) | collective-permute-done | bytes 77856 | tf_op jit(solution)/shard_map/ppermute | solution.py:24
  19.6 0.1 stack.28
  19.7 0.1 fusion.37
  19.8 0.1 fusion.23
  19.9 0.1 reduce_sum.81
  20.0 0.1 multiply_reduce_fusion
  20.1 0.1 multiply_convert_fusion
  20.2 0.0 collective-permute-start.7
  20.2 2.9 %collective-permute-start.8 = (bf16[4,512]{1,0:T(4,128)(2,1)S(1)}, bf16[4,512]{1,0:T(4,128)(2,1)S(1)}, u32[]{:S(2)}, u32[]{:S(2)}) collective-permute-start(bf16[4,512]{1,0:T(4,128)(2,1)S(1)} %multiply_convert_fusion), channel_id=1, source_target_pairs={{0,16},{4,20},{8,24},{12,28},{16,0},{20,4},{24,8},{28,12},{1,17},{... | collective-permute-start | bytes 12296 | tf_op jit(solution)/shard_map/ppermute | solution.py:24
  23.1 1.5 %collective-permute-start.9 = (bf16[4,512]{1,0:T(4,128)(2,1)S(1)}, bf16[4,512]{1,0:T(4,128)(2,1)S(1)}, u32[]{:S(2)}, u32[]{:S(2)}) collective-permute-start(bf16[4,512]{1,0:T(4,128)(2,1)S(1)} %multiply_convert_fusion), channel_id=1, source_target_pairs={{0,24},{4,28},{8,16},{12,20},{16,8},{20,12},{24,0},{28,4},{1,25},{... | collective-permute-start | bytes 12296 | tf_op jit(solution)/shard_map/ppermute | solution.py:24
  24.6 0.1 collective-permute-start.6
  24.7 0.0 collective-permute-done.7
  24.7 0.1 collective-permute-done.8
  24.8 3.7 %collective-permute-done.9 = bf16[4,512]{1,0:T(4,128)(2,1)S(1)} collective-permute-done((bf16[4,512]{1,0:T(4,128)(2,1)S(1)}, bf16[4,512]{1,0:T(4,128)(2,1)S(1)}, u32[]{:S(2)}, u32[]{:S(2)}) %collective-permute-start.9) | collective-permute-done | bytes 4128 | tf_op jit(solution)/shard_map/ppermute | solution.py:24
  28.5 0.1 collective-permute-start.10
  28.6 0.3 fusion.45
  28.9 0.9 %collective-permute-done.10 = bf16[16,512]{1,0:T(8,128)(2,1)S(1)} collective-permute-done((bf16[16,512]{1,0:T(8,128)(2,1)S(1)}, bf16[16,512]{1,0:T(8,128)(2,1)S(1)}, u32[]{:S(2)}, u32[]{:S(2)}) %collective-permute-start.10) | collective-permute-done | bytes 16416 | tf_op jit(solution)/shard_map/ppermute | solution.py:146
  29.8 0.9 %convolution_multiply_fusion = f32[16,512]{1,0:T(8,128)} fusion(bf16[32,512]{1,0:T(8,128)(2,1)S(1)} %concatenate.48, bf16[16,512]{1,0:T(8,128)(2,1)S(1)} %copy-done.2, s32[16]{0:T(128)S(1)} %iota_add_fusion.1, s32[32]{0:T(128)S(1)} %select_reduce_fusion), kind=kOutput, calls=%fused_computation | convolution fusion | flops 1062400 | bytes 82112 | tf_op jit(solution)/shard_map/dot_general | solution.py:160
  30.7 0.0 collective-permute-done.6
  30.7 0.3 fusion.46
  31.1 0.5 %add.434 = f32[4]{0:T(128)} add(f32[4]{0:T(128)S(1)} %get-tuple-element.14, f32[4]{0:T(128)S(1)} %get-tuple-element.16) | non-fusion elementwise | flops 4 | bytes 48 | tf_op jit(solution)/shard_map/add | solution.py:149
  31.6 0.2 fusion.49
  31.8 0.8 %fusion.10 = f32[4,512]{1,0:T(4,128)} fusion(f32[4,512]{1,0:T(4,128)S(1)} %fusion.49, bf16[256,512]{1,0:T(8,128)(2,1)S(1)} %slice_dynamic-update-slice_fusion, f32[4,256]{1,0:T(4,128)S(1)} %get-tuple-element.15, s32[256]{0:T(256)S(1)} %concatenate.39, s32[4]{0:T(128)S(1)} %dynamic_slice.3), kind=kOutput, calls=%fused_computation.14 | convolution fusion | flops 1060864 | bytes 283664 | tf_op jit(solution)/shard_map/dot_general | solution.py:135
  (42 shorter events, 0.3 us)
Async XLA Ops:
  0.6 6.4 %copy-start = (bf16[4,256,1024]{2,1,0:T(8,128)(2,1)S(1)}, bf16[4,256,1024]{2,1,0:T(8,128)(2,1)}, u32[]{:S(2)}) copy-start(bf16[4,256,1024]{2,1,0:T(8,128)(2,1)} %param.6) | copy-start | bytes 6291460
  0.6 9.9 %collective-permute-start = (bf16[16,512]{1,0:T(8,128)(2,1)}, bf16[16,512]{1,0:T(8,128)(2,1)S(1)}, u32[]{:S(2)}, u32[]{:S(2)}) collective-permute-start(bf16[16,512]{1,0:T(8,128)(2,1)} %param.10), channel_id=1, source_target_pairs={{0,8},{4,12},{8,0},{12,4},{16,24},{20,28},{24,16},{28,20},{1,9},{5... | collective-permute-start | bytes 49160 | tf_op jit(solution)/shard_map/ppermute | solution.py:24
  3.7 6.8 %collective-permute-start.1 = (bf16[16,512]{1,0:T(8,128)(2,1)}, bf16[16,512]{1,0:T(8,128)(2,1)S(1)}, u32[]{:S(2)}, u32[]{:S(2)}) collective-permute-start(bf16[16,512]{1,0:T(8,128)(2,1)} %param.10), channel_id=1, source_target_pairs={{0,16},{4,20},{8,24},{12,28},{16,0},{20,4},{24,8},{28,12},{1,17},{... | collective-permute-start | bytes 49160 | tf_op jit(solution)/shard_map/ppermute | solution.py:24
  6.3 5.7 %collective-permute-start.2 = (bf16[16,512]{1,0:T(8,128)(2,1)}, bf16[16,512]{1,0:T(8,128)(2,1)S(1)}, u32[]{:S(2)}, u32[]{:S(2)}) collective-permute-start(bf16[16,512]{1,0:T(8,128)(2,1)} %param.10), channel_id=1, source_target_pairs={{0,24},{4,28},{8,16},{12,20},{16,8},{20,12},{24,0},{28,4},{1,25},{... | collective-permute-start | bytes 49160 | tf_op jit(solution)/shard_map/ppermute | solution.py:24
  7.1 2.2 %copy-start.1 = (bf16[1024,512]{1,0:T(8,128)(2,1)S(1)}, bf16[1024,512]{1,0:T(8,128)(2,1)}, u32[]{:S(2)}) copy-start(bf16[1024,512]{1,0:T(8,128)(2,1)} %param.9) | copy-start | bytes 3145732
  8.8 1.0 %copy-start.2 = (bf16[16,512]{1,0:T(8,128)(2,1)S(1)}, bf16[16,512]{1,0:T(8,128)(2,1)}, u32[]{:S(2)}) copy-start(bf16[16,512]{1,0:T(8,128)(2,1)} %param.10) | copy-start | bytes 49156
  8.8 1.5 %copy-start.3 = (s32[32]{0:T(128)S(1)}, s32[32]{0:T(128)}, u32[]{:S(2)}) copy-start(s32[32]{0:T(128)} %param.11) | copy-start | bytes 388
  12.1 5.9 %collective-permute-start.5 = (bf16[76,512]{1,0:T(8,128)(2,1)S(1)}, bf16[76,512]{1,0:T(8,128)(2,1)S(1)}, u32[]{:S(2)}, u32[]{:S(2)}) collective-permute-start(bf16[76,512]{1,0:T(8,128)(2,1)S(1)} %concatenate.43), channel_id=1, source_target_pairs={{0,3},{1,2},{2,1},{3,0},{4,7},{5,6},{6,5},{7,4},{8,11},{9,10},{10,... | collective-permute-start | bytes 233480 | tf_op jit(solution)/shard_map/ppermute | solution.py:24
  14.6 4.4 %collective-permute-start.4 = (bf16[76,512]{1,0:T(8,128)(2,1)S(1)}, bf16[76,512]{1,0:T(8,128)(2,1)S(1)}, u32[]{:S(2)}, u32[]{:S(2)}) collective-permute-start(bf16[76,512]{1,0:T(8,128)(2,1)S(1)} %concatenate.43), channel_id=1, source_target_pairs={{0,2},{1,3},{2,0},{3,1},{4,6},{5,7},{6,4},{7,5},{8,10},{9,11},{10,... | collective-permute-start | bytes 233480 | tf_op jit(solution)/shard_map/ppermute | solution.py:24
  15.1 4.4 %collective-permute-start.3 = (bf16[76,512]{1,0:T(8,128)(2,1)S(1)}, bf16[76,512]{1,0:T(8,128)(2,1)S(1)}, u32[]{:S(2)}, u32[]{:S(2)}) collective-permute-start(bf16[76,512]{1,0:T(8,128)(2,1)S(1)} %concatenate.43), channel_id=1, source_target_pairs={{0,1},{1,0},{2,3},{3,2},{4,5},{5,4},{6,7},{7,6},{8,9},{9,8},{10,11... | collective-permute-start | bytes 233480 | tf_op jit(solution)/shard_map/ppermute | solution.py:24
  20.2 4.5 %collective-permute-start.7 = (bf16[4,512]{1,0:T(4,128)(2,1)S(1)}, bf16[4,512]{1,0:T(4,128)(2,1)S(1)}, u32[]{:S(2)}, u32[]{:S(2)}) collective-permute-start(bf16[4,512]{1,0:T(4,128)(2,1)S(1)} %multiply_convert_fusion), channel_id=1, source_target_pairs={{0,8},{4,12},{8,0},{12,4},{16,24},{20,28},{24,16},{28,20},{1,9},{5... | collective-permute-start | bytes 12296 | tf_op jit(solution)/shard_map/ppermute | solution.py:24
  20.2 4.6 %collective-permute-start.8 = (bf16[4,512]{1,0:T(4,128)(2,1)S(1)}, bf16[4,512]{1,0:T(4,128)(2,1)S(1)}, u32[]{:S(2)}, u32[]{:S(2)}) collective-permute-start(bf16[4,512]{1,0:T(4,128)(2,1)S(1)} %multiply_convert_fusion), channel_id=1, source_target_pairs={{0,16},{4,20},{8,24},{12,28},{16,0},{20,4},{24,8},{28,12},{1,17},{... | collective-permute-start | bytes 12296 | tf_op jit(solution)/shard_map/ppermute | solution.py:24
  23.1 5.4 %collective-permute-start.9 = (bf16[4,512]{1,0:T(4,128)(2,1)S(1)}, bf16[4,512]{1,0:T(4,128)(2,1)S(1)}, u32[]{:S(2)}, u32[]{:S(2)}) collective-permute-start(bf16[4,512]{1,0:T(4,128)(2,1)S(1)} %multiply_convert_fusion), channel_id=1, source_target_pairs={{0,24},{4,28},{8,16},{12,20},{16,8},{20,12},{24,0},{28,4},{1,25},{... | collective-permute-start | bytes 12296 | tf_op jit(solution)/shard_map/ppermute | solution.py:24
  24.6 6.1 %collective-permute-start.6 = (bf16[256,512]{1,0:T(8,128)(2,1)S(1)}, bf16[256,512]{1,0:T(8,128)(2,1)S(1)}, u32[]{:S(2)}, u32[]{:S(2)}) collective-permute-start(bf16[256,512]{1,0:T(8,128)(2,1)S(1)} %slice_dynamic-update-slice_fusion), channel_id=1, source_target_pairs={{0,4},{4,0},{8,12},{12,8},{16,20},{20,16},{24,28},{28,24},{1,5},{5... | collective-permute-start | bytes 786440 | tf_op jit(solution)/shard_map/ppermute | solution.py:145
  28.5 1.2 %collective-permute-start.10 = (bf16[16,512]{1,0:T(8,128)(2,1)S(1)}, bf16[16,512]{1,0:T(8,128)(2,1)S(1)}, u32[]{:S(2)}, u32[]{:S(2)}) collective-permute-start(bf16[16,512]{1,0:T(8,128)(2,1)S(1)} %pad_maximum_fusion), channel_id=1, source_target_pairs={{0,4},{4,0},{8,12},{12,8},{16,20},{20,16},{24,28},{28,24},{1,5},{5... | collective-permute-start | bytes 49160 | tf_op jit(solution)/shard_map/ppermute | solution.py:146

commit v2 on v0

v2 whole, which is shorter than its diff:
```python
import math

import jax
import jax.numpy as jnp
from jax import lax
from jax.experimental import pallas as pl
from jax.experimental.pallas import tpu as pltpu
from jax.sharding import PartitionSpec as P

logit_scale = 10.0
logit_shift = -8.0
norm_eps = 1e-06
direct_limit = 8
bf16 = jnp.bfloat16
f32 = jnp.float32
BY_ROWS = (((1,), (1,)), ((), ()))
VMEM = pl.BlockSpec(memory_space=pltpu.VMEM)


def in_vmem(kernel, outs, limit_mib, name):
    def call(*operands):
        return pl.pallas_call(
            kernel,
            out_shape=outs,
            in_specs=[VMEM] * len(operands),
            out_specs=jax.tree.map(lambda _: VMEM, outs),
            compiler_params=pltpu.CompilerParams(vmem_limit_bytes=limit_mib * 2**20),
            name=name,
        )(*operands)

    return call


def two_terms(value):
    high = value.astype(bf16)
    return high, (value - high.astype(f32)).astype(bf16)


def pool_kernel(
    scheme,
    blocks,
    counts_hbm,
    index_hbm,
    query_hbm,
    features_hbm,
    proj_hbm,
    out_ref,
    place_ref,
    at_ref,
    counts_ref,
    index_ref,
    query_ref,
    features_ref,
    proj_ref,
    sems,
):
    recs, frames, channels = features_ref.shape
    heads = query_ref.shape[0]
    width = proj_ref.shape[1]
    rows = recs * heads
    copies = [
        pltpu.make_async_copy(source, target, sems.at[n])
        for n, (source, target) in enumerate(
            [(counts_hbm, counts_ref), (query_hbm, query_ref)]
            + [(features_hbm.at[r], features_ref.at[r]) for r in range(recs)]
            + [(proj_hbm, proj_ref), (index_hbm, index_ref)]
        )
    ]
    for copy in copies:
        copy.start()
    copies[0].wait()
    copies[1].wait()
    query = query_ref[...]
    scores, limits = [], []
    start = lax.axis_index("tm") * frames
    for r in range(recs):
        copies[2 + r].wait()
        scores.append(lax.dot_general(query, features_ref[r], BY_ROWS, preferred_element_type=f32))
        limits.append(jnp.full((heads, 1), counts_ref[r] - start, jnp.int32))
    scores = jnp.concatenate(scores, 0) / math.sqrt(channels)
    valid = lax.broadcasted_iota(jnp.int32, (rows, frames), 1) < jnp.concatenate(limits, 0)
    masked = jnp.where(valid, scores, -1e30)
    peak = jnp.max(masked, axis=1, keepdims=True).astype(bf16).astype(f32)
    weights = jnp.where(valid, jnp.exp(masked - peak), 0.0)
    totals = jnp.sum(weights, axis=1, keepdims=True)
    high, low = two_terms(weights)
    sums = []
    for r in range(recs):
        part = slice(r * heads, (r + 1) * heads)
        both = jnp.concatenate([high[part], low[part]], 0)
        both = jnp.dot(both, features_ref[r], preferred_element_type=f32)
        sums.append(both[:heads] + both[heads:])
    high, low = two_terms(jnp.concatenate(sums, 0))
    copies[2 + recs].wait()
    wide = jnp.dot(jnp.concatenate([high, low], 0), proj_ref[...], preferred_element_type=f32)
    wide = wide[:rows] + wide[rows:]
    own = lax.broadcasted_iota(jnp.int32, (rows, width), 1) // (width // heads)
    own = own == lax.broadcasted_iota(jnp.int32, (rows, width), 0) % heads
    lane = lax.broadcasted_iota(jnp.int32, (rows, 128), 1)
    lane = lane == lax.broadcasted_iota(jnp.int32, (rows, 128), 0) % heads

    def over_heads(value):
        return jnp.concatenate(
            [jnp.sum(value[r * heads : (r + 1) * heads], 0, keepdims=True) for r in range(recs)], 0
        )

    pooled = over_heads(jnp.where(own, wide, 0.0))
    pooled_high = pooled.astype(bf16).astype(f32)
    totals = over_heads(jnp.where(lane, totals, 0.0))
    totals_high = totals.astype(bf16).astype(f32)
    peaks = over_heads(jnp.where(lane, peak, 0.0))
    stats = [peaks, totals_high, totals - totals_high, jnp.zeros((recs, width - 384), f32)]
    out_ref[...] = jnp.concatenate(
        [pooled_high, pooled - pooled_high, jnp.concatenate(stats, 1), jnp.zeros((recs, width), f32)], 0
    ).astype(bf16)

    copies[3 + recs].wait()
    group, column, tm = lax.axis_index("grp"), lax.axis_index("tm"), lax.axis_size("tm")
    layer, core = group // 2, group % 2
    docs_dev, far, by_column, by_far = scheme
    row = lax.broadcasted_iota(jnp.int32, place_ref.shape, 0)
    spot = lax.broadcasted_iota(jnp.int32, place_ref.shape, 1)
    place = jnp.full(place_ref.shape, -1, jnp.int32)
    for r in range(2 * recs):
        target = index_ref[(group ^ (r // recs)) * recs + r % recs]
        of_group, rest = target // (tm * docs_dev), target % (tm * docs_dev)
        of_layer = of_group // 2
        chunk = (of_layer ^ layer) % 2 + 2 * ((of_group ^ core) % 2)
        at = ((rest // docs_dev) ^ (column if by_column else 0)) * far
        at = (at + ((of_layer // 2) ^ (layer // 2 if by_far else 0))) * docs_dev + rest % docs_dev
        place = jnp.where((row == r) & (spot == chunk), at, place)
    place_ref[...] = place
    spot = lax.broadcasted_iota(jnp.int32, at_ref.shape, 1)
    ats = jnp.full(at_ref.shape, -1, jnp.int32)
    first = (group * tm + column) * docs_dev
    for n, block in enumerate(blocks):
        if block is not None:
            base = ((layer ^ block[0]) * 2 + (core ^ block[1])) * recs
            for r in range(recs):
                ats = jnp.where(spot == n * recs + r, index_ref[base + r] - first, ats)
    at_ref[...] = ats


def meet_kernel(recs, heads, *refs):
    parts, (send_ref, speech_ref) = refs[:-2], refs[-2:]
    doc_rows = parts[0].shape[0] - 4 * recs
    width = parts[0].shape[1]
    pools = [part[doc_rows:, :].astype(f32) for part in parts]
    peaks = [pool[2 * recs : 3 * recs, :128] for pool in pools]
    totals = [pool[2 * recs : 3 * recs, 128:256] + pool[2 * recs : 3 * recs, 256:384] for pool in pools]
    top = peaks[0]
    for peak in peaks[1:]:
        top = jnp.maximum(top, peak)
    shares = [jnp.exp(peak - top) for peak in peaks]
    whole = shares[0] * totals[0]
    for share, total in zip(shares[1:], totals[1:]):
        whole = whole + share * total
    used = lax.broadcasted_iota(jnp.int32, whole.shape, 1) < heads
    inverse = jnp.where(used, 1.0 / jnp.where(used, whole, 1.0), 0.0)
    high, low = two_terms(jnp.concatenate([share * inverse for share in shares], 0))
    spread = lax.broadcasted_iota(jnp.int32, (128, width), 1) // (width // heads)
    spread = (spread == lax.broadcasted_iota(jnp.int32, (128, width), 0)).astype(f32).astype(bf16)
    scales = jnp.dot(high, spread, preferred_element_type=f32) + jnp.dot(
        low, spread, preferred_element_type=f32
    )
    pooled = jnp.zeros((recs, width), f32)
    for n, pool in enumerate(pools):
        pooled = pooled + (pool[:recs] + pool[recs : 2 * recs]) * scales[n * recs : (n + 1) * recs]
    speech = pooled * lax.rsqrt(jnp.sum(pooled * pooled, axis=1, keepdims=True) + norm_eps)
    speech_ref[...] = speech.astype(bf16)
    for n, part in enumerate(parts):
        send_ref[n * doc_rows : (n + 1) * doc_rows, :] = part[:doc_rows, :]
    send_ref[len(parts) * doc_rows :, :] = jnp.concatenate(
        [speech, jnp.zeros((3 * recs, width), f32)], 0
    ).astype(bf16)


def pair_terms(logits, positive):
    logits = logit_scale * logits + logit_shift
    signed = jnp.where(positive, -logits, logits)
    losses = jnp.maximum(signed, 0.0) + jnp.log1p(jnp.exp(-jnp.abs(signed)))
    slopes = jax.nn.sigmoid(signed)
    return losses, jnp.where(positive, -slopes, slopes).astype(bf16)


def speech_terms(place_ref, chunk, speech, docs):
    logits = lax.dot_general(speech, docs, BY_ROWS, preferred_element_type=f32)
    positive = lax.broadcasted_iota(jnp.int32, logits.shape, 1) == place_ref[:, chunk : chunk + 1]
    losses, grad_b = pair_terms(logits, positive)
    grad = logit_scale * jnp.dot(grad_b, docs, preferred_element_type=f32)
    return jnp.sum(losses, axis=1, keepdims=True), grad


def own_kernel(recs, place_ref, own_ref, other_ref, both_ref, loss_ref, grad_ref):
    doc_rows = own_ref.shape[0] - 4 * recs
    mine = own_ref[doc_rows:, :].astype(f32)[:recs]
    other = other_ref[...].astype(f32)
    both = jnp.concatenate([mine, other, jnp.zeros((2 * recs, mine.shape[1]), f32)], 0).astype(bf16)
    loss, grad = speech_terms(place_ref, 0, both, own_ref[:doc_rows, :])
    both_ref[...] = both
    loss_ref[...] = jnp.broadcast_to(loss, loss_ref.shape)
    grad_ref[...] = grad


def near_kernel(recs, place_ref, both_ref, near_ref, loss_ref, grad_ref, loss_out, grad_out, send_ref):
    doc_rows = near_ref.shape[0] - 4 * recs
    loss, grad = speech_terms(place_ref, 1, both_ref[...], near_ref[:doc_rows, :])
    loss, grad = loss_ref[...] + loss, grad_ref[...] + grad
    loss_out[...] = loss[:recs]
    grad_out[...] = grad[:recs]
    loss, grad = loss[recs : 2 * recs], grad[recs : 2 * recs]
    grad_high = grad.astype(bf16).astype(f32)
    loss_high = loss.astype(bf16).astype(f32)
    loss_low = (loss - loss_high).astype(bf16).astype(f32)
    terms = [loss_high, loss_low, loss - loss_high - loss_low]
    terms.append(jnp.zeros((recs, grad.shape[1] - 384), f32))
    send_ref[...] = jnp.concatenate(
        [grad_high, grad - grad_high, jnp.concatenate(terms, 1), jnp.zeros_like(grad)], 0
    ).astype(bf16)


def last_kernel(recs, at_ref, docs_ref, loss_ref, grad_ref, came_ref, *refs):
    row_refs, (loss_out, speech_out, doc_out) = refs[:-3], refs[-3:]
    came = came_ref[came_ref.shape[0] - 4 * recs :, :].astype(f32)
    speech_out[...] = grad_ref[...] + came[:recs] + came[recs : 2 * recs]
    terms = came[2 * recs : 3 * recs]
    loss = loss_ref[...] + (terms[:, :128] + terms[:, 128:256] + terms[:, 256:384])
    diagonal = lax.broadcasted_iota(jnp.int32, (recs, 128), 0)
    diagonal = diagonal == lax.broadcasted_iota(jnp.int32, (recs, 128), 1)
    loss_out[...] = jnp.sum(jnp.where(diagonal, loss, 0.0), axis=0, keepdims=True)[:, :recs]
    if len(row_refs) == 1:
        rows = row_refs[0][...]
    else:
        rows = jnp.concatenate([ref[: 4 * recs, :] for ref in row_refs], 0)
    logits = lax.dot_general(docs_ref[...], rows, BY_ROWS, preferred_element_type=f32)
    positive = lax.broadcasted_iota(jnp.int32, logits.shape, 0) == at_ref[:1, : logits.shape[1]]
    _, grad_b = pair_terms(logits, positive)
    doc_out[...] = logit_scale * jnp.dot(grad_b, rows, preferred_element_type=f32)


def swap_pairs(count, stride, steps):
    return [(source, source ^ (steps * stride)) for source in range(count)]


def is_direct(extent):
    return extent <= direct_limit and extent & (extent - 1) == 0


def gathered(value, axis, stride, extent):
    count = lax.axis_size(axis)
    if is_direct(extent):
        parts = [value] + [
            lax.ppermute(value, axis, swap_pairs(count, stride, steps)) for steps in range(1, extent)
        ]
        return parts, True
    groups = [
        [base + stride * step for step in range(extent)]
        for base in range(count)
        if (base // stride) % extent == 0
    ]
    whole = lax.all_gather(value, axis, axis_index_groups=groups)
    return [whole[step] for step in range(extent)], False


def body(features, frame_counts, pool_query, w_proj, doc_embed, doc_index):
    recs, frames, channels = features.shape
    heads, width = pool_query.shape[0], w_proj.shape[1]
    docs_dev = doc_embed.shape[0]
    groups, columns = lax.axis_size("grp"), lax.axis_size("tm")
    layers = groups // 2
    direct = layers == 4

    far_docs, far_origin = gathered(doc_embed, "grp", 4, layers // 2)
    blocks = []
    if direct:
        blocks = [(0, 0), (0, 1), None, None, (1, 0), (2, 0), (3, 0), None, (1, 1), (2, 1), (3, 1)]
    scheme = (docs_dev, layers // 2, is_direct(columns), far_origin)
    pools, place, at = pl.pallas_call(
        lambda *refs: pool_kernel(scheme, blocks, *refs),
        out_shape=(
            jax.ShapeDtypeStruct((4 * recs, width), bf16),
            jax.ShapeDtypeStruct((4 * recs, 128), jnp.int32),
            jax.ShapeDtypeStruct((8, 128), jnp.int32),
        ),
        in_specs=[pl.BlockSpec(memory_space=pltpu.HBM)] * 5,
        out_specs=(VMEM, VMEM, VMEM),
        scratch_shapes=[
            pltpu.SMEM(frame_counts.shape, jnp.int32),
            pltpu.SMEM(doc_index.shape, jnp.int32),
            pltpu.VMEM(pool_query.shape, bf16),
            pltpu.VMEM(features.shape, bf16),
            pltpu.VMEM(w_proj.shape, bf16),
            pltpu.SemaphoreType.DMA((recs + 4,)),
        ],
        compiler_params=pltpu.CompilerParams(vmem_limit_bytes=12 * 2**20),
        name="pool",
    )(
        *[
            pltpu.with_memory_space_constraint(operand, pltpu.HBM)
            for operand in (frame_counts, doc_index, pool_query, features, w_proj)
        ]
    )
    parts, _ = gathered(jnp.concatenate(far_docs + [pools]), "tm", 1, columns)
    doc_rows = columns * (layers // 2) * docs_dev
    own, speech = in_vmem(
        lambda *refs: meet_kernel(recs, heads, *refs),
        (
            jax.ShapeDtypeStruct((doc_rows + 4 * recs, width), bf16),
            jax.ShapeDtypeStruct((recs, width), bf16),
        ),
        8,
        "meet",
    )(*parts)

    pairs = swap_pairs(groups, 1, 1)
    near = lax.ppermute(own, "grp", swap_pairs(groups, 2, 1))
    other = lax.ppermute(speech, "grp", pairs)
    mib = 8 + doc_rows // 128
    both, loss, grad = in_vmem(
        lambda *refs: own_kernel(recs, *refs),
        (
            jax.ShapeDtypeStruct((4 * recs, width), bf16),
            jax.ShapeDtypeStruct((4 * recs, 128), f32),
            jax.ShapeDtypeStruct((4 * recs, width), f32),
        ),
        mib,
        "own_docs",
    )(place, own, other)
    loss, grad, send = in_vmem(
        lambda *refs: near_kernel(recs, *refs),
        (
            jax.ShapeDtypeStruct((recs, 128), f32),
            jax.ShapeDtypeStruct((recs, width), f32),
            jax.ShapeDtypeStruct((4 * recs, width), bf16),
        ),
        mib,
        "near_docs",
    )(place, both, near, loss, grad)

    if direct:
        beyond = [lax.ppermute(speech, "grp", swap_pairs(groups, 2, steps)) for steps in (2, 3)]
        spare = jnp.zeros((recs, width), bf16)
        send = jnp.concatenate([near[doc_rows : doc_rows + recs], *beyond, spare, send])
    came = lax.ppermute(send, "grp", pairs)
    if direct:
        rows = (both, send, came)
    else:
        rows = (lax.all_gather(speech, "grp", tiled=True),)
        at = (doc_index - (lax.axis_index("grp") * columns + lax.axis_index("tm")) * docs_dev)[None, :]
    loss, speech_grad, doc_grad = in_vmem(
        lambda *refs: last_kernel(recs, *refs),
        (
            jax.ShapeDtypeStruct((1, recs), f32),
            jax.ShapeDtypeStruct((recs, width), f32),
            jax.ShapeDtypeStruct((docs_dev, width), f32),
        ),
        8,
        "last",
    )(at, doc_embed, loss, grad, came, *rows)
    return (loss[0], speech_grad, doc_grad)


def solution(mesh):
    placed = (P("grp", "tm", None), P("grp"), P(), P(), P(("grp", "tm"), None), P())
    return jax.shard_map(
        body,
        mesh=mesh,
        in_specs=placed,
        out_specs=(P("grp"), P("grp", None), P(("grp", "tm"), None)),
        check_vma=False,
    )
```

time: 92.8 us -> 27.4 us (0.30)
  blocking collectives: 35.5 us -> 0 us
  waiting for transfers between devices: 37.8 us -> 8.12 us
  matrix products: 11.4 us -> 0 us
  starting transfers between devices: 1.76 us -> 12.1 us
  Pallas kernels: 0 us -> 5.36 us
  local copies, waits for them, and re-layouts: 3.66 us -> 0.82 us
  other arithmetic: 1.42 us -> 0 us
    ppermute x16 -> x9, waiting for transfers between devices: 37.8 us -> 8.12 us  [the longest x4 4.51 us: gathered(): lax.ppermute(value, axis, swap_pairs(count, stride, steps))]
    psum x2 -> x0, blocking collectives: 24.2 us -> none  [the longest x1 14.4 us: body(): numerator, totals = lax.psum((numerator, totals), 'tm')]
    dot_general x27 -> x0, matrix products: 11.4 us -> none  [the longest x1 2.47 us: body(): jnp.dot(features.reshape(rec_count * frame_dev, channels), w_proj, prefer...]
    pmax x1 -> x0, blocking collectives: 11.3 us -> none  [body(): peak_score = lax.pmax(jnp.max(masked, axis=2), 'tm')]
    ppermute x16 -> x9, starting transfers between devices: 1.76 us -> 12.1 us  [the longest x4 7.65 us: gathered(): lax.ppermute(value, axis, swap_pairs(count, stride, steps))]
    pallas_call x0 -> x5, Pallas kernels: none -> 5.36 us  [the longest x1 3.58 us: body(): pl.pallas_call(lambda *refs: pool_kernel(scheme, blocks, *refs), out_shap...]
    reshape x2 -> x0, local copies, waits for them, and re-layouts: 2.21 us -> none  [the longest x1 2.14 us: body(): values = values.reshape(rec_count, frame_dev, heads, width // heads)]
  transfers between devices with their start and end apart: 16 -> 9, of which waited for: 16 -> 7; matrix products, arithmetic and copies ran while one was open for 6% -> 3% of each run, Pallas kernels for 0% -> 16%
where the time goes in v2:
time: 27.4 us; the launch traced here: 27.1 us
  starting transfers between devices  12.1 us (44%)
  waiting for transfers between devices  8.12 us (30%)
  Pallas kernels  5.36 us (20%)
  local copies, waits for them, and re-layouts  0.82 us (3%)
  between operations  0.7 us (3%)
    ppermute x4, starting transfers between devices, gathered(): lax.ppermute(value, axis, swap_pairs(count, stride, steps))  7.65 us
    ppermute x4, waiting for transfers between devices, gathered(): lax.ppermute(value, axis, swap_pairs(count, stride, steps))  4.51 us
    pallas_call x1, Pallas kernels, body(): pl.pallas_call(lambda *refs: pool_kernel(scheme, blocks, *refs), out_shap...  3.58 us
    ppermute x2, starting transfers between devices, body(): lax.ppermute(speech, 'grp', swap_pairs(groups, 2, steps))  2.81 us
    ppermute x2, waiting for transfers between devices, body(): lax.ppermute(speech, 'grp', swap_pairs(groups, 2, steps))  1.98 us
    pallas_call x4, Pallas kernels, call(): pl.pallas_call(kernel, out_shape=outs, in_specs=[VMEM] * len(operands), o...  1.78 us
    ppermute x1, starting transfers between devices, body(): near = lax.ppermute(own, 'grp', swap_pairs(groups, 2, 1))  1.58 us
    ppermute x1, waiting for transfers between devices, body(): came = lax.ppermute(send, 'grp', pairs)  1.19 us
  transfers between devices with their start and end apart: 9, of which 7 were waited for; matrix products, arithmetic and copies ran while one was open for 3% of the time, Pallas kernels for 16%

profile of v2, /device:TPU:0, one launch (start us, length us, event | category | flops | bytes accessed | tf_op | source)
XLA Modules:
  0.0 27.1 jit_solution(7160069067250448420)
XLA Ops:
  0.6 0.0 copy-start
  0.6 4.1 %collective-permute-start = (bf16[16,512]{1,0:T(8,128)(2,1)}, bf16[16,512]{1,0:T(8,128)(2,1)S(1)}, u32[]{:S(2)}, u32[]{:S(2)}) collective-permute-start(bf16[16,512]{1,0:T(8,128)(2,1)} %refs_1_.3), channel_id=1, source_target_pairs={{0,16},{4,20},{8,24},{12,28},{16,0},{20,4},{24,8},{28,12},{1,17},{... | collective-permute-start | bytes 49160 | tf_op jit(solution)/shard_map/ppermute | solution.py:253
  4.7 0.8 %constant_dynamic-update-slice_fusion.2 = bf16[48,512]{1,0:T(8,128)(2,1)S(1)} fusion(bf16[16,512]{1,0:T(8,128)(2,1)} %refs_1_.3), kind=kLoop, calls=%fused_computation.2 | loop fusion | bytes 32768
  5.5 3.6 %pool.1 = (bf16[16,512]{1,0:T(8,128)(2,1)S(1)}, s32[16,128]{1,0:T(8,128)S(1)}, s32[8,128]{1,0:T(8,128)S(1)}) custom-call(s32[4]{0:T(128)} %refs_0_.1, s32[32]{0:T(128)} %refs_1_.2, bf16[8,1024]{1,0:T(8,128)(2,1)} %refs_2_.1, bf16[4,256,1024]{2,1,0:T(8,128)(2,1)} %refs_3_.1, bf16[1024,512]{1,0:T(8,128)(2,1)} %refs_4_.1), custom_call_target="tpu_custom_call" | custom-call | tf_op jit(solution)/shard_map/pool/pallas_call | solution.py:278
  9.1 0.0 collective-permute-done
  9.1 1.6 %collective-permute-start.1 = (bf16[48,512]{1,0:T(8,128)(2,1)S(1)}, bf16[48,512]{1,0:T(8,128)(2,1)S(1)}, u32[]{:S(2)}, u32[]{:S(2)}) collective-permute-start(bf16[48,512]{1,0:T(8,128)(2,1)S(1)} %constant_dynamic-update-slice_fusion.refs_0_), channel_id=1, source_target_pairs={{0,1},{1,0},{2,3},{3,2},{4,5},{5,4},{6,7},{7,6},{8,9},{9,8},{10,11... | collective-permute-start | bytes 147464 | tf_op jit(solution)/shard_map/ppermute | solution.py:253
  10.7 1.5 %collective-permute-start.2 = (bf16[48,512]{1,0:T(8,128)(2,1)S(1)}, bf16[48,512]{1,0:T(8,128)(2,1)S(1)}, u32[]{:S(2)}, u32[]{:S(2)}) collective-permute-start(bf16[48,512]{1,0:T(8,128)(2,1)S(1)} %constant_dynamic-update-slice_fusion.refs_0_), channel_id=1, source_target_pairs={{0,2},{1,3},{2,0},{3,1},{4,6},{5,7},{6,4},{7,5},{8,10},{9,11},{10,... | collective-permute-start | bytes 147464 | tf_op jit(solution)/shard_map/ppermute | solution.py:253
  12.2 0.5 %collective-permute-start.3 = (bf16[48,512]{1,0:T(8,128)(2,1)S(1)}, bf16[48,512]{1,0:T(8,128)(2,1)S(1)}, u32[]{:S(2)}, u32[]{:S(2)}) collective-permute-start(bf16[48,512]{1,0:T(8,128)(2,1)S(1)} %constant_dynamic-update-slice_fusion.refs_0_), channel_id=1, source_target_pairs={{0,3},{1,2},{2,1},{3,0},{4,7},{5,6},{6,5},{7,4},{8,11},{9,10},{10,... | collective-permute-start | bytes 147464 | tf_op jit(solution)/shard_map/ppermute | solution.py:253
  12.7 0.6 %collective-permute-done.1.refs_1_ = bf16[48,512]{1,0:T(8,128)(2,1)S(1)} collective-permute-done((bf16[48,512]{1,0:T(8,128)(2,1)S(1)}, bf16[48,512]{1,0:T(8,128)(2,1)S(1)}, u32[]{:S(2)}, u32[]{:S(2)}) %collective-permute-start.1) | collective-permute-done | bytes 49184 | tf_op jit(solution)/shard_map/ppermute | solution.py:253
  13.3 1.5 %collective-permute-done.2.refs_2_ = bf16[48,512]{1,0:T(8,128)(2,1)S(1)} collective-permute-done((bf16[48,512]{1,0:T(8,128)(2,1)S(1)}, bf16[48,512]{1,0:T(8,128)(2,1)S(1)}, u32[]{:S(2)}, u32[]{:S(2)}) %collective-permute-start.2) | collective-permute-done | bytes 49184 | tf_op jit(solution)/shard_map/ppermute | solution.py:253
  14.8 2.4 %collective-permute-done.3.refs_3_ = bf16[48,512]{1,0:T(8,128)(2,1)S(1)} collective-permute-done((bf16[48,512]{1,0:T(8,128)(2,1)S(1)}, bf16[48,512]{1,0:T(8,128)(2,1)S(1)}, u32[]{:S(2)}, u32[]{:S(2)}) %collective-permute-start.3) | collective-permute-done | bytes 49184 | tf_op jit(solution)/shard_map/ppermute | solution.py:253
  17.2 0.2 meet.1
  17.4 1.6 %collective-permute-start.5 = (bf16[144,512]{1,0:T(8,128)(2,1)S(1)}, bf16[144,512]{1,0:T(8,128)(2,1)S(1)}, u32[]{:S(2)}, u32[]{:S(2)}) collective-permute-start(bf16[144,512]{1,0:T(8,128)(2,1)S(1)} %get-tuple-element.20.refs_1_), channel_id=1, source_target_pairs={{0,8},{4,12},{8,0},{12,4},{16,24},{20,28},{24,16},{28,20},{1,9},{5... | collective-permute-start | bytes 442376 | tf_op jit(solution)/shard_map/ppermute | solution.py:316
  19.0 0.0 collective-permute-start.4
  19.0 0.5 %collective-permute-start.6 = (bf16[4,512]{1,0:T(4,128)(2,1)S(1)}, bf16[4,512]{1,0:T(4,128)(2,1)S(1)}, u32[]{:S(2)}, u32[]{:S(2)}) collective-permute-start(bf16[4,512]{1,0:T(4,128)(2,1)S(1)} %get-tuple-element.21), channel_id=1, source_target_pairs={{0,16},{4,20},{8,24},{12,28},{16,0},{20,4},{24,8},{28,12},{1,17},{... | collective-permute-start | bytes 12296 | tf_op jit(solution)/shard_map/ppermute | solution.py:341
  19.5 2.3 %collective-permute-start.7 = (bf16[4,512]{1,0:T(4,128)(2,1)S(1)}, bf16[4,512]{1,0:T(4,128)(2,1)S(1)}, u32[]{:S(2)}, u32[]{:S(2)}) collective-permute-start(bf16[4,512]{1,0:T(4,128)(2,1)S(1)} %get-tuple-element.21), channel_id=1, source_target_pairs={{0,24},{4,28},{8,16},{12,20},{16,8},{20,12},{24,0},{28,4},{1,25},{... | collective-permute-start | bytes 12296 | tf_op jit(solution)/shard_map/ppermute | solution.py:341
  21.8 0.0 collective-permute-done.4.refs_2_
  21.8 0.3 %own_docs.1 = (bf16[16,512]{1,0:T(8,128)(2,1)S(1)}, f32[16,128]{1,0:T(8,128)S(1)}, f32[16,512]{1,0:T(8,128)S(1)}) custom-call(s32[16,128]{1,0:T(8,128)S(1)} %get-tuple-element.18.refs_0_, bf16[144,512]{1,0:T(8,128)(2,1)S(1)} %get-tuple-element.20.refs_1_, bf16[4,512]{1,0:T(4,128)(2,1)S(1)} %collective-permute-done.4.refs_2_), custom_call_target="tpu_custom_call" | custom-call | tf_op jit(solution)/shard_map/own_docs/pallas_call | solution.py:22
  22.2 0.4 %collective-permute-done.5.refs_2_ = bf16[144,512]{1,0:T(8,128)(2,1)S(1)} collective-permute-done((bf16[144,512]{1,0:T(8,128)(2,1)S(1)}, bf16[144,512]{1,0:T(8,128)(2,1)S(1)}, u32[]{:S(2)}, u32[]{:S(2)}) %collective-permute-start.5) | collective-permute-done | bytes 147488 | tf_op jit(solution)/shard_map/ppermute | solution.py:316
  22.6 0.3 %near_docs.1 = (f32[4,128]{1,0:T(4,128)S(1)}, f32[4,512]{1,0:T(4,128)S(1)}, bf16[16,512]{1,0:T(8,128)(2,1)S(1)}) custom-call(s32[16,128]{1,0:T(8,128)S(1)} %get-tuple-element.18.refs_0_, bf16[16,512]{1,0:T(8,128)(2,1)S(1)} %get-tuple-element.22.refs_1_.refs_5_, bf16[144,512]{1,0:T(8,128)(2,1)S(1)} %collective-permute-done.5.refs_2_, ...), custom_call_target="tpu_custom_call" | custom-call | tf_op jit(solution)/shard_map/near_docs/pallas_call | solution.py:22
  22.9 0.6 %collective-permute-done.6 = bf16[4,512]{1,0:T(4,128)(2,1)S(1)} collective-permute-done((bf16[4,512]{1,0:T(4,128)(2,1)S(1)}, bf16[4,512]{1,0:T(4,128)(2,1)S(1)}, u32[]{:S(2)}, u32[]{:S(2)}) %collective-permute-start.6) | collective-permute-done | bytes 4128 | tf_op jit(solution)/shard_map/ppermute | solution.py:341
  23.5 1.4 %collective-permute-done.7 = bf16[4,512]{1,0:T(4,128)(2,1)S(1)} collective-permute-done((bf16[4,512]{1,0:T(4,128)(2,1)S(1)}, bf16[4,512]{1,0:T(4,128)(2,1)S(1)}, u32[]{:S(2)}, u32[]{:S(2)}) %collective-permute-start.7) | collective-permute-done | bytes 4128 | tf_op jit(solution)/shard_map/ppermute | solution.py:341
  24.9 0.1 collective-permute-start.8
  25.0 1.2 %collective-permute-done.8.refs_4_.refs_7_ = bf16[32,512]{1,0:T(8,128)(2,1)S(1)} collective-permute-done((bf16[32,512]{1,0:T(8,128)(2,1)S(1)}, bf16[32,512]{1,0:T(8,128)(2,1)S(1)}, u32[]{:S(2)}, u32[]{:S(2)}) %collective-permute-start.8) | collective-permute-done | bytes 32800 | tf_op jit(solution)/shard_map/ppermute | solution.py:344
  26.2 0.0 copy-done
  26.2 0.9 %last.1 = (f32[1,4]{1,0:T(1,128)}, f32[4,512]{1,0:T(4,128)}, f32[16,512]{1,0:T(8,128)}) custom-call(s32[8,128]{1,0:T(8,128)S(1)} %get-tuple-element.17.refs_0_, bf16[16,512]{1,0:T(8,128)(2,1)S(1)} %copy-done, f32[4,128]{1,0:T(4,128)S(1)} %get-tuple-element.25.refs_2_, f32[4,512]{1,0:T(4,128)S(1)} %get-tuple-element.26.refs_3_, ...), custom_call_target="tpu_custom_call" | custom-call | tf_op jit(solution)/shard_map/last/pallas_call | solution.py:22
  (5 shorter events, 0.1 us)
Async XLA Ops:
  0.6 25.6 %copy-start = (bf16[16,512]{1,0:T(8,128)(2,1)S(1)}, bf16[16,512]{1,0:T(8,128)(2,1)}, u32[]{:S(2)}) copy-start(bf16[16,512]{1,0:T(8,128)(2,1)} %refs_1_.3) | copy-start | bytes 49156
  0.6 8.4 %collective-permute-start = (bf16[16,512]{1,0:T(8,128)(2,1)}, bf16[16,512]{1,0:T(8,128)(2,1)S(1)}, u32[]{:S(2)}, u32[]{:S(2)}) collective-permute-start(bf16[16,512]{1,0:T(8,128)(2,1)} %refs_1_.3), channel_id=1, source_target_pairs={{0,16},{4,20},{8,24},{12,28},{16,0},{20,4},{24,8},{28,12},{1,17},{... | collective-permute-start | bytes 49160 | tf_op jit(solution)/shard_map/ppermute | solution.py:253
  9.1 4.2 %collective-permute-start.1 = (bf16[48,512]{1,0:T(8,128)(2,1)S(1)}, bf16[48,512]{1,0:T(8,128)(2,1)S(1)}, u32[]{:S(2)}, u32[]{:S(2)}) collective-permute-start(bf16[48,512]{1,0:T(8,128)(2,1)S(1)} %constant_dynamic-update-slice_fusion.refs_0_), channel_id=1, source_target_pairs={{0,1},{1,0},{2,3},{3,2},{4,5},{5,4},{6,7},{7,6},{8,9},{9,8},{10,11... | collective-permute-start | bytes 147464 | tf_op jit(solution)/shard_map/ppermute | solution.py:253
  10.7 4.1 %collective-permute-start.2 = (bf16[48,512]{1,0:T(8,128)(2,1)S(1)}, bf16[48,512]{1,0:T(8,128)(2,1)S(1)}, u32[]{:S(2)}, u32[]{:S(2)}) collective-permute-start(bf16[48,512]{1,0:T(8,128)(2,1)S(1)} %constant_dynamic-update-slice_fusion.refs_0_), channel_id=1, source_target_pairs={{0,2},{1,3},{2,0},{3,1},{4,6},{5,7},{6,4},{7,5},{8,10},{9,11},{10,... | collective-permute-start | bytes 147464 | tf_op jit(solution)/shard_map/ppermute | solution.py:253
  12.2 5.0 %collective-permute-start.3 = (bf16[48,512]{1,0:T(8,128)(2,1)S(1)}, bf16[48,512]{1,0:T(8,128)(2,1)S(1)}, u32[]{:S(2)}, u32[]{:S(2)}) collective-permute-start(bf16[48,512]{1,0:T(8,128)(2,1)S(1)} %constant_dynamic-update-slice_fusion.refs_0_), channel_id=1, source_target_pairs={{0,3},{1,2},{2,1},{3,0},{4,7},{5,6},{6,5},{7,4},{8,11},{9,10},{10,... | collective-permute-start | bytes 147464 | tf_op jit(solution)/shard_map/ppermute | solution.py:253
  17.4 5.2 %collective-permute-start.5 = (bf16[144,512]{1,0:T(8,128)(2,1)S(1)}, bf16[144,512]{1,0:T(8,128)(2,1)S(1)}, u32[]{:S(2)}, u32[]{:S(2)}) collective-permute-start(bf16[144,512]{1,0:T(8,128)(2,1)S(1)} %get-tuple-element.20.refs_1_), channel_id=1, source_target_pairs={{0,8},{4,12},{8,0},{12,4},{16,24},{20,28},{24,16},{28,20},{1,9},{5... | collective-permute-start | bytes 442376 | tf_op jit(solution)/shard_map/ppermute | solution.py:316
  19.0 2.8 %collective-permute-start.4 = (bf16[4,512]{1,0:T(4,128)(2,1)S(1)}, bf16[4,512]{1,0:T(4,128)(2,1)S(1)}, u32[]{:S(2)}, u32[]{:S(2)}) collective-permute-start(bf16[4,512]{1,0:T(4,128)(2,1)S(1)} %get-tuple-element.21), channel_id=1, source_target_pairs={{0,4},{4,0},{8,12},{12,8},{16,20},{20,16},{24,28},{28,24},{1,5},{5... | collective-permute-start | bytes 12296 | tf_op jit(solution)/shard_map/ppermute | solution.py:317
  19.0 4.5 %collective-permute-start.6 = (bf16[4,512]{1,0:T(4,128)(2,1)S(1)}, bf16[4,512]{1,0:T(4,128)(2,1)S(1)}, u32[]{:S(2)}, u32[]{:S(2)}) collective-permute-start(bf16[4,512]{1,0:T(4,128)(2,1)S(1)} %get-tuple-element.21), channel_id=1, source_target_pairs={{0,16},{4,20},{8,24},{12,28},{16,0},{20,4},{24,8},{28,12},{1,17},{... | collective-permute-start | bytes 12296 | tf_op jit(solution)/shard_map/ppermute | solution.py:341
  19.5 5.4 %collective-permute-start.7 = (bf16[4,512]{1,0:T(4,128)(2,1)S(1)}, bf16[4,512]{1,0:T(4,128)(2,1)S(1)}, u32[]{:S(2)}, u32[]{:S(2)}) collective-permute-start(bf16[4,512]{1,0:T(4,128)(2,1)S(1)} %get-tuple-element.21), channel_id=1, source_target_pairs={{0,24},{4,28},{8,16},{12,20},{16,8},{20,12},{24,0},{28,4},{1,25},{... | collective-permute-start | bytes 12296 | tf_op jit(solution)/shard_map/ppermute | solution.py:341
  24.9 1.3 %collective-permute-start.8 = (bf16[32,512]{1,0:T(8,128)(2,1)S(1)}, bf16[32,512]{1,0:T(8,128)(2,1)S(1)}, u32[]{:S(2)}, u32[]{:S(2)}) collective-permute-start(bf16[32,512]{1,0:T(8,128)(2,1)S(1)} %concatenate.7.refs_6_), channel_id=1, source_target_pairs={{0,4},{4,0},{8,12},{12,8},{16,20},{20,16},{24,28},{28,24},{1,5},{5... | collective-permute-start | bytes 98312 | tf_op jit(solution)/shard_map/ppermute | solution.py:344

commit v3 on v2

v3 whole, which is shorter than its diff:
```python
import math

import jax
import jax.numpy as jnp
from jax import lax
from jax.experimental import pallas as pl
from jax.experimental.pallas import tpu as pltpu
from jax.sharding import PartitionSpec as P

logit_scale = 10.0
logit_shift = -8.0
norm_eps = 1e-06
direct_limit = 8
bf16 = jnp.bfloat16
f32 = jnp.float32
BY_ROWS = (((1,), (1,)), ((), ()))
VMEM = pl.BlockSpec(memory_space=pltpu.VMEM)


def in_vmem(kernel, outs, limit_mib, name):
    def call(*operands):
        return pl.pallas_call(
            kernel,
            out_shape=outs,
            in_specs=[VMEM] * len(operands),
            out_specs=jax.tree.map(lambda _: VMEM, outs),
            compiler_params=pltpu.CompilerParams(vmem_limit_bytes=limit_mib * 2**20),
            name=name,
        )(*operands)

    return call


def two_terms(value):
    high = value.astype(bf16)
    return high, (value - high.astype(f32)).astype(bf16)


def pool_kernel(
    scheme,
    blocks,
    counts_hbm,
    index_hbm,
    query_hbm,
    features_hbm,
    proj_hbm,
    docs_hbm,
    out_ref,
    place_ref,
    at_ref,
    counts_ref,
    index_ref,
    query_ref,
    features_ref,
    proj_ref,
    sems,
):
    recs, frames, channels = features_ref.shape
    heads = query_ref.shape[0]
    width = proj_ref.shape[1]
    rows = recs * heads
    docs_dev, by_column, by_layer = scheme
    copies = [
        pltpu.make_async_copy(source, target, sems.at[n])
        for n, (source, target) in enumerate(
            [(counts_hbm, counts_ref), (index_hbm, index_ref), (query_hbm, query_ref)]
            + [(features_hbm.at[r], features_ref.at[r]) for r in range(recs)]
            + [(proj_hbm, proj_ref), (docs_hbm, out_ref.at[:docs_dev])]
        )
    ]
    for copy in copies:
        copy.start()
    copies[1].wait()
    group, column, tm = lax.axis_index("grp"), lax.axis_index("tm"), lax.axis_size("tm")
    layer, core = group // 2, group % 2
    row = lax.broadcasted_iota(jnp.int32, place_ref.shape, 0)
    spot = lax.broadcasted_iota(jnp.int32, place_ref.shape, 1)
    place = jnp.full(place_ref.shape, -1, jnp.int32)
    for r in range(2 * recs):
        target = index_ref[(group ^ (r // recs)) * recs + r % recs]
        of_group, rest = target // (tm * docs_dev), target % (tm * docs_dev)
        of_layer = of_group // 2
        at = ((rest // docs_dev) ^ (column if by_column else 0)) * docs_dev + rest % docs_dev
        chunk = of_layer ^ layer if by_layer else 0
        at = at if by_layer else of_layer * tm * docs_dev + at
        chunk = jnp.where((of_group ^ core) % 2 == 0, chunk, -1)
        place = jnp.where((row == r) & (spot == chunk), at, place)
    place_ref[...] = place
    spot = lax.broadcasted_iota(jnp.int32, at_ref.shape, 1)
    ats = jnp.full(at_ref.shape, -1, jnp.int32)
    first = (group * tm + column) * docs_dev
    for n, block in enumerate(blocks):
        if block is not None:
            base = ((layer ^ block[0]) * 2 + (core ^ block[1])) * recs
            for r in range(recs):
                ats = jnp.where(spot == n * recs + r, index_ref[base + r] - first, ats)
    at_ref[...] = ats
    copies[0].wait()
    copies[2].wait()
    query = jnp.concatenate([query_ref[...].astype(f32), jnp.zeros((128 - heads, channels), f32)], 0).T.astype(bf16)
    start = lax.axis_index("tm") * frames
    spots = lax.broadcasted_iota(jnp.int32, (heads, frames), 1)
    scores, weights, peaks, totals, highs, lows = [], [], [], [], [], []
    for step in range(recs + 2):
        if step < recs:
            copies[3 + step].wait()
            scores.append(
                jnp.dot(features_ref[step], query, preferred_element_type=f32).T[:heads]
            )
        if 0 <= step - 1 < recs:
            r = step - 1
            valid = spots < counts_ref[r] - start
            masked = jnp.where(valid, scores[r] / math.sqrt(channels), -1e30)
            peak = jnp.max(masked, axis=1, keepdims=True).astype(bf16).astype(f32)
            weight = jnp.where(valid, jnp.exp(masked - peak), 0.0)
            peaks.append(peak)
            totals.append(jnp.sum(weight, axis=1, keepdims=True))
            weights.append(jnp.concatenate(two_terms(weight), 0))
        if 0 <= step - 2 < recs:
            r = step - 2
            both = jnp.dot(weights[r], features_ref[r], preferred_element_type=f32)
            high, low = two_terms(both[:heads] + both[heads:])
            highs.append(high)
            lows.append(low)
    peak, totals = jnp.concatenate(peaks, 0), jnp.concatenate(totals, 0)
    copies[3 + recs].wait()
    wide = jnp.dot(jnp.concatenate(highs + lows, 0), proj_ref[...], preferred_element_type=f32)
    wide = wide[:rows] + wide[rows:]
    own = lax.broadcasted_iota(jnp.int32, (rows, width), 1) // (width // heads)
    own = own == lax.broadcasted_iota(jnp.int32, (rows, width), 0) % heads
    lane = lax.broadcasted_iota(jnp.int32, (rows, 128), 1)
    lane = lane == lax.broadcasted_iota(jnp.int32, (rows, 128), 0) % heads

    def over_heads(value):
        return jnp.concatenate(
            [jnp.sum(value[r * heads : (r + 1) * heads], 0, keepdims=True) for r in range(recs)], 0
        )

    pooled = over_heads(jnp.where(own, wide, 0.0))
    pooled_high = pooled.astype(bf16).astype(f32)
    totals = over_heads(jnp.where(lane, totals, 0.0))
    totals_high = totals.astype(bf16).astype(f32)
    peaks = over_heads(jnp.where(lane, peak, 0.0))
    stats = [peaks, totals_high, totals - totals_high, jnp.zeros((recs, width - 384), f32)]
    copies[4 + recs].wait()
    out_ref[docs_dev:, :] = jnp.concatenate(
        [pooled_high, pooled - pooled_high, jnp.concatenate(stats, 1), jnp.zeros((recs, width), f32)], 0
    ).astype(bf16)


def meet_kernel(recs, heads, *refs):
    parts, (send_ref, speech_ref) = refs[:-2], refs[-2:]
    doc_rows = parts[0].shape[0] - 4 * recs
    width = parts[0].shape[1]
    pools = [part[doc_rows:, :].astype(f32) for part in parts]
    peaks = [pool[2 * recs : 3 * recs, :128] for pool in pools]
    totals = [pool[2 * recs : 3 * recs, 128:256] + pool[2 * recs : 3 * recs, 256:384] for pool in pools]
    top = peaks[0]
    for peak in peaks[1:]:
        top = jnp.maximum(top, peak)
    shares = [jnp.exp(peak - top) for peak in peaks]
    whole = shares[0] * totals[0]
    for share, total in zip(shares[1:], totals[1:]):
        whole = whole + share * total
    used = lax.broadcasted_iota(jnp.int32, whole.shape, 1) < heads
    inverse = jnp.where(used, 1.0 / jnp.where(used, whole, 1.0), 0.0)
    high, low = two_terms(jnp.concatenate([share * inverse for share in shares], 0))
    spread = lax.broadcasted_iota(jnp.int32, (128, width), 1) // (width // heads)
    spread = (spread == lax.broadcasted_iota(jnp.int32, (128, width), 0)).astype(f32).astype(bf16)
    scales = jnp.dot(high, spread, preferred_element_type=f32) + jnp.dot(
        low, spread, preferred_element_type=f32
    )
    pooled = jnp.zeros((recs, width), f32)
    for n, pool in enumerate(pools):
        pooled = pooled + (pool[:recs] + pool[recs : 2 * recs]) * scales[n * recs : (n + 1) * recs]
    speech = pooled * lax.rsqrt(jnp.sum(pooled * pooled, axis=1, keepdims=True) + norm_eps)
    speech_ref[...] = speech.astype(bf16)
    for n, part in enumerate(parts):
        send_ref[n * doc_rows : (n + 1) * doc_rows, :] = part[:doc_rows, :]
    send_ref[len(parts) * doc_rows :, :] = jnp.concatenate(
        [speech, jnp.zeros((recs, width), f32)], 0
    ).astype(bf16)


def pair_terms(logits, positive):
    logits = logit_scale * logits + logit_shift
    signed = jnp.where(positive, -logits, logits)
    losses = jnp.maximum(signed, 0.0) + jnp.log1p(jnp.exp(-jnp.abs(signed)))
    slopes = jax.nn.sigmoid(signed)
    return losses, jnp.where(positive, -slopes, slopes).astype(bf16)


def speech_terms(place_ref, chunk, speech, docs):
    logits = lax.dot_general(speech, docs, BY_ROWS, preferred_element_type=f32)
    positive = lax.broadcasted_iota(jnp.int32, logits.shape, 1) == place_ref[:, chunk : chunk + 1]
    losses, grad_b = pair_terms(logits, positive)
    grad = logit_scale * jnp.dot(grad_b, docs, preferred_element_type=f32)
    return jnp.sum(losses, axis=1, keepdims=True), grad


def first_docs_kernel(recs, place_ref, own_ref, other_ref, docs_ref, both_ref, loss_ref, grad_ref):
    mine = own_ref[own_ref.shape[0] - 2 * recs :, :].astype(f32)[:recs]
    other = other_ref[...].astype(f32)
    both = jnp.concatenate([mine, other, jnp.zeros((2 * recs, mine.shape[1]), f32)], 0).astype(bf16)
    loss, grad = speech_terms(place_ref, 0, both, docs_ref[: docs_ref.shape[0] - 2 * recs, :])
    both_ref[...] = both
    loss_ref[...] = jnp.broadcast_to(loss, loss_ref.shape)
    grad_ref[...] = grad


def next_docs_kernel(recs, chunk, place_ref, both_ref, loss_ref, grad_ref, docs_ref, loss_out, grad_out):
    doc_rows = docs_ref.shape[0] - 2 * recs
    loss, grad = speech_terms(place_ref, chunk, both_ref[...], docs_ref[:doc_rows, :])
    loss_out[...] = loss_ref[...] + loss
    grad_out[...] = grad_ref[...] + grad


def share_kernel(recs, chunk, place_ref, both_ref, loss_ref, grad_ref, *refs):
    blocks, (loss_out, grad_out, send_ref) = refs[:-3], refs[-3:]
    loss, grad = loss_ref[...], grad_ref[...]
    head = []
    if blocks:
        doc_rows = blocks[0].shape[0] - 2 * recs
        more = speech_terms(place_ref, chunk, both_ref[...], blocks[-1][:doc_rows, :])
        loss, grad = loss + more[0], grad + more[1]
        head = [block[doc_rows:, :].astype(f32)[:recs] for block in blocks]
        head = [jnp.concatenate(head + [jnp.zeros_like(head[0])], 0)]
    loss_out[...] = loss[:recs]
    grad_out[...] = grad[:recs]
    loss, grad = loss[recs : 2 * recs], grad[recs : 2 * recs]
    grad_high = grad.astype(bf16).astype(f32)
    loss_high = loss.astype(bf16).astype(f32)
    loss_low = (loss - loss_high).astype(bf16).astype(f32)
    terms = [loss_high, loss_low, loss - loss_high - loss_low]
    terms.append(jnp.zeros((recs, grad.shape[1] - 384), f32))
    send_ref[...] = jnp.concatenate(
        head + [grad_high, grad - grad_high, jnp.concatenate(terms, 1), jnp.zeros_like(grad)], 0
    ).astype(bf16)


def last_kernel(recs, at_ref, docs_ref, loss_ref, grad_ref, came_ref, *refs):
    row_refs, (loss_out, speech_out, doc_out) = refs[:-3], refs[-3:]
    came = came_ref[came_ref.shape[0] - 4 * recs :, :].astype(f32)
    speech_out[...] = grad_ref[...] + came[:recs] + came[recs : 2 * recs]
    terms = came[2 * recs : 3 * recs]
    loss = loss_ref[...] + (terms[:, :128] + terms[:, 128:256] + terms[:, 256:384])
    diagonal = lax.broadcasted_iota(jnp.int32, (recs, 128), 0)
    diagonal = diagonal == lax.broadcasted_iota(jnp.int32, (recs, 128), 1)
    loss_out[...] = jnp.sum(jnp.where(diagonal, loss, 0.0), axis=0, keepdims=True)[:, :recs]
    if len(row_refs) == 1:
        rows = row_refs[0][...]
    else:
        rows = jnp.concatenate([ref[: 4 * recs, :] for ref in row_refs], 0)
    logits = lax.dot_general(docs_ref[...], rows, BY_ROWS, preferred_element_type=f32)
    positive = lax.broadcasted_iota(jnp.int32, logits.shape, 0) == at_ref[:1, : logits.shape[1]]
    _, grad_b = pair_terms(logits, positive)
    doc_out[...] = logit_scale * jnp.dot(grad_b, rows, preferred_element_type=f32)


def swap_pairs(count, stride, steps):
    return [(source, source ^ (steps * stride)) for source in range(count)]


def is_direct(extent):
    return extent <= direct_limit and extent & (extent - 1) == 0


def gathered(value, axis, stride, extent):
    count = lax.axis_size(axis)
    if is_direct(extent):
        parts = [value] + [
            lax.ppermute(value, axis, swap_pairs(count, stride, steps)) for steps in range(1, extent)
        ]
        return parts
    groups = [
        [base + stride * step for step in range(extent)]
        for base in range(count)
        if (base // stride) % extent == 0
    ]
    whole = lax.all_gather(value, axis, axis_index_groups=groups)
    return [whole[step] for step in range(extent)]


def body(features, frame_counts, pool_query, w_proj, doc_embed, doc_index):
    recs, frames, channels = features.shape
    heads, width = pool_query.shape[0], w_proj.shape[1]
    docs_dev = doc_embed.shape[0]
    groups, columns = lax.axis_size("grp"), lax.axis_size("tm")
    layers = groups // 2
    direct = layers == 4
    order = (2, 3, 1) if direct else ()

    def shape(rows, lanes, kind=f32):
        return jax.ShapeDtypeStruct((rows, lanes), kind)

    blocks = []
    if direct:
        blocks = [(0, 0), (0, 1), None, None, *[(n, 0) for n in order], None, *[(n, 1) for n in order]]
    payload, place, at = pl.pallas_call(
        lambda *refs: pool_kernel((docs_dev, is_direct(columns), direct), blocks, *refs),
        out_shape=(
            shape(docs_dev + 4 * recs, width, bf16),
            shape(4 * recs, 128, jnp.int32),
            shape(8, 128, jnp.int32),
        ),
        in_specs=[pl.BlockSpec(memory_space=pltpu.HBM)] * 6,
        out_specs=(VMEM, VMEM, VMEM),
        scratch_shapes=[
            pltpu.SMEM(frame_counts.shape, jnp.int32),
            pltpu.SMEM(doc_index.shape, jnp.int32),
            pltpu.VMEM(pool_query.shape, bf16),
            pltpu.VMEM(features.shape, bf16),
            pltpu.VMEM(w_proj.shape, bf16),
            pltpu.SemaphoreType.DMA((recs + 5,)),
        ],
        compiler_params=pltpu.CompilerParams(vmem_limit_bytes=12 * 2**20),
        name="pool",
    )(
        *[
            pltpu.with_memory_space_constraint(operand, pltpu.HBM)
            for operand in (frame_counts, doc_index, pool_query, features, w_proj, doc_embed)
        ]
    )
    parts = gathered(payload, "tm", 1, columns)
    doc_rows = columns * docs_dev
    own, speech = in_vmem(
        lambda *refs: meet_kernel(recs, heads, *refs),
        (shape(doc_rows + 2 * recs, width, bf16), shape(recs, width, bf16)),
        8,
        "meet",
    )(*parts)

    pairs = swap_pairs(groups, 1, 1)
    other = lax.ppermute(speech, "grp", pairs)
    if direct:
        came = [lax.ppermute(own, "grp", swap_pairs(groups, 2, steps)) for steps in order]
        docs = own
    else:
        came = []
        docs = jnp.concatenate([part[:doc_rows] for part in gathered(own, "grp", 2, layers)] + [own[doc_rows:]])
    mib = 8 + docs.shape[0] // 128
    both, loss, grad = in_vmem(
        lambda *refs: first_docs_kernel(recs, *refs),
        (shape(4 * recs, width, bf16), shape(4 * recs, 128), shape(4 * recs, width)),
        mib,
        "first_docs",
    )(place, own, other, docs)
    for n, block in zip(order[:-1], came[:-1]):
        loss, grad = in_vmem(
            lambda *refs, chunk=n: next_docs_kernel(recs, chunk, *refs),
            (shape(4 * recs, 128), shape(4 * recs, width)),
            8,
            "next_docs",
        )(place, both, loss, grad, block)
    send_rows = 4 * recs * (2 if direct else 1)
    loss, grad, send = in_vmem(
        lambda *refs: share_kernel(recs, order[-1] if order else 0, *refs),
        (shape(recs, 128), shape(recs, width), shape(send_rows, width, bf16)),
        8,
        "share",
    )(place, both, loss, grad, *came)
    back = lax.ppermute(send, "grp", pairs)
    if direct:
        rows = (both, send, back)
    else:
        rows = (lax.all_gather(speech, "grp", tiled=True),)
        at = (doc_index - (lax.axis_index("grp") * columns + lax.axis_index("tm")) * docs_dev)[None, :]
    loss, speech_grad, doc_grad = in_vmem(
        lambda *refs: last_kernel(recs, *refs),
        (shape(1, recs), shape(recs, width), shape(docs_dev, width)),
        8,
        "last",
    )(at, doc_embed, loss, grad, back, *rows)
    return (loss[0], speech_grad, doc_grad)


def solution(mesh):
    placed = (P("grp", "tm", None), P("grp"), P(), P(), P(("grp", "tm"), None), P())
    return jax.shard_map(
        body,
        mesh=mesh,
        in_specs=placed,
        out_specs=(P("grp"), P("grp", None), P(("grp", "tm"), None)),
        check_vma=False,
    )
```

time: 27.4 us -> 24.2 us (0.88)
  starting transfers between devices: 12.1 us -> 8.84 us
  waiting for transfers between devices: 8.12 us -> 9.13 us
  local copies, waits for them, and re-layouts: 0.82 us -> 0.01 us
    ppermute x4 -> x3, starting transfers between devices: 7.65 us -> 4.6 us  [gathered(): lax.ppermute(value, axis, swap_pairs(count, stride, steps))]
    ppermute x1, waiting for transfers between devices: 0.01 us -> 1.16 us  [body(): other = lax.ppermute(speech, 'grp', pairs)]
    unnamed x4 -> x2, local copies, waits for them, and re-layouts: 0.76 us -> 0.01 us
    ppermute x4 -> x3, waiting for transfers between devices: 4.51 us -> 3.78 us  [gathered(): lax.ppermute(value, axis, swap_pairs(count, stride, steps))]
    ppermute x4, waiting for transfers between devices: 3.6 us -> 4.18 us  [the longest x3 2.99 us: body(): lax.ppermute(own, 'grp', swap_pairs(groups, 2, steps))]
    pallas_call x4 -> x6, Pallas kernels: 1.78 us -> 2.27 us  [call(): pl.pallas_call(kernel, out_shape=outs, in_specs=[VMEM] * len(operands), o...]
    pallas_call x1, Pallas kernels: 3.58 us -> 3.09 us  [body(): pl.pallas_call(lambda *refs: pool_kernel((docs_dev, is_direct(columns), d...]
  transfers between devices with their start and end apart: 9 -> 8, of which waited for: 7 -> 7; matrix products, arithmetic and copies ran while one was open for 3% -> 0% of each run, Pallas kernels for 16% -> 4%
where the time goes in v3:
time: 24.2 us; the launch traced here: 24 us
  waiting for transfers between devices  9.13 us (38%)
  starting transfers between devices  8.84 us (37%)
  Pallas kernels  5.36 us (22%)
  between operations  0.68 us (3%)
    ppermute x3, starting transfers between devices, gathered(): lax.ppermute(value, axis, swap_pairs(count, stride, steps))  4.6 us
    ppermute x3, starting transfers between devices, body(): lax.ppermute(own, 'grp', swap_pairs(groups, 2, steps))  4.16 us
    ppermute x3, waiting for transfers between devices, gathered(): lax.ppermute(value, axis, swap_pairs(count, stride, steps))  3.78 us
    pallas_call x1, Pallas kernels, body(): pl.pallas_call(lambda *refs: pool_kernel((docs_dev, is_direct(columns), d...  3.09 us
    ppermute x3, waiting for transfers between devices, body(): lax.ppermute(own, 'grp', swap_pairs(groups, 2, steps))  2.99 us
    pallas_call x6, Pallas kernels, call(): pl.pallas_call(kernel, out_shape=outs, in_specs=[VMEM] * len(operands), o...  2.27 us
    ppermute x1, waiting for transfers between devices, body(): back = lax.ppermute(send, 'grp', pairs)  1.19 us
    ppermute x1, waiting for transfers between devices, body(): other = lax.ppermute(speech, 'grp', pairs)  1.16 us
  transfers between devices with their start and end apart: 8, of which 7 were waited for; matrix products, arithmetic and copies ran while one was open for 0% of the time, Pallas kernels for 4%

profile of v3, /device:TPU:0, one launch (start us, length us, event | category | flops | bytes accessed | tf_op | source)
XLA Modules:
  0.0 24.0 jit_solution(8430751891888750481)
XLA Ops:
  0.6 0.0 copy-start
  0.6 3.1 %pool.1 = (bf16[32,512]{1,0:T(8,128)(2,1)S(1)}, s32[16,128]{1,0:T(8,128)S(1)}, s32[8,128]{1,0:T(8,128)S(1)}) custom-call(s32[4]{0:T(128)} %refs_0_.1, s32[32]{0:T(128)} %refs_1_.2, bf16[8,1024]{1,0:T(8,128)(2,1)} %refs_2_.1, bf16[4,256,1024]{2,1,0:T(8,128)(2,1)} %refs_3_.1, bf16[1024,512]{1,0:T(8,128)(2,1)} %refs_4_.1, bf16[16,512]{1,0:T(8,128)(2,1)} %refs_1_.3), custom_call_target="tpu_custom_call" | custom-call | tf_op jit(solution)/shard_map/pool/pallas_call | solution.py:299
  3.7 4.0 %collective-permute-start.2 = (bf16[32,512]{1,0:T(8,128)(2,1)S(1)}, bf16[32,512]{1,0:T(8,128)(2,1)S(1)}, u32[]{:S(2)}, u32[]{:S(2)}) collective-permute-start(bf16[32,512]{1,0:T(8,128)(2,1)S(1)} %get-tuple-element.23.refs_0_), channel_id=1, source_target_pairs={{0,3},{1,2},{2,1},{3,0},{4,7},{5,6},{6,5},{7,4},{8,11},{9,10},{10,... | collective-permute-start | bytes 98312 | tf_op jit(solution)/shard_map/ppermute | solution.py:272
  7.7 0.5 %collective-permute-start.1 = (bf16[32,512]{1,0:T(8,128)(2,1)S(1)}, bf16[32,512]{1,0:T(8,128)(2,1)S(1)}, u32[]{:S(2)}, u32[]{:S(2)}) collective-permute-start(bf16[32,512]{1,0:T(8,128)(2,1)S(1)} %get-tuple-element.23.refs_0_), channel_id=1, source_target_pairs={{0,2},{1,3},{2,0},{3,1},{4,6},{5,7},{6,4},{7,5},{8,10},{9,11},{10,... | collective-permute-start | bytes 98312 | tf_op jit(solution)/shard_map/ppermute | solution.py:272
  8.2 0.1 collective-permute-start
  8.3 1.3 %collective-permute-done.2.refs_3_ = bf16[32,512]{1,0:T(8,128)(2,1)S(1)} collective-permute-done((bf16[32,512]{1,0:T(8,128)(2,1)S(1)}, bf16[32,512]{1,0:T(8,128)(2,1)S(1)}, u32[]{:S(2)}, u32[]{:S(2)}) %collective-permute-start.2) | collective-permute-done | bytes 32800 | tf_op jit(solution)/shard_map/ppermute | solution.py:272
  9.6 2.0 %collective-permute-done.1.refs_2_ = bf16[32,512]{1,0:T(8,128)(2,1)S(1)} collective-permute-done((bf16[32,512]{1,0:T(8,128)(2,1)S(1)}, bf16[32,512]{1,0:T(8,128)(2,1)S(1)}, u32[]{:S(2)}, u32[]{:S(2)}) %collective-permute-start.1) | collective-permute-done | bytes 32800 | tf_op jit(solution)/shard_map/ppermute | solution.py:272
  11.6 0.5 %collective-permute-done.refs_1_ = bf16[32,512]{1,0:T(8,128)(2,1)S(1)} collective-permute-done((bf16[32,512]{1,0:T(8,128)(2,1)S(1)}, bf16[32,512]{1,0:T(8,128)(2,1)S(1)}, u32[]{:S(2)}, u32[]{:S(2)}) %collective-permute-start) | collective-permute-done | bytes 32800 | tf_op jit(solution)/shard_map/ppermute | solution.py:272
  12.1 0.2 %meet.1 = (bf16[72,512]{1,0:T(8,128)(2,1)S(1)}, bf16[4,512]{1,0:T(4,128)(2,1)S(1)}) custom-call(bf16[32,512]{1,0:T(8,128)(2,1)S(1)} %get-tuple-element.23.refs_0_, bf16[32,512]{1,0:T(8,128)(2,1)S(1)} %collective-permute-done.refs_1_, bf16[32,512]{1,0:T(8,128)(2,1)S(1)} %collective-permute-done.1.refs_2_, bf16[32,512]{1,0:T(8,128)(2,1)S(1)} %collective-permute-done.2.refs_3_), custom_call_target="tpu_custom_call" | custom-call | tf_op jit(solution)/shard_map/meet/pallas_call | solution.py:22
  12.4 2.6 %collective-permute-start.4 = (bf16[72,512]{1,0:T(8,128)(2,1)S(1)}, bf16[72,512]{1,0:T(8,128)(2,1)S(1)}, u32[]{:S(2)}, u32[]{:S(2)}) collective-permute-start(bf16[72,512]{1,0:T(8,128)(2,1)S(1)} %get-tuple-element.24.refs_1_.refs_3_), channel_id=1, source_target_pairs={{0,16},{4,20},{8,24},{12,28},{16,0},{20,4},{24,8},{28,12},{1,17},{... | collective-permute-start | bytes 221192 | tf_op jit(solution)/shard_map/ppermute | solution.py:336
  15.0 1.4 %collective-permute-start.5 = (bf16[72,512]{1,0:T(8,128)(2,1)S(1)}, bf16[72,512]{1,0:T(8,128)(2,1)S(1)}, u32[]{:S(2)}, u32[]{:S(2)}) collective-permute-start(bf16[72,512]{1,0:T(8,128)(2,1)S(1)} %get-tuple-element.24.refs_1_.refs_3_), channel_id=1, source_target_pairs={{0,24},{4,28},{8,16},{12,20},{16,8},{20,12},{24,0},{28,4},{1,25},{... | collective-permute-start | bytes 221192 | tf_op jit(solution)/shard_map/ppermute | solution.py:336
  16.3 0.2 collective-permute-start.6
  16.5 0.0 collective-permute-start.3
  16.5 1.2 %collective-permute-done.3.refs_2_ = bf16[4,512]{1,0:T(4,128)(2,1)S(1)} collective-permute-done((bf16[4,512]{1,0:T(4,128)(2,1)S(1)}, bf16[4,512]{1,0:T(4,128)(2,1)S(1)}, u32[]{:S(2)}, u32[]{:S(2)}) %collective-permute-start.3) | collective-permute-done | bytes 4128 | tf_op jit(solution)/shard_map/ppermute | solution.py:334
  17.7 0.3 %first_docs.1 = (bf16[16,512]{1,0:T(8,128)(2,1)S(1)}, f32[16,128]{1,0:T(8,128)S(1)}, f32[16,512]{1,0:T(8,128)S(1)}) custom-call(s32[16,128]{1,0:T(8,128)S(1)} %get-tuple-element.22.refs_0_, bf16[72,512]{1,0:T(8,128)(2,1)S(1)} %get-tuple-element.24.refs_1_.refs_3_, bf16[4,512]{1,0:T(4,128)(2,1)S(1)} %collective-permute-done.3.refs_2_, ...), custom_call_target="tpu_custom_call" | custom-call | tf_op jit(solution)/shard_map/first_docs/pallas_call | solution.py:22
  18.0 1.6 %collective-permute-done.4.refs_4_ = bf16[72,512]{1,0:T(8,128)(2,1)S(1)} collective-permute-done((bf16[72,512]{1,0:T(8,128)(2,1)S(1)}, bf16[72,512]{1,0:T(8,128)(2,1)S(1)}, u32[]{:S(2)}, u32[]{:S(2)}) %collective-permute-start.4) | collective-permute-done | bytes 73760 | tf_op jit(solution)/shard_map/ppermute | solution.py:336
  19.6 0.3 %next_docs.2 = (f32[16,128]{1,0:T(8,128)S(1)}, f32[16,512]{1,0:T(8,128)S(1)}) custom-call(s32[16,128]{1,0:T(8,128)S(1)} %get-tuple-element.22.refs_0_, bf16[16,512]{1,0:T(8,128)(2,1)S(1)} %get-tuple-element.26.refs_1_.refs_5_, f32[16,128]{1,0:T(8,128)S(1)} %get-tuple-element.27.refs_2_, f32[16,512]{1,0:T(8,128)S(1)} %get-tuple-element.28.refs_3_, ...), custom_call_target="tpu_custom_call" | custom-call | tf_op jit(solution)/shard_map/next_docs/pallas_call | solution.py:22
  19.9 1.4 %collective-permute-done.5.refs_4_.refs_5_ = bf16[72,512]{1,0:T(8,128)(2,1)S(1)} collective-permute-done((bf16[72,512]{1,0:T(8,128)(2,1)S(1)}, bf16[72,512]{1,0:T(8,128)(2,1)S(1)}, u32[]{:S(2)}, u32[]{:S(2)}) %collective-permute-start.5) | collective-permute-done | bytes 73760 | tf_op jit(solution)/shard_map/ppermute | solution.py:336
  21.3 0.3 %next_docs.3 = (f32[16,128]{1,0:T(8,128)S(1)}, f32[16,512]{1,0:T(8,128)S(1)}) custom-call(s32[16,128]{1,0:T(8,128)S(1)} %get-tuple-element.22.refs_0_, bf16[16,512]{1,0:T(8,128)(2,1)S(1)} %get-tuple-element.26.refs_1_.refs_5_, f32[16,128]{1,0:T(8,128)S(1)} %get-tuple-element.29.refs_2_, f32[16,512]{1,0:T(8,128)S(1)} %get-tuple-element.30.refs_3_, ...), custom_call_target="tpu_custom_call" | custom-call | tf_op jit(solution)/shard_map/next_docs/pallas_call | solution.py:22
  21.5 0.0 collective-permute-done.6.refs_6_
  21.5 0.3 %share.1 = (f32[4,128]{1,0:T(4,128)S(1)}, f32[4,512]{1,0:T(4,128)S(1)}, bf16[32,512]{1,0:T(8,128)(2,1)S(1)}) custom-call(s32[16,128]{1,0:T(8,128)S(1)} %get-tuple-element.22.refs_0_, bf16[16,512]{1,0:T(8,128)(2,1)S(1)} %get-tuple-element.26.refs_1_.refs_5_, f32[16,128]{1,0:T(8,128)S(1)} %get-tuple-element.31.refs_2_, ...), custom_call_target="tpu_custom_call" | custom-call | tf_op jit(solution)/shard_map/share/pallas_call | solution.py:22
  21.8 0.1 collective-permute-start.7
  21.9 1.2 %collective-permute-done.7.refs_4_.refs_7_ = bf16[32,512]{1,0:T(8,128)(2,1)S(1)} collective-permute-done((bf16[32,512]{1,0:T(8,128)(2,1)S(1)}, bf16[32,512]{1,0:T(8,128)(2,1)S(1)}, u32[]{:S(2)}, u32[]{:S(2)}) %collective-permute-start.7) | collective-permute-done | bytes 32800 | tf_op jit(solution)/shard_map/ppermute | solution.py:362
  23.1 0.0 copy-done
  23.1 0.9 %last.1 = (f32[1,4]{1,0:T(1,128)}, f32[4,512]{1,0:T(4,128)}, f32[16,512]{1,0:T(8,128)}) custom-call(s32[8,128]{1,0:T(8,128)S(1)} %get-tuple-element.21.refs_0_, bf16[16,512]{1,0:T(8,128)(2,1)S(1)} %copy-done, f32[4,128]{1,0:T(4,128)S(1)} %get-tuple-element.33.refs_2_, f32[4,512]{1,0:T(4,128)S(1)} %get-tuple-element.34.refs_3_, ...), custom_call_target="tpu_custom_call" | custom-call | tf_op jit(solution)/shard_map/last/pallas_call | solution.py:22
Async XLA Ops:
  0.6 22.5 %copy-start = (bf16[16,512]{1,0:T(8,128)(2,1)S(1)}, bf16[16,512]{1,0:T(8,128)(2,1)}, u32[]{:S(2)}) copy-start(bf16[16,512]{1,0:T(8,128)(2,1)} %refs_1_.3) | copy-start | bytes 49156
  3.7 5.9 %collective-permute-start.2 = (bf16[32,512]{1,0:T(8,128)(2,1)S(1)}, bf16[32,512]{1,0:T(8,128)(2,1)S(1)}, u32[]{:S(2)}, u32[]{:S(2)}) collective-permute-start(bf16[32,512]{1,0:T(8,128)(2,1)S(1)} %get-tuple-element.23.refs_0_), channel_id=1, source_target_pairs={{0,3},{1,2},{2,1},{3,0},{4,7},{5,6},{6,5},{7,4},{8,11},{9,10},{10,... | collective-permute-start | bytes 98312 | tf_op jit(solution)/shard_map/ppermute | solution.py:272
  7.7 3.9 %collective-permute-start.1 = (bf16[32,512]{1,0:T(8,128)(2,1)S(1)}, bf16[32,512]{1,0:T(8,128)(2,1)S(1)}, u32[]{:S(2)}, u32[]{:S(2)}) collective-permute-start(bf16[32,512]{1,0:T(8,128)(2,1)S(1)} %get-tuple-element.23.refs_0_), channel_id=1, source_target_pairs={{0,2},{1,3},{2,0},{3,1},{4,6},{5,7},{6,4},{7,5},{8,10},{9,11},{10,... | collective-permute-start | bytes 98312 | tf_op jit(solution)/shard_map/ppermute | solution.py:272
  8.2 3.9 %collective-permute-start = (bf16[32,512]{1,0:T(8,128)(2,1)S(1)}, bf16[32,512]{1,0:T(8,128)(2,1)S(1)}, u32[]{:S(2)}, u32[]{:S(2)}) collective-permute-start(bf16[32,512]{1,0:T(8,128)(2,1)S(1)} %get-tuple-element.23.refs_0_), channel_id=1, source_target_pairs={{0,1},{1,0},{2,3},{3,2},{4,5},{5,4},{6,7},{7,6},{8,9},{9,8},{10,11... | collective-permute-start | bytes 98312 | tf_op jit(solution)/shard_map/ppermute | solution.py:272
  12.4 7.2 %collective-permute-start.4 = (bf16[72,512]{1,0:T(8,128)(2,1)S(1)}, bf16[72,512]{1,0:T(8,128)(2,1)S(1)}, u32[]{:S(2)}, u32[]{:S(2)}) collective-permute-start(bf16[72,512]{1,0:T(8,128)(2,1)S(1)} %get-tuple-element.24.refs_1_.refs_3_), channel_id=1, source_target_pairs={{0,16},{4,20},{8,24},{12,28},{16,0},{20,4},{24,8},{28,12},{1,17},{... | collective-permute-start | bytes 221192 | tf_op jit(solution)/shard_map/ppermute | solution.py:336
  15.0 6.3 %collective-permute-start.5 = (bf16[72,512]{1,0:T(8,128)(2,1)S(1)}, bf16[72,512]{1,0:T(8,128)(2,1)S(1)}, u32[]{:S(2)}, u32[]{:S(2)}) collective-permute-start(bf16[72,512]{1,0:T(8,128)(2,1)S(1)} %get-tuple-element.24.refs_1_.refs_3_), channel_id=1, source_target_pairs={{0,24},{4,28},{8,16},{12,20},{16,8},{20,12},{24,0},{28,4},{1,25},{... | collective-permute-start | bytes 221192 | tf_op jit(solution)/shard_map/ppermute | solution.py:336
  16.3 5.2 %collective-permute-start.6 = (bf16[72,512]{1,0:T(8,128)(2,1)S(1)}, bf16[72,512]{1,0:T(8,128)(2,1)S(1)}, u32[]{:S(2)}, u32[]{:S(2)}) collective-permute-start(bf16[72,512]{1,0:T(8,128)(2,1)S(1)} %get-tuple-element.24.refs_1_.refs_3_), channel_id=1, source_target_pairs={{0,8},{4,12},{8,0},{12,4},{16,24},{20,28},{24,16},{28,20},{1,9},{5... | collective-permute-start | bytes 221192 | tf_op jit(solution)/shard_map/ppermute | solution.py:336
  16.5 1.2 %collective-permute-start.3 = (bf16[4,512]{1,0:T(4,128)(2,1)S(1)}, bf16[4,512]{1,0:T(4,128)(2,1)S(1)}, u32[]{:S(2)}, u32[]{:S(2)}) collective-permute-start(bf16[4,512]{1,0:T(4,128)(2,1)S(1)} %get-tuple-element.25), channel_id=1, source_target_pairs={{0,4},{4,0},{8,12},{12,8},{16,20},{20,16},{24,28},{28,24},{1,5},{5... | collective-permute-start | bytes 12296 | tf_op jit(solution)/shard_map/ppermute | solution.py:334
  21.8 1.3 %collective-permute-start.7 = (bf16[32,512]{1,0:T(8,128)(2,1)S(1)}, bf16[32,512]{1,0:T(8,128)(2,1)S(1)}, u32[]{:S(2)}, u32[]{:S(2)}) collective-permute-start(bf16[32,512]{1,0:T(8,128)(2,1)S(1)} %get-tuple-element.35.refs_6_), channel_id=1, source_target_pairs={{0,4},{4,0},{8,12},{12,8},{16,20},{20,16},{24,28},{28,24},{1,5},{5... | collective-permute-start | bytes 98312 | tf_op jit(solution)/shard_map/ppermute | solution.py:362

commit v4 on v3

--- a/solution.py
+++ b/solution.py
@@ -77,13 +77,21 @@
     spot = lax.broadcasted_iota(jnp.int32, place_ref.shape, 1)
     place = jnp.full(place_ref.shape, -1, jnp.int32)
     for r in range(2 * recs):
-        target = index_ref[(group ^ (r // recs)) * recs + r % recs]
+        target = index_ref[(group ^ (1 - r // recs)) * recs + r % recs]
         of_group, rest = target // (tm * docs_dev), target % (tm * docs_dev)
         of_layer = of_group // 2
-        at = ((rest // docs_dev) ^ (column if by_column else 0)) * docs_dev + rest % docs_dev
-        chunk = of_layer ^ layer if by_layer else 0
-        at = at if by_layer else of_layer * tm * docs_dev + at
-        chunk = jnp.where((of_group ^ core) % 2 == 0, chunk, -1)
+        at = (rest // docs_dev) ^ (tm - 1 - column if by_column else 0)
+        if by_layer:
+            steps = of_layer ^ layer
+            far = steps // 2
+            at = (at * 2 + far) * docs_dev + rest % docs_dev
+            chunk = steps % 2
+            mine = (chunk + far + of_group + core) % 2 == 1
+        else:
+            at = (of_layer * tm + at) * docs_dev + rest % docs_dev
+            chunk = 0
+            mine = (of_group + core) % 2 == 1
+        chunk = jnp.where(mine, chunk, -1)
         place = jnp.where((row == r) & (spot == chunk), at, place)
     place_ref[...] = place
     spot = lax.broadcasted_iota(jnp.int32, at_ref.shape, 1)
@@ -148,11 +156,11 @@
     ).astype(bf16)
 
 
-def meet_kernel(recs, heads, *refs):
+def meet_kernel(recs, heads, docs_dev, *refs):
     parts, (send_ref, speech_ref) = refs[:-2], refs[-2:]
     doc_rows = parts[0].shape[0] - 4 * recs
     width = parts[0].shape[1]
-    pools = [part[doc_rows:, :].astype(f32) for part in parts]
+    pools = [part[docs_dev : docs_dev + 4 * recs, :].astype(f32) for part in parts]
     peaks = [pool[2 * recs : 3 * recs, :128] for pool in pools]
     totals = [pool[2 * recs : 3 * recs, 128:256] + pool[2 * recs : 3 * recs, 256:384] for pool in pools]
     top = peaks[0]
@@ -176,7 +184,9 @@
     speech = pooled * lax.rsqrt(jnp.sum(pooled * pooled, axis=1, keepdims=True) + norm_eps)
     speech_ref[...] = speech.astype(bf16)
     for n, part in enumerate(parts):
-        send_ref[n * doc_rows : (n + 1) * doc_rows, :] = part[:doc_rows, :]
+        send_ref[n * doc_rows : n * doc_rows + docs_dev, :] = part[:docs_dev, :]
+        if doc_rows > docs_dev:
+            send_ref[n * doc_rows + docs_dev : (n + 1) * doc_rows, :] = part[docs_dev + 4 * recs :, :]
     send_ref[len(parts) * doc_rows :, :] = jnp.concatenate(
         [speech, jnp.zeros((recs, width), f32)], 0
     ).astype(bf16)
@@ -198,51 +208,42 @@
     return jnp.sum(losses, axis=1, keepdims=True), grad
 
 
-def first_docs_kernel(recs, place_ref, own_ref, other_ref, docs_ref, both_ref, loss_ref, grad_ref):
-    mine = own_ref[own_ref.shape[0] - 2 * recs :, :].astype(f32)[:recs]
-    other = other_ref[...].astype(f32)
-    both = jnp.concatenate([mine, other, jnp.zeros((2 * recs, mine.shape[1]), f32)], 0).astype(bf16)
-    loss, grad = speech_terms(place_ref, 0, both, docs_ref[: docs_ref.shape[0] - 2 * recs, :])
-    both_ref[...] = both
+def first_docs_kernel(place_ref, both_ref, docs_ref, loss_ref, grad_ref):
+    recs = both_ref.shape[0] // 4
+    loss, grad = speech_terms(place_ref, 0, both_ref[...], docs_ref[: docs_ref.shape[0] - 2 * recs, :])
     loss_ref[...] = jnp.broadcast_to(loss, loss_ref.shape)
     grad_ref[...] = grad
 
 
-def next_docs_kernel(recs, chunk, place_ref, both_ref, loss_ref, grad_ref, docs_ref, loss_out, grad_out):
-    doc_rows = docs_ref.shape[0] - 2 * recs
-    loss, grad = speech_terms(place_ref, chunk, both_ref[...], docs_ref[:doc_rows, :])
-    loss_out[...] = loss_ref[...] + loss
-    grad_out[...] = grad_ref[...] + grad
-
-
-def share_kernel(recs, chunk, place_ref, both_ref, loss_ref, grad_ref, *refs):
+def share_kernel(place_ref, both_ref, loss_ref, grad_ref, *refs):
     blocks, (loss_out, grad_out, send_ref) = refs[:-3], refs[-3:]
+    recs = both_ref.shape[0] // 4
     loss, grad = loss_ref[...], grad_ref[...]
-    head = []
-    if blocks:
-        doc_rows = blocks[0].shape[0] - 2 * recs
-        more = speech_terms(place_ref, chunk, both_ref[...], blocks[-1][:doc_rows, :])
+    head = jnp.zeros((recs, grad.shape[1]), f32)
+    for block in blocks:
+        doc_rows = block.shape[0] - 2 * recs
+        more = speech_terms(place_ref, 1, both_ref[...], block[:doc_rows, :])
         loss, grad = loss + more[0], grad + more[1]
-        head = [block[doc_rows:, :].astype(f32)[:recs] for block in blocks]
-        head = [jnp.concatenate(head + [jnp.zeros_like(head[0])], 0)]
-    loss_out[...] = loss[:recs]
-    grad_out[...] = grad[:recs]
-    loss, grad = loss[recs : 2 * recs], grad[recs : 2 * recs]
+        head = block[doc_rows:, :].astype(f32)[:recs]
+    loss_out[...] = loss[recs : 2 * recs]
+    grad_out[...] = grad[recs : 2 * recs]
+    loss, grad = loss[:recs], grad[:recs]
     grad_high = grad.astype(bf16).astype(f32)
     loss_high = loss.astype(bf16).astype(f32)
     loss_low = (loss - loss_high).astype(bf16).astype(f32)
     terms = [loss_high, loss_low, loss - loss_high - loss_low]
     terms.append(jnp.zeros((recs, grad.shape[1] - 384), f32))
     send_ref[...] = jnp.concatenate(
-        head + [grad_high, grad - grad_high, jnp.concatenate(terms, 1), jnp.zeros_like(grad)], 0
+        [head, grad_high, grad - grad_high, jnp.concatenate(terms, 1)], 0
     ).astype(bf16)
 
 
-def last_kernel(recs, at_ref, docs_ref, loss_ref, grad_ref, came_ref, *refs):
+def last_kernel(at_ref, docs_ref, loss_ref, grad_ref, back_ref, *refs):
     row_refs, (loss_out, speech_out, doc_out) = refs[:-3], refs[-3:]
-    came = came_ref[came_ref.shape[0] - 4 * recs :, :].astype(f32)
-    speech_out[...] = grad_ref[...] + came[:recs] + came[recs : 2 * recs]
-    terms = came[2 * recs : 3 * recs]
+    recs = speech_out.shape[0]
+    back = back_ref[...].astype(f32)
+    speech_out[...] = grad_ref[...] + back[recs : 2 * recs] + back[2 * recs : 3 * recs]
+    terms = back[3 * recs :]
     loss = loss_ref[...] + (terms[:, :128] + terms[:, 128:256] + terms[:, 256:384])
     diagonal = lax.broadcasted_iota(jnp.int32, (recs, 128), 0)
     diagonal = diagonal == lax.broadcasted_iota(jnp.int32, (recs, 128), 1)
@@ -250,7 +251,9 @@
     if len(row_refs) == 1:
         rows = row_refs[0][...]
     else:
-        rows = jnp.concatenate([ref[: 4 * recs, :] for ref in row_refs], 0)
+        both, send, *beyond = [ref[...].astype(f32) for ref in row_refs]
+        beyond = [part[: 2 * recs] for part in beyond]
+        rows = jnp.concatenate([both, send[:recs], back[:recs], *beyond], 0).astype(bf16)
     logits = lax.dot_general(docs_ref[...], rows, BY_ROWS, preferred_element_type=f32)
     positive = lax.broadcasted_iota(jnp.int32, logits.shape, 0) == at_ref[:1, : logits.shape[1]]
     _, grad_b = pair_terms(logits, positive)
@@ -265,20 +268,15 @@
     return extent <= direct_limit and extent & (extent - 1) == 0
 
 
-def gathered(value, axis, stride, extent):
-    count = lax.axis_size(axis)
-    if is_direct(extent):
-        parts = [value] + [
-            lax.ppermute(value, axis, swap_pairs(count, stride, steps)) for steps in range(1, extent)
-        ]
-        return parts
-    groups = [
-        [base + stride * step for step in range(extent)]
-        for base in range(count)
-        if (base // stride) % extent == 0
-    ]
-    whole = lax.all_gather(value, axis, axis_index_groups=groups)
-    return [whole[step] for step in range(extent)]
+def to_other_core(value):
+    return lax.ppermute(value, "grp", swap_pairs(lax.axis_size("grp"), 1, 1))
+
+
+def crossing(value, layer_steps, column_steps):
+    columns = lax.axis_size("tm")
+    count = lax.axis_size("grp") * columns
+    steps = (2 * layer_steps + 1) * columns + column_steps
+    return lax.ppermute(value, ("grp", "tm"), swap_pairs(count, 1, steps))
 
 
 def body(features, frame_counts, pool_query, w_proj, doc_embed, doc_index):
@@ -288,14 +286,16 @@
     groups, columns = lax.axis_size("grp"), lax.axis_size("tm")
     layers = groups // 2
     direct = layers == 4
-    order = (2, 3, 1) if direct else ()
+    order = (3, 2) if direct else ()
 
     def shape(rows, lanes, kind=f32):
         return jax.ShapeDtypeStruct((rows, lanes), kind)
 
     blocks = []
     if direct:
-        blocks = [(0, 0), (0, 1), None, None, *[(n, 0) for n in order], None, *[(n, 1) for n in order]]
+        blocks = [(0, 1), (0, 0), None, None, (1, 0), (1, 1)]
+        blocks += [(steps, flip) for steps in order for flip in (0, 1)]
+        far = crossing(doc_embed, 2, 0)
     payload, place, at = pl.pallas_call(
         lambda *refs: pool_kernel((docs_dev, is_direct(columns), direct), blocks, *refs),
         out_shape=(
@@ -321,52 +321,53 @@
             for operand in (frame_counts, doc_index, pool_query, features, w_proj, doc_embed)
         ]
     )
-    parts = gathered(payload, "tm", 1, columns)
-    doc_rows = columns * docs_dev
+    if direct:
+        payload = jnp.concatenate([payload, far])
+    parts = [to_other_core(payload)]
+    if is_direct(columns):
+        parts = [crossing(payload, 0, steps) for steps in range(columns - 1, 0, -1)] + parts
+    else:
+        parts = list(lax.all_gather(parts[0], "tm"))
+    doc_rows = columns * (payload.shape[0] - 4 * recs)
     own, speech = in_vmem(
-        lambda *refs: meet_kernel(recs, heads, *refs),
+        lambda *refs: meet_kernel(recs, heads, docs_dev, *refs),
         (shape(doc_rows + 2 * recs, width, bf16), shape(recs, width, bf16)),
         8,
         "meet",
     )(*parts)
 
-    pairs = swap_pairs(groups, 1, 1)
-    other = lax.ppermute(speech, "grp", pairs)
+    other = to_other_core(speech)
+    chip = jnp.concatenate([speech, other])
+    both = jnp.concatenate([chip, jnp.zeros((2 * recs, width), bf16)])
+    docs, near = own, []
     if direct:
-        came = [lax.ppermute(own, "grp", swap_pairs(groups, 2, steps)) for steps in order]
-        docs = own
+        near = [crossing(own, 1, 0)]
+        beyond = [crossing(both, steps, 0) for steps in order]
     else:
-        came = []
-        docs = jnp.concatenate([part[:doc_rows] for part in gathered(own, "grp", 2, layers)] + [own[doc_rows:]])
-    mib = 8 + docs.shape[0] // 128
-    both, loss, grad = in_vmem(
-        lambda *refs: first_docs_kernel(recs, *refs),
-        (shape(4 * recs, width, bf16), shape(4 * recs, 128), shape(4 * recs, width)),
-        mib,
+        same_core = [[2 * n + core for n in range(layers)] for core in range(2)]
+        docs = lax.all_gather(own[:doc_rows], "grp", axis_index_groups=same_core, tiled=True)
+        docs = jnp.concatenate([docs, own[doc_rows:]])
+    loss, grad = in_vmem(
+        first_docs_kernel,
+        (shape(4 * recs, 128), shape(4 * recs, width)),
+        8 + docs.shape[0] // 128,
         "first_docs",
-    )(place, own, other, docs)
-    for n, block in zip(order[:-1], came[:-1]):
-        loss, grad = in_vmem(
-            lambda *refs, chunk=n: next_docs_kernel(recs, chunk, *refs),
-            (shape(4 * recs, 128), shape(4 * recs, width)),
-            8,
-            "next_docs",
-        )(place, both, loss, grad, block)
-    send_rows = 4 * recs * (2 if direct else 1)
+    )(place, both, docs)
     loss, grad, send = in_vmem(
-        lambda *refs: share_kernel(recs, order[-1] if order else 0, *refs),
-        (shape(recs, 128), shape(recs, width), shape(send_rows, width, bf16)),
+        share_kernel,
+        (shape(recs, 128), shape(recs, width), shape(4 * recs, width, bf16)),
         8,
         "share",
-    )(place, both, loss, grad, *came)
-    back = lax.ppermute(send, "grp", pairs)
+    )(place, both, loss, grad, *near)
+    back = to_other_core(send)
     if direct:
-        rows = (both, send, back)
+        rows = (both, send, *beyond)
     else:
         rows = (lax.all_gather(speech, "grp", tiled=True),)
-        at = (doc_index - (lax.axis_index("grp") * columns + lax.axis_index("tm")) * docs_dev)[None, :]
+        at = doc_index.reshape(layers, 2, recs)[:, ::-1].reshape(1, -1)
+        at = at - (lax.axis_index("grp") * columns + lax.axis_index("tm")) * docs_dev
     loss, speech_grad, doc_grad = in_vmem(
-        lambda *refs: last_kernel(recs, *refs),
+        last_kernel,
         (shape(1, recs), shape(recs, width), shape(docs_dev, width)),
         8,
         "last",

time: 24.2 us -> 23.5 us (0.971)
  waiting for transfers between devices: 9.13 us -> 6.42 us
  starting transfers between devices: 8.84 us -> 11.3 us
  Pallas kernels: 5.36 us -> 4.78 us
    ppermute x8 -> x10, waiting for transfers between devices: 9.13 us -> 6.42 us  [the longest x7 6.41 us: crossing(): return lax.ppermute(value, ('grp', 'tm'), swap_pairs(count, 1, steps))]
    ppermute x8 -> x10, starting transfers between devices: 8.84 us -> 11.3 us  [the longest x7 10.8 us: crossing(): return lax.ppermute(value, ('grp', 'tm'), swap_pairs(count, 1, steps))]
    pallas_call x6 -> x4, Pallas kernels: 2.27 us -> 1.78 us  [call(): pl.pallas_call(kernel, out_shape=outs, in_specs=[VMEM] * len(operands), o...]
  transfers between devices with their start and end apart: 8 -> 10, of which waited for: 7 -> 5; matrix products, arithmetic and copies ran while one was open for 0% -> 1% of each run, Pallas kernels for 4% -> 16%
where the time goes in v4:
time: 23.5 us; the launch traced here: 23.4 us
  starting transfers between devices  11.3 us (48%)
  waiting for transfers between devices  6.42 us (27%)
  Pallas kernels  4.78 us (20%)
  between operations  0.69 us (3%)
    ppermute x7, starting transfers between devices, crossing(): return lax.ppermute(value, ('grp', 'tm'), swap_pairs(count, 1, steps))  10.8 us
    ppermute x7, waiting for transfers between devices, crossing(): return lax.ppermute(value, ('grp', 'tm'), swap_pairs(count, 1, steps))  6.41 us
    pallas_call x1, Pallas kernels, body(): pl.pallas_call(lambda *refs: pool_kernel((docs_dev, is_direct(columns), d...  3 us
    pallas_call x4, Pallas kernels, call(): pl.pallas_call(kernel, out_shape=outs, in_specs=[VMEM] * len(operands), o...  1.78 us
    ppermute x3, starting transfers between devices, to_other_core(): return lax.ppermute(value, 'grp', swap_pairs(lax.axis_size('grp'), 1, 1))  0.49 us
  transfers between devices with their start and end apart: 10, of which 5 were waited for; matrix products, arithmetic and copies ran while one was open for 1% of the time, Pallas kernels for 16%

profile of v4, /device:TPU:0, one launch (start us, length us, event | category | flops | bytes accessed | tf_op | source)
XLA Modules:
  0.0 23.4 jit_solution(12482778613895401192)
XLA Ops:
  0.6 0.0 copy-start
  0.6 3.5 %collective-permute-start = (bf16[16,512]{1,0:T(8,128)(2,1)}, bf16[16,512]{1,0:T(8,128)(2,1)S(1)}, u32[]{:S(2)}, u32[]{:S(2)}) collective-permute-start(bf16[16,512]{1,0:T(8,128)(2,1)} %docs_ref.1), channel_id=1, source_target_pairs={{0,20},{1,21},{2,22},{3,23},{4,16},{5,17},{6,18},{7,19},{8,28},{9,... | collective-permute-start | bytes 49160 | tf_op jit(solution)/shard_map/ppermute | solution.py:279
  4.2 3.0 %pool.1 = (bf16[32,512]{1,0:T(8,128)(2,1)S(1)}, s32[16,128]{1,0:T(8,128)S(1)}, s32[8,128]{1,0:T(8,128)S(1)}) custom-call(s32[4]{0:T(128)} %refs_0_.1, s32[32]{0:T(128)} %refs_1_.1, bf16[8,1024]{1,0:T(8,128)(2,1)} %refs_2_.1, bf16[4,256,1024]{2,1,0:T(8,128)(2,1)} %refs_3_.1, bf16[1024,512]{1,0:T(8,128)(2,1)} %refs_4_.1, bf16[16,512]{1,0:T(8,128)(2,1)} %docs_ref.1), custom_call_target="tpu_custom_call" | custom-call | tf_op jit(solution)/shard_map/pool/pallas_call | solution.py:299
  7.2 0.0 collective-permute-done
  7.2 2.8 %collective-permute-start.1 = (bf16[48,512]{1,0:T(8,128)(2,1)S(1)}, bf16[48,512]{1,0:T(8,128)(2,1)S(1)}, u32[]{:S(2)}, u32[]{:S(2)}) collective-permute-start(bf16[48,512]{1,0:T(8,128)(2,1)S(1)} %constant_dynamic-update-slice_fusion), channel_id=1, source_target_pairs={{0,7},{1,6},{2,5},{3,4},{4,3},{5,2},{6,1},{7,0},{8,15},{9,14},{10,... | collective-permute-start | bytes 147464 | tf_op jit(solution)/shard_map/ppermute | solution.py:279
  10.0 0.0 collective-permute-start.2
  10.0 0.8 %collective-permute-start.3 = (bf16[48,512]{1,0:T(8,128)(2,1)S(1)}, bf16[48,512]{1,0:T(8,128)(2,1)S(1)}, u32[]{:S(2)}, u32[]{:S(2)}) collective-permute-start(bf16[48,512]{1,0:T(8,128)(2,1)S(1)} %constant_dynamic-update-slice_fusion), channel_id=1, source_target_pairs={{0,5},{1,4},{2,7},{3,6},{4,1},{5,0},{6,3},{7,2},{8,13},{9,12},{10,... | collective-permute-start | bytes 147464 | tf_op jit(solution)/shard_map/ppermute | solution.py:279
  10.8 0.0 collective-permute-start.4
  10.8 1.3 %collective-permute-done.1.refs_0_ = bf16[48,512]{1,0:T(8,128)(2,1)S(1)} collective-permute-done((bf16[48,512]{1,0:T(8,128)(2,1)S(1)}, bf16[48,512]{1,0:T(8,128)(2,1)S(1)}, u32[]{:S(2)}, u32[]{:S(2)}) %collective-permute-start.1) | collective-permute-done | bytes 49184 | tf_op jit(solution)/shard_map/ppermute | solution.py:279
  12.1 2.0 %collective-permute-done.2.refs_1_ = bf16[48,512]{1,0:T(8,128)(2,1)S(1)} collective-permute-done((bf16[48,512]{1,0:T(8,128)(2,1)S(1)}, bf16[48,512]{1,0:T(8,128)(2,1)S(1)}, u32[]{:S(2)}, u32[]{:S(2)}) %collective-permute-start.2) | collective-permute-done | bytes 49184 | tf_op jit(solution)/shard_map/ppermute | solution.py:279
  14.0 0.0 collective-permute-done.3.refs_2_
  14.1 0.0 collective-permute-done.4.refs_3_
  14.1 0.2 %meet.1 = (bf16[136,512]{1,0:T(8,128)(2,1)S(1)}, bf16[4,512]{1,0:T(4,128)(2,1)S(1)}) custom-call(bf16[48,512]{1,0:T(8,128)(2,1)S(1)} %collective-permute-done.1.refs_0_, bf16[48,512]{1,0:T(8,128)(2,1)S(1)} %collective-permute-done.2.refs_1_, bf16[48,512]{1,0:T(8,128)(2,1)S(1)} %collective-permute-done.3.refs_2_, ...), custom_call_target="tpu_custom_call" | custom-call | tf_op jit(solution)/shard_map/meet/pallas_call | solution.py:22
  14.3 0.1 collective-permute-start.5
  14.4 0.1 pad.2.clone
  14.5 1.6 %collective-permute-start.6 = (bf16[136,512]{1,0:T(8,128)(2,1)S(1)}, bf16[136,512]{1,0:T(8,128)(2,1)S(1)}, u32[]{:S(2)}, u32[]{:S(2)}) collective-permute-start(bf16[136,512]{1,0:T(8,128)(2,1)S(1)} %get-tuple-element.20.docs_ref), channel_id=1, source_target_pairs={{0,12},{1,13},{2,14},{3,15},{4,8},{5,9},{6,10},{7,11},{8,4},{9,5},... | collective-permute-start | bytes 417800 | tf_op jit(solution)/shard_map/ppermute | solution.py:279
  16.1 0.0 collective-permute-done.5
  16.1 0.1 maximum_maximum_fusion.both_ref.refs_0_
  16.2 2.0 %collective-permute-start.8 = (bf16[16,512]{1,0:T(8,128)(2,1)S(1)}, bf16[16,512]{1,0:T(8,128)(2,1)S(1)}, u32[]{:S(2)}, u32[]{:S(2)}) collective-permute-start(bf16[16,512]{1,0:T(8,128)(2,1)S(1)} %maximum_maximum_fusion.both_ref.refs_0_), channel_id=1, source_target_pairs={{0,28},{1,29},{2,30},{3,31},{4,24},{5,25},{6,26},{7,27},{8,20},{9,... | collective-permute-start | bytes 49160 | tf_op jit(solution)/shard_map/ppermute | solution.py:279
  18.2 0.1 collective-permute-start.9
  18.3 0.3 %first_docs.1 = (f32[16,128]{1,0:T(8,128)S(1)}, f32[16,512]{1,0:T(8,128)S(1)}) custom-call(s32[16,128]{1,0:T(8,128)S(1)} %get-tuple-element.17.place_ref, bf16[16,512]{1,0:T(8,128)(2,1)S(1)} %maximum_maximum_fusion.both_ref.refs_0_, bf16[136,512]{1,0:T(8,128)(2,1)S(1)} %get-tuple-element.20.docs_ref), custom_call_target="tpu_custom_call" | custom-call | tf_op jit(solution)/shard_map/first_docs/pallas_call | solution.py:22
  18.6 1.4 %collective-permute-done.6.refs_0_ = bf16[136,512]{1,0:T(8,128)(2,1)S(1)} collective-permute-done((bf16[136,512]{1,0:T(8,128)(2,1)S(1)}, bf16[136,512]{1,0:T(8,128)(2,1)S(1)}, u32[]{:S(2)}, u32[]{:S(2)}) %collective-permute-start.6) | collective-permute-done | bytes 139296 | tf_op jit(solution)/shard_map/ppermute | solution.py:279
  20.0 0.3 %share.1 = (f32[4,128]{1,0:T(4,128)S(1)}, f32[4,512]{1,0:T(4,128)S(1)}, bf16[16,512]{1,0:T(8,128)(2,1)S(1)}) custom-call(s32[16,128]{1,0:T(8,128)S(1)} %get-tuple-element.17.place_ref, bf16[16,512]{1,0:T(8,128)(2,1)S(1)} %maximum_maximum_fusion.both_ref.refs_0_, f32[16,128]{1,0:T(8,128)S(1)} %get-tuple-element.21.loss_ref, ...), custom_call_target="tpu_custom_call" | custom-call | tf_op jit(solution)/shard_map/share/pallas_call | solution.py:22
  20.4 0.4 %collective-permute-start.7 = (bf16[16,512]{1,0:T(8,128)(2,1)S(1)}, bf16[16,512]{1,0:T(8,128)(2,1)S(1)}, u32[]{:S(2)}, u32[]{:S(2)}) collective-permute-start(bf16[16,512]{1,0:T(8,128)(2,1)S(1)} %get-tuple-element.25.refs_1_), channel_id=1, source_target_pairs={{0,4},{4,0},{8,12},{12,8},{16,20},{20,16},{24,28},{28,24},{1,5},{5... | collective-permute-start | bytes 49160 | tf_op jit(solution)/shard_map/ppermute | solution.py:272
  20.7 0.8 %collective-permute-done.8.refs_2_ = bf16[16,512]{1,0:T(8,128)(2,1)S(1)} collective-permute-done((bf16[16,512]{1,0:T(8,128)(2,1)S(1)}, bf16[16,512]{1,0:T(8,128)(2,1)S(1)}, u32[]{:S(2)}, u32[]{:S(2)}) %collective-permute-start.8) | collective-permute-done | bytes 16416 | tf_op jit(solution)/shard_map/ppermute | solution.py:279
  21.5 1.0 %collective-permute-done.9.refs_3_ = bf16[16,512]{1,0:T(8,128)(2,1)S(1)} collective-permute-done((bf16[16,512]{1,0:T(8,128)(2,1)S(1)}, bf16[16,512]{1,0:T(8,128)(2,1)S(1)}, u32[]{:S(2)}, u32[]{:S(2)}) %collective-permute-start.9) | collective-permute-done | bytes 16416 | tf_op jit(solution)/shard_map/ppermute | solution.py:279
  22.5 0.0 collective-permute-done.7.back_ref
  22.5 0.0 copy-done
  22.5 0.9 %last.1 = (f32[1,4]{1,0:T(1,128)}, f32[4,512]{1,0:T(4,128)}, f32[16,512]{1,0:T(8,128)}) custom-call(s32[8,128]{1,0:T(8,128)S(1)} %get-tuple-element.16.at_ref, bf16[16,512]{1,0:T(8,128)(2,1)S(1)} %copy-done, f32[4,128]{1,0:T(4,128)S(1)} %get-tuple-element.23.loss_ref, f32[4,512]{1,0:T(4,128)S(1)} %get-tuple-element.24.grad_ref, ...), custom_call_target="tpu_custom_call" | custom-call | tf_op jit(solution)/shard_map/last/pallas_call | solution.py:22
  (3 shorter events, 0.0 us)
Async XLA Ops:
  0.6 21.9 %copy-start = (bf16[16,512]{1,0:T(8,128)(2,1)S(1)}, bf16[16,512]{1,0:T(8,128)(2,1)}, u32[]{:S(2)}) copy-start(bf16[16,512]{1,0:T(8,128)(2,1)} %docs_ref.1) | copy-start | bytes 49156
  0.6 6.6 %collective-permute-start = (bf16[16,512]{1,0:T(8,128)(2,1)}, bf16[16,512]{1,0:T(8,128)(2,1)S(1)}, u32[]{:S(2)}, u32[]{:S(2)}) collective-permute-start(bf16[16,512]{1,0:T(8,128)(2,1)} %docs_ref.1), channel_id=1, source_target_pairs={{0,20},{1,21},{2,22},{3,23},{4,16},{5,17},{6,18},{7,19},{8,28},{9,... | collective-permute-start | bytes 49160 | tf_op jit(solution)/shard_map/ppermute | solution.py:279
  7.2 4.9 %collective-permute-start.1 = (bf16[48,512]{1,0:T(8,128)(2,1)S(1)}, bf16[48,512]{1,0:T(8,128)(2,1)S(1)}, u32[]{:S(2)}, u32[]{:S(2)}) collective-permute-start(bf16[48,512]{1,0:T(8,128)(2,1)S(1)} %constant_dynamic-update-slice_fusion), channel_id=1, source_target_pairs={{0,7},{1,6},{2,5},{3,4},{4,3},{5,2},{6,1},{7,0},{8,15},{9,14},{10,... | collective-permute-start | bytes 147464 | tf_op jit(solution)/shard_map/ppermute | solution.py:279
  10.0 4.0 %collective-permute-start.2 = (bf16[48,512]{1,0:T(8,128)(2,1)S(1)}, bf16[48,512]{1,0:T(8,128)(2,1)S(1)}, u32[]{:S(2)}, u32[]{:S(2)}) collective-permute-start(bf16[48,512]{1,0:T(8,128)(2,1)S(1)} %constant_dynamic-update-slice_fusion), channel_id=1, source_target_pairs={{0,6},{1,7},{2,4},{3,5},{4,2},{5,3},{6,0},{7,1},{8,14},{9,15},{10,... | collective-permute-start | bytes 147464 | tf_op jit(solution)/shard_map/ppermute | solution.py:279
  10.0 4.0 %collective-permute-start.3 = (bf16[48,512]{1,0:T(8,128)(2,1)S(1)}, bf16[48,512]{1,0:T(8,128)(2,1)S(1)}, u32[]{:S(2)}, u32[]{:S(2)}) collective-permute-start(bf16[48,512]{1,0:T(8,128)(2,1)S(1)} %constant_dynamic-update-slice_fusion), channel_id=1, source_target_pairs={{0,5},{1,4},{2,7},{3,6},{4,1},{5,0},{6,3},{7,2},{8,13},{9,12},{10,... | collective-permute-start | bytes 147464 | tf_op jit(solution)/shard_map/ppermute | solution.py:279
  10.8 3.3 %collective-permute-start.4 = (bf16[48,512]{1,0:T(8,128)(2,1)S(1)}, bf16[48,512]{1,0:T(8,128)(2,1)S(1)}, u32[]{:S(2)}, u32[]{:S(2)}) collective-permute-start(bf16[48,512]{1,0:T(8,128)(2,1)S(1)} %constant_dynamic-update-slice_fusion), channel_id=1, source_target_pairs={{0,4},{4,0},{8,12},{12,8},{16,20},{20,16},{24,28},{28,24},{1,5},{5... | collective-permute-start | bytes 147464 | tf_op jit(solution)/shard_map/ppermute | solution.py:272
  14.3 1.8 %collective-permute-start.5 = (bf16[4,512]{1,0:T(4,128)(2,1)S(1)}, bf16[4,512]{1,0:T(4,128)(2,1)S(1)}, u32[]{:S(2)}, u32[]{:S(2)}) collective-permute-start(bf16[4,512]{1,0:T(4,128)(2,1)S(1)} %get-tuple-element.19), channel_id=1, source_target_pairs={{0,4},{4,0},{8,12},{12,8},{16,20},{20,16},{24,28},{28,24},{1,5},{5... | collective-permute-start | bytes 12296 | tf_op jit(solution)/shard_map/ppermute | solution.py:272
  14.5 5.5 %collective-permute-start.6 = (bf16[136,512]{1,0:T(8,128)(2,1)S(1)}, bf16[136,512]{1,0:T(8,128)(2,1)S(1)}, u32[]{:S(2)}, u32[]{:S(2)}) collective-permute-start(bf16[136,512]{1,0:T(8,128)(2,1)S(1)} %get-tuple-element.20.docs_ref), channel_id=1, source_target_pairs={{0,12},{1,13},{2,14},{3,15},{4,8},{5,9},{6,10},{7,11},{8,4},{9,5},... | collective-permute-start | bytes 417800 | tf_op jit(solution)/shard_map/ppermute | solution.py:279
  16.2 5.4 %collective-permute-start.8 = (bf16[16,512]{1,0:T(8,128)(2,1)S(1)}, bf16[16,512]{1,0:T(8,128)(2,1)S(1)}, u32[]{:S(2)}, u32[]{:S(2)}) collective-permute-start(bf16[16,512]{1,0:T(8,128)(2,1)S(1)} %maximum_maximum_fusion.both_ref.refs_0_), channel_id=1, source_target_pairs={{0,28},{1,29},{2,30},{3,31},{4,24},{5,25},{6,26},{7,27},{8,20},{9,... | collective-permute-start | bytes 49160 | tf_op jit(solution)/shard_map/ppermute | solution.py:279
  18.2 4.3 %collective-permute-start.9 = (bf16[16,512]{1,0:T(8,128)(2,1)S(1)}, bf16[16,512]{1,0:T(8,128)(2,1)S(1)}, u32[]{:S(2)}, u32[]{:S(2)}) collective-permute-start(bf16[16,512]{1,0:T(8,128)(2,1)S(1)} %maximum_maximum_fusion.both_ref.refs_0_), channel_id=1, source_target_pairs={{0,20},{1,21},{2,22},{3,23},{4,16},{5,17},{6,18},{7,19},{8,28},{9,... | collective-permute-start | bytes 49160 | tf_op jit(solution)/shard_map/ppermute | solution.py:279
  20.4 2.1 %collective-permute-start.7 = (bf16[16,512]{1,0:T(8,128)(2,1)S(1)}, bf16[16,512]{1,0:T(8,128)(2,1)S(1)}, u32[]{:S(2)}, u32[]{:S(2)}) collective-permute-start(bf16[16,512]{1,0:T(8,128)(2,1)S(1)} %get-tuple-element.25.refs_1_), channel_id=1, source_target_pairs={{0,4},{4,0},{8,12},{12,8},{16,20},{20,16},{24,28},{28,24},{1,5},{5... | collective-permute-start | bytes 49160 | tf_op jit(solution)/shard_map/ppermute | solution.py:272

commit v5 on v4

--- a/solution.py
+++ b/solution.py
@@ -45,6 +45,7 @@
     features_hbm,
     proj_hbm,
     docs_hbm,
+    docs_ref,
     out_ref,
     place_ref,
     at_ref,
@@ -65,7 +66,7 @@
         for n, (source, target) in enumerate(
             [(counts_hbm, counts_ref), (index_hbm, index_ref), (query_hbm, query_ref)]
             + [(features_hbm.at[r], features_ref.at[r]) for r in range(recs)]
-            + [(proj_hbm, proj_ref), (docs_hbm, out_ref.at[:docs_dev])]
+            + [(proj_hbm, proj_ref), (docs_hbm, docs_ref)]
         )
     ]
     for copy in copies:
@@ -80,13 +81,13 @@
         target = index_ref[(group ^ (1 - r // recs)) * recs + r % recs]
         of_group, rest = target // (tm * docs_dev), target % (tm * docs_dev)
         of_layer = of_group // 2
-        at = (rest // docs_dev) ^ (tm - 1 - column if by_column else 0)
+        at = (rest // docs_dev) ^ (column if by_column else 0)
         if by_layer:
             steps = of_layer ^ layer
             far = steps // 2
             at = (at * 2 + far) * docs_dev + rest % docs_dev
             chunk = steps % 2
-            mine = (chunk + far + of_group + core) % 2 == 1
+            mine = (chunk + of_group + core) % 2 == 1
         else:
             at = (of_layer * tm + at) * docs_dev + rest % docs_dev
             chunk = 0
@@ -151,18 +152,29 @@
     peaks = over_heads(jnp.where(lane, peak, 0.0))
     stats = [peaks, totals_high, totals - totals_high, jnp.zeros((recs, width - 384), f32)]
     copies[4 + recs].wait()
-    out_ref[docs_dev:, :] = jnp.concatenate(
+    out_ref[...] = jnp.concatenate(
         [pooled_high, pooled - pooled_high, jnp.concatenate(stats, 1), jnp.zeros((recs, width), f32)], 0
     ).astype(bf16)
 
 
-def meet_kernel(recs, heads, docs_dev, *refs):
-    parts, (send_ref, speech_ref) = refs[:-2], refs[-2:]
-    doc_rows = parts[0].shape[0] - 4 * recs
+def meet_kernel(recs, heads, doc_rows, apart, *refs):
+    parts, (send_ref, both_ref) = list(refs[:-2]), refs[-2:]
     width = parts[0].shape[1]
-    pools = [part[docs_dev : docs_dev + 4 * recs, :].astype(f32) for part in parts]
-    peaks = [pool[2 * recs : 3 * recs, :128] for pool in pools]
-    totals = [pool[2 * recs : 3 * recs, 128:256] + pool[2 * recs : 3 * recs, 256:384] for pool in pools]
+    last = [parts.pop(), parts.pop()][::-1] if apart else []
+    sums, peaks, totals = [], [], []
+    for part in parts:
+        pool = part[doc_rows:, :].astype(f32)
+        sums.append([pool[n : n + recs] + pool[n + recs : n + 2 * recs] for n in (0, 2 * recs)])
+        peaks.append(pool[4 * recs :, :128])
+        totals.append(pool[4 * recs :, 128:256] + pool[4 * recs :, 256:384])
+    if apart:
+        pools = [part[part.shape[0] - 4 * recs :, :].astype(f32) for part in last]
+        sums.append([pool[:recs] + pool[recs : 2 * recs] for pool in pools])
+        stats = jnp.concatenate([pool[2 * recs : 3 * recs] for pool in pools], 0)
+        peaks.append(stats[:, :128])
+        totals.append(stats[:, 128:256] + stats[:, 256:384])
+        parts.append(last[0])
+    sums = [jnp.concatenate(pair, 0) for pair in sums]
     top = peaks[0]
     for peak in peaks[1:]:
         top = jnp.maximum(top, peak)
@@ -178,18 +190,14 @@
     scales = jnp.dot(high, spread, preferred_element_type=f32) + jnp.dot(
         low, spread, preferred_element_type=f32
     )
-    pooled = jnp.zeros((recs, width), f32)
-    for n, pool in enumerate(pools):
-        pooled = pooled + (pool[:recs] + pool[recs : 2 * recs]) * scales[n * recs : (n + 1) * recs]
+    pooled = jnp.zeros((2 * recs, width), f32)
+    for n, part in enumerate(sums):
+        pooled = pooled + part * scales[2 * n * recs : 2 * (n + 1) * recs]
     speech = pooled * lax.rsqrt(jnp.sum(pooled * pooled, axis=1, keepdims=True) + norm_eps)
-    speech_ref[...] = speech.astype(bf16)
+    both_ref[...] = jnp.concatenate([speech, jnp.zeros((2 * recs, width), f32)], 0).astype(bf16)
     for n, part in enumerate(parts):
-        send_ref[n * doc_rows : n * doc_rows + docs_dev, :] = part[:docs_dev, :]
-        if doc_rows > docs_dev:
-            send_ref[n * doc_rows + docs_dev : (n + 1) * doc_rows, :] = part[docs_dev + 4 * recs :, :]
-    send_ref[len(parts) * doc_rows :, :] = jnp.concatenate(
-        [speech, jnp.zeros((recs, width), f32)], 0
-    ).astype(bf16)
+        send_ref[n * doc_rows : (n + 1) * doc_rows, :] = part[:doc_rows, :]
+    send_ref[len(parts) * doc_rows :, :] = speech.astype(bf16)
 
 
 def pair_terms(logits, positive):
@@ -219,12 +227,10 @@
     blocks, (loss_out, grad_out, send_ref) = refs[:-3], refs[-3:]
     recs = both_ref.shape[0] // 4
     loss, grad = loss_ref[...], grad_ref[...]
-    head = jnp.zeros((recs, grad.shape[1]), f32)
     for block in blocks:
         doc_rows = block.shape[0] - 2 * recs
         more = speech_terms(place_ref, 1, both_ref[...], block[:doc_rows, :])
         loss, grad = loss + more[0], grad + more[1]
-        head = block[doc_rows:, :].astype(f32)[:recs]
     loss_out[...] = loss[recs : 2 * recs]
     grad_out[...] = grad[recs : 2 * recs]
     loss, grad = loss[:recs], grad[:recs]
@@ -234,7 +240,7 @@
     terms = [loss_high, loss_low, loss - loss_high - loss_low]
     terms.append(jnp.zeros((recs, grad.shape[1] - 384), f32))
     send_ref[...] = jnp.concatenate(
-        [head, grad_high, grad - grad_high, jnp.concatenate(terms, 1)], 0
+        [grad_high, grad - grad_high, jnp.concatenate(terms, 1), jnp.zeros_like(grad)], 0
     ).astype(bf16)
 
 
@@ -242,8 +248,8 @@
     row_refs, (loss_out, speech_out, doc_out) = refs[:-3], refs[-3:]
     recs = speech_out.shape[0]
     back = back_ref[...].astype(f32)
-    speech_out[...] = grad_ref[...] + back[recs : 2 * recs] + back[2 * recs : 3 * recs]
-    terms = back[3 * recs :]
+    speech_out[...] = grad_ref[...] + back[:recs] + back[recs : 2 * recs]
+    terms = back[2 * recs : 3 * recs]
     loss = loss_ref[...] + (terms[:, :128] + terms[:, 128:256] + terms[:, 256:384])
     diagonal = lax.broadcasted_iota(jnp.int32, (recs, 128), 0)
     diagonal = diagonal == lax.broadcasted_iota(jnp.int32, (recs, 128), 1)
@@ -251,9 +257,10 @@
     if len(row_refs) == 1:
         rows = row_refs[0][...]
     else:
-        both, send, *beyond = [ref[...].astype(f32) for ref in row_refs]
-        beyond = [part[: 2 * recs] for part in beyond]
-        rows = jnp.concatenate([both, send[:recs], back[:recs], *beyond], 0).astype(bf16)
+        both, near, *beyond = row_refs
+        near = near[near.shape[0] - 2 * recs :, :].astype(f32)
+        beyond = [ref[...].astype(f32)[: 2 * recs] for ref in beyond]
+        rows = jnp.concatenate([both[...].astype(f32), near, *beyond], 0).astype(bf16)
     logits = lax.dot_general(docs_ref[...], rows, BY_ROWS, preferred_element_type=f32)
     positive = lax.broadcasted_iota(jnp.int32, logits.shape, 0) == at_ref[:1, : logits.shape[1]]
     _, grad_b = pair_terms(logits, positive)
@@ -286,7 +293,7 @@
     groups, columns = lax.axis_size("grp"), lax.axis_size("tm")
     layers = groups // 2
     direct = layers == 4
-    order = (3, 2) if direct else ()
+    order = (2, 3) if direct else ()
 
     def shape(rows, lanes, kind=f32):
         return jax.ShapeDtypeStruct((rows, lanes), kind)
@@ -295,16 +302,17 @@
     if direct:
         blocks = [(0, 1), (0, 0), None, None, (1, 0), (1, 1)]
         blocks += [(steps, flip) for steps in order for flip in (0, 1)]
-        far = crossing(doc_embed, 2, 0)
-    payload, place, at = pl.pallas_call(
+        far = lax.ppermute(doc_embed, "grp", swap_pairs(groups, 2, 2))
+    docs, pools, place, at = pl.pallas_call(
         lambda *refs: pool_kernel((docs_dev, is_direct(columns), direct), blocks, *refs),
         out_shape=(
-            shape(docs_dev + 4 * recs, width, bf16),
+            shape(docs_dev, width, bf16),
+            shape(4 * recs, width, bf16),
             shape(4 * recs, 128, jnp.int32),
             shape(8, 128, jnp.int32),
         ),
         in_specs=[pl.BlockSpec(memory_space=pltpu.HBM)] * 6,
-        out_specs=(VMEM, VMEM, VMEM),
+        out_specs=(VMEM,) * 4,
         scratch_shapes=[
             pltpu.SMEM(frame_counts.shape, jnp.int32),
             pltpu.SMEM(doc_index.shape, jnp.int32),
@@ -321,24 +329,25 @@
             for operand in (frame_counts, doc_index, pool_query, features, w_proj, doc_embed)
         ]
     )
-    if direct:
-        payload = jnp.concatenate([payload, far])
+    other = to_other_core(pools)
+    docs = [docs, *([far] if direct else [])]
+    payload = [pools[: 2 * recs], other[: 2 * recs], pools[2 * recs : 3 * recs], other[2 * recs : 3 * recs]]
+    payload = jnp.concatenate([*docs, *payload])
     parts = [to_other_core(payload)]
+    doc_rows = columns * (payload.shape[0] - 6 * recs)
     if is_direct(columns):
-        parts = [crossing(payload, 0, steps) for steps in range(columns - 1, 0, -1)] + parts
+        parts += [crossing(payload, 0, steps) for steps in range(1, columns - 1)]
+        parts.append(crossing(jnp.concatenate([*docs, pools]), 0, columns - 1))
+        parts.append(to_other_core(parts[-1][doc_rows // columns :]))
     else:
         parts = list(lax.all_gather(parts[0], "tm"))
-    doc_rows = columns * (payload.shape[0] - 4 * recs)
-    own, speech = in_vmem(
-        lambda *refs: meet_kernel(recs, heads, docs_dev, *refs),
-        (shape(doc_rows + 2 * recs, width, bf16), shape(recs, width, bf16)),
+    own, both = in_vmem(
+        lambda *refs: meet_kernel(recs, heads, doc_rows // columns, is_direct(columns), *refs),
+        (shape(doc_rows + 2 * recs, width, bf16), shape(4 * recs, width, bf16)),
         8,
         "meet",
     )(*parts)
 
-    other = to_other_core(speech)
-    chip = jnp.concatenate([speech, other])
-    both = jnp.concatenate([chip, jnp.zeros((2 * recs, width), bf16)])
     docs, near = own, []
     if direct:
         near = [crossing(own, 1, 0)]
@@ -361,9 +370,9 @@
     )(place, both, loss, grad, *near)
     back = to_other_core(send)
     if direct:
-        rows = (both, send, *beyond)
+        rows = (both, *near, *beyond)
     else:
-        rows = (lax.all_gather(speech, "grp", tiled=True),)
+        rows = (lax.all_gather(both[:recs], "grp", tiled=True),)
         at = doc_index.reshape(layers, 2, recs)[:, ::-1].reshape(1, -1)
         at = at - (lax.axis_index("grp") * columns + lax.axis_index("tm")) * docs_dev
     loss, speech_grad, doc_grad = in_vmem(

time: 23.5 us -> 23.3 us (level)
  waiting for transfers between devices: 6.42 us -> 5.38 us
  starting transfers between devices: 11.3 us -> 12.2 us
    ppermute x0 -> x1, starting transfers between devices: none -> 4.1 us  [body(): far = lax.ppermute(doc_embed, 'grp', swap_pairs(groups, 2, 2))]
    ppermute x7 -> x6, starting transfers between devices: 10.8 us -> 7.2 us  [crossing(): return lax.ppermute(value, ('grp', 'tm'), swap_pairs(count, 1, steps))]
    ppermute x7 -> x6, waiting for transfers between devices: 6.41 us -> 5.37 us  [crossing(): return lax.ppermute(value, ('grp', 'tm'), swap_pairs(count, 1, steps))]
    ppermute x3 -> x4, starting transfers between devices: 0.49 us -> 0.92 us  [to_other_core(): return lax.ppermute(value, 'grp', swap_pairs(lax.axis_size('grp'), 1, 1))]
  transfers between devices with their start and end apart: 10 -> 11, of which waited for: 5 -> 4; matrix products, arithmetic and copies ran while one was open for 1% -> 0% of each run, Pallas kernels for 16% -> 16%
where the time goes in v5:
time: 23.3 us; the launch traced here: 23.2 us
  starting transfers between devices  12.2 us (52%)
  waiting for transfers between devices  5.38 us (23%)
  Pallas kernels  4.8 us (21%)
  between operations  0.71 us (3%)
    ppermute x6, starting transfers between devices, crossing(): return lax.ppermute(value, ('grp', 'tm'), swap_pairs(count, 1, steps))  7.2 us
    ppermute x6, waiting for transfers between devices, crossing(): return lax.ppermute(value, ('grp', 'tm'), swap_pairs(count, 1, steps))  5.37 us
    ppermute x1, starting transfers between devices, body(): far = lax.ppermute(doc_embed, 'grp', swap_pairs(groups, 2, 2))  4.1 us
    pallas_call x1, Pallas kernels, body(): pl.pallas_call(lambda *refs: pool_kernel((docs_dev, is_direct(columns), d...  3 us
    pallas_call x4, Pallas kernels, call(): pl.pallas_call(kernel, out_shape=outs, in_specs=[VMEM] * len(operands), o...  1.8 us
    ppermute x4, starting transfers between devices, to_other_core(): return lax.ppermute(value, 'grp', swap_pairs(lax.axis_size('grp'), 1, 1))  0.92 us
  transfers between devices with their start and end apart: 11, of which 4 were waited for; matrix products, arithmetic and copies ran while one was open for 0% of the time, Pallas kernels for 16%

profile of v5, /device:TPU:0, one launch (start us, length us, event | category | flops | bytes accessed | tf_op | source)
XLA Modules:
  0.0 23.2 jit_solution(11522473845026480251)
XLA Ops:
  0.6 0.0 copy-start
  0.6 4.1 %collective-permute-start = (bf16[16,512]{1,0:T(8,128)(2,1)}, bf16[16,512]{1,0:T(8,128)(2,1)S(1)}, u32[]{:S(2)}, u32[]{:S(2)}) collective-permute-start(bf16[16,512]{1,0:T(8,128)(2,1)} %docs_ref.1), channel_id=1, source_target_pairs={{0,16},{4,20},{8,24},{12,28},{16,0},{20,4},{24,8},{28,12},{1,17},{... | collective-permute-start | bytes 49160 | tf_op jit(solution)/shard_map/ppermute | solution.py:305
  4.7 3.0 %pool.1 = (bf16[16,512]{1,0:T(8,128)(2,1)S(1)}, bf16[16,512]{1,0:T(8,128)(2,1)S(1)}, s32[16,128]{1,0:T(8,128)S(1)}, s32[8,128]{1,0:T(8,128)S(1)}) custom-call(s32[4]{0:T(128)} %refs_0_.1, s32[32]{0:T(128)} %refs_1_.1, bf16[8,1024]{1,0:T(8,128)(2,1)} %refs_2_.1, bf16[4,256,1024]{2,1,0:T(8,128)(2,1)} %refs_3_.1, bf16[1024,512]{1,0:T(8,128)(2,1)} %refs_4_.1, ...), custom_call_target="tpu_custom_call" | custom-call | tf_op jit(solution)/shard_map/pool/pallas_call | solution.py:306
  7.8 0.1 collective-permute-start.1
  7.8 0.0 collective-permute-done
  7.9 2.6 %collective-permute-start.5 = (bf16[48,512]{1,0:T(8,128)(2,1)S(1)}, bf16[48,512]{1,0:T(8,128)(2,1)S(1)}, u32[]{:S(2)}, u32[]{:S(2)}) collective-permute-start(bf16[48,512]{1,0:T(8,128)(2,1)S(1)} %pad_maximum_fusion), channel_id=1, source_target_pairs={{0,7},{1,6},{2,5},{3,4},{4,3},{5,2},{6,1},{7,0},{8,15},{9,14},{10,... | collective-permute-start | bytes 147464 | tf_op jit(solution)/shard_map/ppermute | solution.py:286
  10.5 0.0 collective-permute-done.1
  10.5 0.2 collective-permute-start.4
  10.7 1.1 %collective-permute-start.3 = (bf16[56,512]{1,0:T(8,128)(2,1)S(1)}, bf16[56,512]{1,0:T(8,128)(2,1)S(1)}, u32[]{:S(2)}, u32[]{:S(2)}) collective-permute-start(bf16[56,512]{1,0:T(8,128)(2,1)S(1)} %concatenate.6), channel_id=1, source_target_pairs={{0,5},{1,4},{2,7},{3,6},{4,1},{5,0},{6,3},{7,2},{8,13},{9,12},{10,... | collective-permute-start | bytes 172040 | tf_op jit(solution)/shard_map/ppermute | solution.py:286
  11.8 0.2 collective-permute-start.2
  12.0 0.3 %collective-permute-done.5.refs_3_ = bf16[48,512]{1,0:T(8,128)(2,1)S(1)} collective-permute-done((bf16[48,512]{1,0:T(8,128)(2,1)S(1)}, bf16[48,512]{1,0:T(8,128)(2,1)S(1)}, u32[]{:S(2)}, u32[]{:S(2)}) %collective-permute-start.5) | collective-permute-done | bytes 49184 | tf_op jit(solution)/shard_map/ppermute | solution.py:286
  12.3 0.5 %collective-permute-start.6 = (bf16[16,512]{1,0:T(8,128)(2,1)S(1)}, bf16[16,512]{1,0:T(8,128)(2,1)S(1)}, u32[]{:S(2)}, u32[]{:S(2)}) collective-permute-start(bf16[16,512]{1,0:T(8,128)(2,1)S(1)} %slice.22), channel_id=1, source_target_pairs={{0,4},{4,0},{8,12},{12,8},{16,20},{20,16},{24,28},{28,24},{1,5},{5... | collective-permute-start | bytes 49160 | tf_op jit(solution)/shard_map/ppermute | solution.py:279
  12.8 1.8 %collective-permute-done.4.refs_2_ = bf16[56,512]{1,0:T(8,128)(2,1)S(1)} collective-permute-done((bf16[56,512]{1,0:T(8,128)(2,1)S(1)}, bf16[56,512]{1,0:T(8,128)(2,1)S(1)}, u32[]{:S(2)}, u32[]{:S(2)}) %collective-permute-start.4) | collective-permute-done | bytes 57376 | tf_op jit(solution)/shard_map/ppermute | solution.py:286
  14.6 0.0 collective-permute-done.3.refs_1_
  14.6 0.0 collective-permute-done.2.refs_0_
  14.6 0.0 collective-permute-done.6.refs_4_
  14.6 0.3 %meet.1 = (bf16[136,512]{1,0:T(8,128)(2,1)S(1)}, bf16[16,512]{1,0:T(8,128)(2,1)S(1)}) custom-call(bf16[56,512]{1,0:T(8,128)(2,1)S(1)} %collective-permute-done.2.refs_0_, bf16[56,512]{1,0:T(8,128)(2,1)S(1)} %collective-permute-done.3.refs_1_, bf16[56,512]{1,0:T(8,128)(2,1)S(1)} %collective-permute-done.4.refs_2_, ...), custom_call_target="tpu_custom_call" | custom-call | tf_op jit(solution)/shard_map/meet/pallas_call | solution.py:22
  14.9 1.4 %collective-permute-start.7 = (bf16[136,512]{1,0:T(8,128)(2,1)S(1)}, bf16[136,512]{1,0:T(8,128)(2,1)S(1)}, u32[]{:S(2)}, u32[]{:S(2)}) collective-permute-start(bf16[136,512]{1,0:T(8,128)(2,1)S(1)} %get-tuple-element.22.docs_ref), channel_id=1, source_target_pairs={{0,12},{1,13},{2,14},{3,15},{4,8},{5,9},{6,10},{7,11},{8,4},{9,5},... | collective-permute-start | bytes 417800 | tf_op jit(solution)/shard_map/ppermute | solution.py:286
  16.3 1.7 %collective-permute-start.10 = (bf16[16,512]{1,0:T(8,128)(2,1)S(1)}, bf16[16,512]{1,0:T(8,128)(2,1)S(1)}, u32[]{:S(2)}, u32[]{:S(2)}) collective-permute-start(bf16[16,512]{1,0:T(8,128)(2,1)S(1)} %get-tuple-element.21.both_ref.refs_0_), channel_id=1, source_target_pairs={{0,28},{1,29},{2,30},{3,31},{4,24},{5,25},{6,26},{7,27},{8,20},{9,... | collective-permute-start | bytes 49160 | tf_op jit(solution)/shard_map/ppermute | solution.py:286
  18.0 0.2 collective-permute-start.9
  18.1 0.3 %first_docs.1 = (f32[16,128]{1,0:T(8,128)S(1)}, f32[16,512]{1,0:T(8,128)S(1)}) custom-call(s32[16,128]{1,0:T(8,128)S(1)} %get-tuple-element.18.place_ref, bf16[16,512]{1,0:T(8,128)(2,1)S(1)} %get-tuple-element.21.both_ref.refs_0_, bf16[136,512]{1,0:T(8,128)(2,1)S(1)} %get-tuple-element.22.docs_ref), custom_call_target="tpu_custom_call" | custom-call | tf_op jit(solution)/shard_map/first_docs/pallas_call | solution.py:22
  18.5 2.1 %collective-permute-done.7.refs_0_.refs_1_ = bf16[136,512]{1,0:T(8,128)(2,1)S(1)} collective-permute-done((bf16[136,512]{1,0:T(8,128)(2,1)S(1)}, bf16[136,512]{1,0:T(8,128)(2,1)S(1)}, u32[]{:S(2)}, u32[]{:S(2)}) %collective-permute-start.7) | collective-permute-done | bytes 139296 | tf_op jit(solution)/shard_map/ppermute | solution.py:286
  20.5 0.3 %share.1 = (f32[4,128]{1,0:T(4,128)S(1)}, f32[4,512]{1,0:T(4,128)S(1)}, bf16[16,512]{1,0:T(8,128)(2,1)S(1)}) custom-call(s32[16,128]{1,0:T(8,128)S(1)} %get-tuple-element.18.place_ref, bf16[16,512]{1,0:T(8,128)(2,1)S(1)} %get-tuple-element.21.both_ref.refs_0_, f32[16,128]{1,0:T(8,128)S(1)} %get-tuple-element.23.loss_ref, ...), custom_call_target="tpu_custom_call" | custom-call | tf_op jit(solution)/shard_map/share/pallas_call | solution.py:22
  20.9 0.2 collective-permute-start.8
  21.1 1.2 %collective-permute-done.10.refs_3_ = bf16[16,512]{1,0:T(8,128)(2,1)S(1)} collective-permute-done((bf16[16,512]{1,0:T(8,128)(2,1)S(1)}, bf16[16,512]{1,0:T(8,128)(2,1)S(1)}, u32[]{:S(2)}, u32[]{:S(2)}) %collective-permute-start.10) | collective-permute-done | bytes 16416 | tf_op jit(solution)/shard_map/ppermute | solution.py:286
  22.2 0.0 collective-permute-done.9.refs_2_
  22.3 0.0 collective-permute-done.8.back_ref
  22.3 0.0 copy-done
  22.3 0.9 %last.1 = (f32[1,4]{1,0:T(1,128)}, f32[4,512]{1,0:T(4,128)}, f32[16,512]{1,0:T(8,128)}) custom-call(s32[8,128]{1,0:T(8,128)S(1)} %get-tuple-element.17.at_ref, bf16[16,512]{1,0:T(8,128)(2,1)S(1)} %copy-done, f32[4,128]{1,0:T(4,128)S(1)} %get-tuple-element.25.loss_ref, f32[4,512]{1,0:T(4,128)S(1)} %get-tuple-element.26.grad_ref, ...), custom_call_target="tpu_custom_call" | custom-call | tf_op jit(solution)/shard_map/last/pallas_call | solution.py:22
  (7 shorter events, 0.1 us)
Async XLA Ops:
  0.6 21.6 %copy-start = (bf16[16,512]{1,0:T(8,128)(2,1)S(1)}, bf16[16,512]{1,0:T(8,128)(2,1)}, u32[]{:S(2)}) copy-start(bf16[16,512]{1,0:T(8,128)(2,1)} %docs_ref.1) | copy-start | bytes 49156
  0.6 7.2 %collective-permute-start = (bf16[16,512]{1,0:T(8,128)(2,1)}, bf16[16,512]{1,0:T(8,128)(2,1)S(1)}, u32[]{:S(2)}, u32[]{:S(2)}) collective-permute-start(bf16[16,512]{1,0:T(8,128)(2,1)} %docs_ref.1), channel_id=1, source_target_pairs={{0,16},{4,20},{8,24},{12,28},{16,0},{20,4},{24,8},{28,12},{1,17},{... | collective-permute-start | bytes 49160 | tf_op jit(solution)/shard_map/ppermute | solution.py:305
  7.8 2.7 %collective-permute-start.1 = (bf16[16,512]{1,0:T(8,128)(2,1)S(1)}, bf16[16,512]{1,0:T(8,128)(2,1)S(1)}, u32[]{:S(2)}, u32[]{:S(2)}) collective-permute-start(bf16[16,512]{1,0:T(8,128)(2,1)S(1)} %get-tuple-element.20), channel_id=1, source_target_pairs={{0,4},{4,0},{8,12},{12,8},{16,20},{20,16},{24,28},{28,24},{1,5},{5... | collective-permute-start | bytes 49160 | tf_op jit(solution)/shard_map/ppermute | solution.py:279
  7.9 4.5 %collective-permute-start.5 = (bf16[48,512]{1,0:T(8,128)(2,1)S(1)}, bf16[48,512]{1,0:T(8,128)(2,1)S(1)}, u32[]{:S(2)}, u32[]{:S(2)}) collective-permute-start(bf16[48,512]{1,0:T(8,128)(2,1)S(1)} %pad_maximum_fusion), channel_id=1, source_target_pairs={{0,7},{1,6},{2,5},{3,4},{4,3},{5,2},{6,1},{7,0},{8,15},{9,14},{10,... | collective-permute-start | bytes 147464 | tf_op jit(solution)/shard_map/ppermute | solution.py:286
  10.5 4.1 %collective-permute-start.4 = (bf16[56,512]{1,0:T(8,128)(2,1)S(1)}, bf16[56,512]{1,0:T(8,128)(2,1)S(1)}, u32[]{:S(2)}, u32[]{:S(2)}) collective-permute-start(bf16[56,512]{1,0:T(8,128)(2,1)S(1)} %concatenate.6), channel_id=1, source_target_pairs={{0,6},{1,7},{2,4},{3,5},{4,2},{5,3},{6,0},{7,1},{8,14},{9,15},{10,... | collective-permute-start | bytes 172040 | tf_op jit(solution)/shard_map/ppermute | solution.py:286
  10.7 3.8 %collective-permute-start.3 = (bf16[56,512]{1,0:T(8,128)(2,1)S(1)}, bf16[56,512]{1,0:T(8,128)(2,1)S(1)}, u32[]{:S(2)}, u32[]{:S(2)}) collective-permute-start(bf16[56,512]{1,0:T(8,128)(2,1)S(1)} %concatenate.6), channel_id=1, source_target_pairs={{0,5},{1,4},{2,7},{3,6},{4,1},{5,0},{6,3},{7,2},{8,13},{9,12},{10,... | collective-permute-start | bytes 172040 | tf_op jit(solution)/shard_map/ppermute | solution.py:286
  11.8 2.8 %collective-permute-start.2 = (bf16[56,512]{1,0:T(8,128)(2,1)S(1)}, bf16[56,512]{1,0:T(8,128)(2,1)S(1)}, u32[]{:S(2)}, u32[]{:S(2)}) collective-permute-start(bf16[56,512]{1,0:T(8,128)(2,1)S(1)} %concatenate.6), channel_id=1, source_target_pairs={{0,4},{4,0},{8,12},{12,8},{16,20},{20,16},{24,28},{28,24},{1,5},{5... | collective-permute-start | bytes 172040 | tf_op jit(solution)/shard_map/ppermute | solution.py:279
  12.3 2.3 %collective-permute-start.6 = (bf16[16,512]{1,0:T(8,128)(2,1)S(1)}, bf16[16,512]{1,0:T(8,128)(2,1)S(1)}, u32[]{:S(2)}, u32[]{:S(2)}) collective-permute-start(bf16[16,512]{1,0:T(8,128)(2,1)S(1)} %slice.22), channel_id=1, source_target_pairs={{0,4},{4,0},{8,12},{12,8},{16,20},{20,16},{24,28},{28,24},{1,5},{5... | collective-permute-start | bytes 49160 | tf_op jit(solution)/shard_map/ppermute | solution.py:279
  14.9 5.7 %collective-permute-start.7 = (bf16[136,512]{1,0:T(8,128)(2,1)S(1)}, bf16[136,512]{1,0:T(8,128)(2,1)S(1)}, u32[]{:S(2)}, u32[]{:S(2)}) collective-permute-start(bf16[136,512]{1,0:T(8,128)(2,1)S(1)} %get-tuple-element.22.docs_ref), channel_id=1, source_target_pairs={{0,12},{1,13},{2,14},{3,15},{4,8},{5,9},{6,10},{7,11},{8,4},{9,5},... | collective-permute-start | bytes 417800 | tf_op jit(solution)/shard_map/ppermute | solution.py:286
  16.3 6.0 %collective-permute-start.10 = (bf16[16,512]{1,0:T(8,128)(2,1)S(1)}, bf16[16,512]{1,0:T(8,128)(2,1)S(1)}, u32[]{:S(2)}, u32[]{:S(2)}) collective-permute-start(bf16[16,512]{1,0:T(8,128)(2,1)S(1)} %get-tuple-element.21.both_ref.refs_0_), channel_id=1, source_target_pairs={{0,28},{1,29},{2,30},{3,31},{4,24},{5,25},{6,26},{7,27},{8,20},{9,... | collective-permute-start | bytes 49160 | tf_op jit(solution)/shard_map/ppermute | solution.py:286
  18.0 4.3 %collective-permute-start.9 = (bf16[16,512]{1,0:T(8,128)(2,1)S(1)}, bf16[16,512]{1,0:T(8,128)(2,1)S(1)}, u32[]{:S(2)}, u32[]{:S(2)}) collective-permute-start(bf16[16,512]{1,0:T(8,128)(2,1)S(1)} %get-tuple-element.21.both_ref.refs_0_), channel_id=1, source_target_pairs={{0,20},{1,21},{2,22},{3,23},{4,16},{5,17},{6,18},{7,19},{8,28},{9,... | collective-permute-start | bytes 49160 | tf_op jit(solution)/shard_map/ppermute | solution.py:286
  20.9 1.4 %collective-permute-start.8 = (bf16[16,512]{1,0:T(8,128)(2,1)S(1)}, bf16[16,512]{1,0:T(8,128)(2,1)S(1)}, u32[]{:S(2)}, u32[]{:S(2)}) collective-permute-start(bf16[16,512]{1,0:T(8,128)(2,1)S(1)} %get-tuple-element.27), channel_id=1, source_target_pairs={{0,4},{4,0},{8,12},{12,8},{16,20},{20,16},{24,28},{28,24},{1,5},{5... | collective-permute-start | bytes 49160 | tf_op jit(solution)/shard_map/ppermute | solution.py:279

commit v6 on v5

--- a/solution.py
+++ b/solution.py
@@ -78,7 +78,7 @@
     spot = lax.broadcasted_iota(jnp.int32, place_ref.shape, 1)
     place = jnp.full(place_ref.shape, -1, jnp.int32)
     for r in range(2 * recs):
-        target = index_ref[(group ^ (1 - r // recs)) * recs + r % recs]
+        target = index_ref[(group ^ (r // recs)) * recs + r % recs]
         of_group, rest = target // (tm * docs_dev), target % (tm * docs_dev)
         of_layer = of_group // 2
         at = (rest // docs_dev) ^ (column if by_column else 0)
@@ -87,11 +87,11 @@
             far = steps // 2
             at = (at * 2 + far) * docs_dev + rest % docs_dev
             chunk = steps % 2
-            mine = (chunk + of_group + core) % 2 == 1
+            mine = (of_group + core) % 2 == 0
         else:
             at = (of_layer * tm + at) * docs_dev + rest % docs_dev
             chunk = 0
-            mine = (of_group + core) % 2 == 1
+            mine = (of_group + core) % 2 == 0
         chunk = jnp.where(mine, chunk, -1)
         place = jnp.where((row == r) & (spot == chunk), at, place)
     place_ref[...] = place
@@ -231,9 +231,9 @@
         doc_rows = block.shape[0] - 2 * recs
         more = speech_terms(place_ref, 1, both_ref[...], block[:doc_rows, :])
         loss, grad = loss + more[0], grad + more[1]
-    loss_out[...] = loss[recs : 2 * recs]
-    grad_out[...] = grad[recs : 2 * recs]
-    loss, grad = loss[:recs], grad[:recs]
+    loss_out[...] = loss[:recs]
+    grad_out[...] = grad[:recs]
+    loss, grad = loss[recs : 2 * recs], grad[recs : 2 * recs]
     grad_high = grad.astype(bf16).astype(f32)
     loss_high = loss.astype(bf16).astype(f32)
     loss_low = (loss - loss_high).astype(bf16).astype(f32)
@@ -279,11 +279,10 @@
     return lax.ppermute(value, "grp", swap_pairs(lax.axis_size("grp"), 1, 1))
 
 
-def crossing(value, layer_steps, column_steps):
+def across(value, layer_steps, column_steps, core_steps=0):
     columns = lax.axis_size("tm")
-    count = lax.axis_size("grp") * columns
-    steps = (2 * layer_steps + 1) * columns + column_steps
-    return lax.ppermute(value, ("grp", "tm"), swap_pairs(count, 1, steps))
+    steps = (2 * layer_steps + core_steps) * columns + column_steps
+    return lax.ppermute(value, ("grp", "tm"), swap_pairs(lax.axis_size("grp") * columns, 1, steps))
 
 
 def body(features, frame_counts, pool_query, w_proj, doc_embed, doc_index):
@@ -300,9 +299,9 @@
 
     blocks = []
     if direct:
-        blocks = [(0, 1), (0, 0), None, None, (1, 0), (1, 1)]
-        blocks += [(steps, flip) for steps in order for flip in (0, 1)]
-        far = lax.ppermute(doc_embed, "grp", swap_pairs(groups, 2, 2))
+        blocks = [(0, 0), (0, 1), None, None, (1, 0), (1, 1)]
+        blocks += [(steps, flip) for steps in order for flip in (1, 0)]
+        far = across(doc_embed, 2, 0)
     docs, pools, place, at = pl.pallas_call(
         lambda *refs: pool_kernel((docs_dev, is_direct(columns), direct), blocks, *refs),
         out_shape=(
@@ -333,14 +332,14 @@
     docs = [docs, *([far] if direct else [])]
     payload = [pools[: 2 * recs], other[: 2 * recs], pools[2 * recs : 3 * recs], other[2 * recs : 3 * recs]]
     payload = jnp.concatenate([*docs, *payload])
-    parts = [to_other_core(payload)]
+    parts = [payload]
     doc_rows = columns * (payload.shape[0] - 6 * recs)
     if is_direct(columns):
-        parts += [crossing(payload, 0, steps) for steps in range(1, columns - 1)]
-        parts.append(crossing(jnp.concatenate([*docs, pools]), 0, columns - 1))
+        parts += [across(payload, 0, steps) for steps in range(1, columns - 1)]
+        parts.append(across(jnp.concatenate([*docs, pools]), 0, columns - 1))
         parts.append(to_other_core(parts[-1][doc_rows // columns :]))
     else:
-        parts = list(lax.all_gather(parts[0], "tm"))
+        parts = list(lax.all_gather(payload, "tm"))
     own, both = in_vmem(
         lambda *refs: meet_kernel(recs, heads, doc_rows // columns, is_direct(columns), *refs),
         (shape(doc_rows + 2 * recs, width, bf16), shape(4 * recs, width, bf16)),
@@ -350,8 +349,8 @@
 
     docs, near = own, []
     if direct:
-        near = [crossing(own, 1, 0)]
-        beyond = [crossing(both, steps, 0) for steps in order]
+        near = [across(own, 1, 0)]
+        beyond = [across(both, steps, 0, 1) for steps in order]
     else:
         same_core = [[2 * n + core for n in range(layers)] for core in range(2)]
         docs = lax.all_gather(own[:doc_rows], "grp", axis_index_groups=same_core, tiled=True)
@@ -373,8 +372,7 @@
         rows = (both, *near, *beyond)
     else:
         rows = (lax.all_gather(both[:recs], "grp", tiled=True),)
-        at = doc_index.reshape(layers, 2, recs)[:, ::-1].reshape(1, -1)
-        at = at - (lax.axis_index("grp") * columns + lax.axis_index("tm")) * docs_dev
+        at = doc_index[None, :] - (lax.axis_index("grp") * columns + lax.axis_index("tm")) * docs_dev
     loss, speech_grad, doc_grad = in_vmem(
         last_kernel,
         (shape(1, recs), shape(recs, width), shape(docs_dev, width)),

time: 23.3 us -> 23.4 us (level); the launches traced: 23.2 us -> 23 us
  starting transfers between devices: 12.2 us -> 11.6 us
  waiting for transfers between devices: 5.38 us -> 5.77 us
    ppermute x4 -> x3, starting transfers between devices: 0.92 us -> 0.14 us  [to_other_core(): return lax.ppermute(value, 'grp', swap_pairs(lax.axis_size('grp'), 1, 1))]
    ppermute x7, waiting for transfers between devices: 5.37 us -> 5.67 us  [across(): lax.ppermute(value, ('grp', 'tm'), swap_pairs(lax.axis_size('grp') * colu...]
  transfers between devices with their start and end apart: 11 -> 10, of which waited for: 4 -> 6; matrix products, arithmetic and copies ran while one was open for 0% -> 0% of each run, Pallas kernels for 16% -> 16%
where the time goes in v6:
time: 23.4 us; the launch traced here: 23 us
  starting transfers between devices  11.6 us (50%)
  waiting for transfers between devices  5.77 us (25%)
  Pallas kernels  4.8 us (21%)
  between operations  0.72 us (3%)
    ppermute x7, starting transfers between devices, across(): lax.ppermute(value, ('grp', 'tm'), swap_pairs(lax.axis_size('grp') * colu...  11.5 us
    ppermute x7, waiting for transfers between devices, across(): lax.ppermute(value, ('grp', 'tm'), swap_pairs(lax.axis_size('grp') * colu...  5.67 us
    pallas_call x1, Pallas kernels, body(): pl.pallas_call(lambda *refs: pool_kernel((docs_dev, is_direct(columns), d...  3 us
    pallas_call x4, Pallas kernels, call(): pl.pallas_call(kernel, out_shape=outs, in_specs=[VMEM] * len(operands), o...  1.8 us
  transfers between devices with their start and end apart: 10, of which 6 were waited for; matrix products, arithmetic and copies ran while one was open for 0% of the time, Pallas kernels for 16%

profile of v6, /device:TPU:0, one launch (start us, length us, event | category | flops | bytes accessed | tf_op | source)
XLA Modules:
  0.0 23.0 jit_solution(15568712520466429978)
XLA Ops:
  0.6 0.0 copy-start
  0.6 4.1 %collective-permute-start = (bf16[16,512]{1,0:T(8,128)(2,1)}, bf16[16,512]{1,0:T(8,128)(2,1)S(1)}, u32[]{:S(2)}, u32[]{:S(2)}) collective-permute-start(bf16[16,512]{1,0:T(8,128)(2,1)} %docs_ref.1), channel_id=1, source_target_pairs={{0,16},{1,17},{2,18},{3,19},{4,20},{5,21},{6,22},{7,23},{8,24},{9,... | collective-permute-start | bytes 49160 | tf_op jit(solution)/shard_map/ppermute | solution.py:285
  4.7 3.0 %pool.1 = (bf16[16,512]{1,0:T(8,128)(2,1)S(1)}, bf16[16,512]{1,0:T(8,128)(2,1)S(1)}, s32[16,128]{1,0:T(8,128)S(1)}, s32[8,128]{1,0:T(8,128)S(1)}) custom-call(s32[4]{0:T(128)} %refs_0_.1, s32[32]{0:T(128)} %refs_1_.1, bf16[8,1024]{1,0:T(8,128)(2,1)} %refs_2_.1, bf16[4,256,1024]{2,1,0:T(8,128)(2,1)} %refs_3_.1, bf16[1024,512]{1,0:T(8,128)(2,1)} %refs_4_.1, ...), custom_call_target="tpu_custom_call" | custom-call | tf_op jit(solution)/shard_map/pool/pallas_call | solution.py:305
  7.8 0.1 collective-permute-start.1
  7.8 0.0 collective-permute-done
  7.9 2.5 %collective-permute-start.4 = (bf16[48,512]{1,0:T(8,128)(2,1)S(1)}, bf16[48,512]{1,0:T(8,128)(2,1)S(1)}, u32[]{:S(2)}, u32[]{:S(2)}) collective-permute-start(bf16[48,512]{1,0:T(8,128)(2,1)S(1)} %pad_maximum_fusion), channel_id=1, source_target_pairs={{0,3},{1,2},{2,1},{3,0},{4,7},{5,6},{6,5},{7,4},{8,11},{9,10},{10,... | collective-permute-start | bytes 147464 | tf_op jit(solution)/shard_map/ppermute | solution.py:285
  10.4 0.0 collective-permute-done.1
  10.4 0.6 %collective-permute-start.3 = (bf16[56,512]{1,0:T(8,128)(2,1)S(1)}, bf16[56,512]{1,0:T(8,128)(2,1)S(1)}, u32[]{:S(2)}, u32[]{:S(2)}) collective-permute-start(bf16[56,512]{1,0:T(8,128)(2,1)S(1)} %concatenate.6.refs_0_), channel_id=1, source_target_pairs={{0,2},{1,3},{2,0},{3,1},{4,6},{5,7},{6,4},{7,5},{8,10},{9,11},{10,... | collective-permute-start | bytes 172040 | tf_op jit(solution)/shard_map/ppermute | solution.py:285
  11.0 1.1 %collective-permute-start.2 = (bf16[56,512]{1,0:T(8,128)(2,1)S(1)}, bf16[56,512]{1,0:T(8,128)(2,1)S(1)}, u32[]{:S(2)}, u32[]{:S(2)}) collective-permute-start(bf16[56,512]{1,0:T(8,128)(2,1)S(1)} %concatenate.6.refs_0_), channel_id=1, source_target_pairs={{0,1},{1,0},{2,3},{3,2},{4,5},{5,4},{6,7},{7,6},{8,9},{9,8},{10,11... | collective-permute-start | bytes 172040 | tf_op jit(solution)/shard_map/ppermute | solution.py:285
  12.1 0.8 %collective-permute-done.4.refs_3_ = bf16[48,512]{1,0:T(8,128)(2,1)S(1)} collective-permute-done((bf16[48,512]{1,0:T(8,128)(2,1)S(1)}, bf16[48,512]{1,0:T(8,128)(2,1)S(1)}, u32[]{:S(2)}, u32[]{:S(2)}) %collective-permute-start.4) | collective-permute-done | bytes 49184 | tf_op jit(solution)/shard_map/ppermute | solution.py:285
  12.9 0.0 collective-permute-start.5
  12.9 1.7 %collective-permute-done.3.refs_2_ = bf16[56,512]{1,0:T(8,128)(2,1)S(1)} collective-permute-done((bf16[56,512]{1,0:T(8,128)(2,1)S(1)}, bf16[56,512]{1,0:T(8,128)(2,1)S(1)}, u32[]{:S(2)}, u32[]{:S(2)}) %collective-permute-start.3) | collective-permute-done | bytes 57376 | tf_op jit(solution)/shard_map/ppermute | solution.py:285
  14.7 0.5 %collective-permute-done.2.refs_1_ = bf16[56,512]{1,0:T(8,128)(2,1)S(1)} collective-permute-done((bf16[56,512]{1,0:T(8,128)(2,1)S(1)}, bf16[56,512]{1,0:T(8,128)(2,1)S(1)}, u32[]{:S(2)}, u32[]{:S(2)}) %collective-permute-start.2) | collective-permute-done | bytes 57376 | tf_op jit(solution)/shard_map/ppermute | solution.py:285
  15.2 0.0 collective-permute-done.5.refs_4_
  15.2 0.3 %meet.1 = (bf16[136,512]{1,0:T(8,128)(2,1)S(1)}, bf16[16,512]{1,0:T(8,128)(2,1)S(1)}) custom-call(bf16[56,512]{1,0:T(8,128)(2,1)S(1)} %concatenate.6.refs_0_, bf16[56,512]{1,0:T(8,128)(2,1)S(1)} %collective-permute-done.2.refs_1_, bf16[56,512]{1,0:T(8,128)(2,1)S(1)} %collective-permute-done.3.refs_2_, bf16[48,512]{1,0:T(8,128)(2,1)S(1)} %collective-permute-done.4.refs_3_, ...), custom_call_target="tpu_custom_call" | custom-call | tf_op jit(solution)/shard_map/meet/pallas_call | solution.py:22
  15.4 1.6 %collective-permute-start.6 = (bf16[136,512]{1,0:T(8,128)(2,1)S(1)}, bf16[136,512]{1,0:T(8,128)(2,1)S(1)}, u32[]{:S(2)}, u32[]{:S(2)}) collective-permute-start(bf16[136,512]{1,0:T(8,128)(2,1)S(1)} %get-tuple-element.22.docs_ref), channel_id=1, source_target_pairs={{0,8},{1,9},{2,10},{3,11},{4,12},{5,13},{6,14},{7,15},{8,0},{9,1},... | collective-permute-start | bytes 417800 | tf_op jit(solution)/shard_map/ppermute | solution.py:285
  17.0 0.1 collective-permute-start.9
  17.1 1.5 %collective-permute-start.8 = (bf16[16,512]{1,0:T(8,128)(2,1)S(1)}, bf16[16,512]{1,0:T(8,128)(2,1)S(1)}, u32[]{:S(2)}, u32[]{:S(2)}) collective-permute-start(bf16[16,512]{1,0:T(8,128)(2,1)S(1)} %get-tuple-element.21.both_ref.refs_0_), channel_id=1, source_target_pairs={{0,20},{1,21},{2,22},{3,23},{4,16},{5,17},{6,18},{7,19},{8,28},{9,... | collective-permute-start | bytes 49160 | tf_op jit(solution)/shard_map/ppermute | solution.py:285
  18.7 0.3 %first_docs.1 = (f32[16,128]{1,0:T(8,128)S(1)}, f32[16,512]{1,0:T(8,128)S(1)}) custom-call(s32[16,128]{1,0:T(8,128)S(1)} %get-tuple-element.18.place_ref, bf16[16,512]{1,0:T(8,128)(2,1)S(1)} %get-tuple-element.21.both_ref.refs_0_, bf16[136,512]{1,0:T(8,128)(2,1)S(1)} %get-tuple-element.22.docs_ref), custom_call_target="tpu_custom_call" | custom-call | tf_op jit(solution)/shard_map/first_docs/pallas_call | solution.py:22
  19.0 1.5 %collective-permute-done.6.refs_0_.refs_1_ = bf16[136,512]{1,0:T(8,128)(2,1)S(1)} collective-permute-done((bf16[136,512]{1,0:T(8,128)(2,1)S(1)}, bf16[136,512]{1,0:T(8,128)(2,1)S(1)}, u32[]{:S(2)}, u32[]{:S(2)}) %collective-permute-start.6) | collective-permute-done | bytes 139296 | tf_op jit(solution)/shard_map/ppermute | solution.py:285
  20.5 0.3 %share.1 = (f32[4,128]{1,0:T(4,128)S(1)}, f32[4,512]{1,0:T(4,128)S(1)}, bf16[16,512]{1,0:T(8,128)(2,1)S(1)}) custom-call(s32[16,128]{1,0:T(8,128)S(1)} %get-tuple-element.18.place_ref, bf16[16,512]{1,0:T(8,128)(2,1)S(1)} %get-tuple-element.21.both_ref.refs_0_, f32[16,128]{1,0:T(8,128)S(1)} %get-tuple-element.23.loss_ref, ...), custom_call_target="tpu_custom_call" | custom-call | tf_op jit(solution)/shard_map/share/pallas_call | solution.py:22
  20.8 0.1 collective-permute-start.7
  20.9 1.1 %collective-permute-done.9.refs_3_ = bf16[16,512]{1,0:T(8,128)(2,1)S(1)} collective-permute-done((bf16[16,512]{1,0:T(8,128)(2,1)S(1)}, bf16[16,512]{1,0:T(8,128)(2,1)S(1)}, u32[]{:S(2)}, u32[]{:S(2)}) %collective-permute-start.9) | collective-permute-done | bytes 16416 | tf_op jit(solution)/shard_map/ppermute | solution.py:285
  22.0 0.0 collective-permute-done.8.refs_2_
  22.0 0.1 collective-permute-done.7.back_ref
  22.1 0.0 copy-done
  22.1 0.9 %last.1 = (f32[1,4]{1,0:T(1,128)}, f32[4,512]{1,0:T(4,128)}, f32[16,512]{1,0:T(8,128)}) custom-call(s32[8,128]{1,0:T(8,128)S(1)} %get-tuple-element.17.at_ref, bf16[16,512]{1,0:T(8,128)(2,1)S(1)} %copy-done, f32[4,128]{1,0:T(4,128)S(1)} %get-tuple-element.25.loss_ref, f32[4,512]{1,0:T(4,128)S(1)} %get-tuple-element.26.grad_ref, ...), custom_call_target="tpu_custom_call" | custom-call | tf_op jit(solution)/shard_map/last/pallas_call | solution.py:22
  (7 shorter events, 0.1 us)
Async XLA Ops:
  0.6 21.5 %copy-start = (bf16[16,512]{1,0:T(8,128)(2,1)S(1)}, bf16[16,512]{1,0:T(8,128)(2,1)}, u32[]{:S(2)}) copy-start(bf16[16,512]{1,0:T(8,128)(2,1)} %docs_ref.1) | copy-start | bytes 49156
  0.6 7.2 %collective-permute-start = (bf16[16,512]{1,0:T(8,128)(2,1)}, bf16[16,512]{1,0:T(8,128)(2,1)S(1)}, u32[]{:S(2)}, u32[]{:S(2)}) collective-permute-start(bf16[16,512]{1,0:T(8,128)(2,1)} %docs_ref.1), channel_id=1, source_target_pairs={{0,16},{1,17},{2,18},{3,19},{4,20},{5,21},{6,22},{7,23},{8,24},{9,... | collective-permute-start | bytes 49160 | tf_op jit(solution)/shard_map/ppermute | solution.py:285
  7.8 2.6 %collective-permute-start.1 = (bf16[16,512]{1,0:T(8,128)(2,1)S(1)}, bf16[16,512]{1,0:T(8,128)(2,1)S(1)}, u32[]{:S(2)}, u32[]{:S(2)}) collective-permute-start(bf16[16,512]{1,0:T(8,128)(2,1)S(1)} %get-tuple-element.20), channel_id=1, source_target_pairs={{0,4},{4,0},{8,12},{12,8},{16,20},{20,16},{24,28},{28,24},{1,5},{5... | collective-permute-start | bytes 49160 | tf_op jit(solution)/shard_map/ppermute | solution.py:279
  7.9 5.1 %collective-permute-start.4 = (bf16[48,512]{1,0:T(8,128)(2,1)S(1)}, bf16[48,512]{1,0:T(8,128)(2,1)S(1)}, u32[]{:S(2)}, u32[]{:S(2)}) collective-permute-start(bf16[48,512]{1,0:T(8,128)(2,1)S(1)} %pad_maximum_fusion), channel_id=1, source_target_pairs={{0,3},{1,2},{2,1},{3,0},{4,7},{5,6},{6,5},{7,4},{8,11},{9,10},{10,... | collective-permute-start | bytes 147464 | tf_op jit(solution)/shard_map/ppermute | solution.py:285
  10.4 4.2 %collective-permute-start.3 = (bf16[56,512]{1,0:T(8,128)(2,1)S(1)}, bf16[56,512]{1,0:T(8,128)(2,1)S(1)}, u32[]{:S(2)}, u32[]{:S(2)}) collective-permute-start(bf16[56,512]{1,0:T(8,128)(2,1)S(1)} %concatenate.6.refs_0_), channel_id=1, source_target_pairs={{0,2},{1,3},{2,0},{3,1},{4,6},{5,7},{6,4},{7,5},{8,10},{9,11},{10,... | collective-permute-start | bytes 172040 | tf_op jit(solution)/shard_map/ppermute | solution.py:285
  11.0 4.2 %collective-permute-start.2 = (bf16[56,512]{1,0:T(8,128)(2,1)S(1)}, bf16[56,512]{1,0:T(8,128)(2,1)S(1)}, u32[]{:S(2)}, u32[]{:S(2)}) collective-permute-start(bf16[56,512]{1,0:T(8,128)(2,1)S(1)} %concatenate.6.refs_0_), channel_id=1, source_target_pairs={{0,1},{1,0},{2,3},{3,2},{4,5},{5,4},{6,7},{7,6},{8,9},{9,8},{10,11... | collective-permute-start | bytes 172040 | tf_op jit(solution)/shard_map/ppermute | solution.py:285
  12.9 2.2 %collective-permute-start.5 = (bf16[16,512]{1,0:T(8,128)(2,1)S(1)}, bf16[16,512]{1,0:T(8,128)(2,1)S(1)}, u32[]{:S(2)}, u32[]{:S(2)}) collective-permute-start(bf16[16,512]{1,0:T(8,128)(2,1)S(1)} %slice.22), channel_id=1, source_target_pairs={{0,4},{4,0},{8,12},{12,8},{16,20},{20,16},{24,28},{28,24},{1,5},{5... | collective-permute-start | bytes 49160 | tf_op jit(solution)/shard_map/ppermute | solution.py:279
  15.4 5.1 %collective-permute-start.6 = (bf16[136,512]{1,0:T(8,128)(2,1)S(1)}, bf16[136,512]{1,0:T(8,128)(2,1)S(1)}, u32[]{:S(2)}, u32[]{:S(2)}) collective-permute-start(bf16[136,512]{1,0:T(8,128)(2,1)S(1)} %get-tuple-element.22.docs_ref), channel_id=1, source_target_pairs={{0,8},{1,9},{2,10},{3,11},{4,12},{5,13},{6,14},{7,15},{8,0},{9,1},... | collective-permute-start | bytes 417800 | tf_op jit(solution)/shard_map/ppermute | solution.py:285
  17.0 5.0 %collective-permute-start.9 = (bf16[16,512]{1,0:T(8,128)(2,1)S(1)}, bf16[16,512]{1,0:T(8,128)(2,1)S(1)}, u32[]{:S(2)}, u32[]{:S(2)}) collective-permute-start(bf16[16,512]{1,0:T(8,128)(2,1)S(1)} %get-tuple-element.21.both_ref.refs_0_), channel_id=1, source_target_pairs={{0,28},{1,29},{2,30},{3,31},{4,24},{5,25},{6,26},{7,27},{8,20},{9,... | collective-permute-start | bytes 49160 | tf_op jit(solution)/shard_map/ppermute | solution.py:285
  17.1 4.9 %collective-permute-start.8 = (bf16[16,512]{1,0:T(8,128)(2,1)S(1)}, bf16[16,512]{1,0:T(8,128)(2,1)S(1)}, u32[]{:S(2)}, u32[]{:S(2)}) collective-permute-start(bf16[16,512]{1,0:T(8,128)(2,1)S(1)} %get-tuple-element.21.both_ref.refs_0_), channel_id=1, source_target_pairs={{0,20},{1,21},{2,22},{3,23},{4,16},{5,17},{6,18},{7,19},{8,28},{9,... | collective-permute-start | bytes 49160 | tf_op jit(solution)/shard_map/ppermute | solution.py:285
  20.8 1.2 %collective-permute-start.7 = (bf16[16,512]{1,0:T(8,128)(2,1)S(1)}, bf16[16,512]{1,0:T(8,128)(2,1)S(1)}, u32[]{:S(2)}, u32[]{:S(2)}) collective-permute-start(bf16[16,512]{1,0:T(8,128)(2,1)S(1)} %get-tuple-element.27), channel_id=1, source_target_pairs={{0,4},{4,0},{8,12},{12,8},{16,20},{20,16},{24,28},{28,24},{1,5},{5... | collective-permute-start | bytes 49160 | tf_op jit(solution)/shard_map/ppermute | solution.py:279

commit v7 on v6

--- a/solution.py
+++ b/solution.py
@@ -163,12 +163,12 @@
     last = [parts.pop(), parts.pop()][::-1] if apart else []
     sums, peaks, totals = [], [], []
     for part in parts:
-        pool = part[doc_rows:, :].astype(f32)
+        pool = part[...].astype(f32)[doc_rows:]
         sums.append([pool[n : n + recs] + pool[n + recs : n + 2 * recs] for n in (0, 2 * recs)])
         peaks.append(pool[4 * recs :, :128])
         totals.append(pool[4 * recs :, 128:256] + pool[4 * recs :, 256:384])
     if apart:
-        pools = [part[part.shape[0] - 4 * recs :, :].astype(f32) for part in last]
+        pools = [part[...].astype(f32)[part.shape[0] - 4 * recs :] for part in last]
         sums.append([pool[:recs] + pool[recs : 2 * recs] for pool in pools])
         stats = jnp.concatenate([pool[2 * recs : 3 * recs] for pool in pools], 0)
         peaks.append(stats[:, :128])
@@ -195,9 +195,7 @@
         pooled = pooled + part * scales[2 * n * recs : 2 * (n + 1) * recs]
     speech = pooled * lax.rsqrt(jnp.sum(pooled * pooled, axis=1, keepdims=True) + norm_eps)
     both_ref[...] = jnp.concatenate([speech, jnp.zeros((2 * recs, width), f32)], 0).astype(bf16)
-    for n, part in enumerate(parts):
-        send_ref[n * doc_rows : (n + 1) * doc_rows, :] = part[:doc_rows, :]
-    send_ref[len(parts) * doc_rows :, :] = speech.astype(bf16)
+    send_ref[...] = jnp.concatenate([part[:doc_rows, :] for part in parts] + [speech.astype(bf16)], 0)
 
 
 def pair_terms(logits, positive):
@@ -257,10 +255,9 @@
     if len(row_refs) == 1:
         rows = row_refs[0][...]
     else:
-        both, near, *beyond = row_refs
-        near = near[near.shape[0] - 2 * recs :, :].astype(f32)
-        beyond = [ref[...].astype(f32)[: 2 * recs] for ref in beyond]
-        rows = jnp.concatenate([both[...].astype(f32), near, *beyond], 0).astype(bf16)
+        both, near, *beyond = [ref[...].astype(f32) for ref in row_refs]
+        beyond = [part[: 2 * recs] for part in beyond]
+        rows = jnp.concatenate([both, near, *beyond], 0).astype(bf16)
     logits = lax.dot_general(docs_ref[...], rows, BY_ROWS, preferred_element_type=f32)
     positive = lax.broadcasted_iota(jnp.int32, logits.shape, 0) == at_ref[:1, : logits.shape[1]]
     _, grad_b = pair_terms(logits, positive)
@@ -369,7 +366,7 @@
     )(place, both, loss, grad, *near)
     back = to_other_core(send)
     if direct:
-        rows = (both, *near, *beyond)
+        rows = (both, near[0][doc_rows:], *beyond)
     else:
         rows = (lax.all_gather(both[:recs], "grp", tiled=True),)
         at = doc_index[None, :] - (lax.axis_index("grp") * columns + lax.axis_index("tm")) * docs_dev

time: 23.4 us -> 23.4 us (level)
  no operation moved by 1% of the time
where the time goes in v7:
time: 23.4 us; the launch traced here: 23 us
  starting transfers between devices  11.6 us (50%)
  waiting for transfers between devices  5.76 us (25%)
  Pallas kernels  4.8 us (21%)
  between operations  0.72 us (3%)
    ppermute x7, starting transfers between devices, across(): lax.ppermute(value, ('grp', 'tm'), swap_pairs(lax.axis_size('grp') * colu...  11.5 us
    ppermute x7, waiting for transfers between devices, across(): lax.ppermute(value, ('grp', 'tm'), swap_pairs(lax.axis_size('grp') * colu...  5.66 us
    pallas_call x1, Pallas kernels, body(): pl.pallas_call(lambda *refs: pool_kernel((docs_dev, is_direct(columns), d...  3 us
    pallas_call x4, Pallas kernels, call(): pl.pallas_call(kernel, out_shape=outs, in_specs=[VMEM] * len(operands), o...  1.8 us
  transfers between devices with their start and end apart: 10, of which 6 were waited for; matrix products, arithmetic and copies ran while one was open for 0% of the time, Pallas kernels for 16%

profile of v7, /device:TPU:0, one launch (start us, length us, event | category | flops | bytes accessed | tf_op | source)
XLA Modules:
  0.0 23.0 jit_solution(10304721842018329012)
XLA Ops:
  0.6 0.0 copy-start
  0.6 4.1 %collective-permute-start = (bf16[16,512]{1,0:T(8,128)(2,1)}, bf16[16,512]{1,0:T(8,128)(2,1)S(1)}, u32[]{:S(2)}, u32[]{:S(2)}) collective-permute-start(bf16[16,512]{1,0:T(8,128)(2,1)} %docs_ref.1), channel_id=1, source_target_pairs={{0,16},{1,17},{2,18},{3,19},{4,20},{5,21},{6,22},{7,23},{8,24},{9,... | collective-permute-start | bytes 49160 | tf_op jit(solution)/shard_map/ppermute | solution.py:282
  4.7 3.0 %pool.1 = (bf16[16,512]{1,0:T(8,128)(2,1)S(1)}, bf16[16,512]{1,0:T(8,128)(2,1)S(1)}, s32[16,128]{1,0:T(8,128)S(1)}, s32[8,128]{1,0:T(8,128)S(1)}) custom-call(s32[4]{0:T(128)} %refs_0_.1, s32[32]{0:T(128)} %refs_1_.1, bf16[8,1024]{1,0:T(8,128)(2,1)} %refs_2_.1, bf16[4,256,1024]{2,1,0:T(8,128)(2,1)} %refs_3_.1, bf16[1024,512]{1,0:T(8,128)(2,1)} %refs_4_.1, ...), custom_call_target="tpu_custom_call" | custom-call | tf_op jit(solution)/shard_map/pool/pallas_call | solution.py:302
  7.8 0.1 collective-permute-start.1
  7.8 0.0 collective-permute-done
  7.9 2.5 %collective-permute-start.4 = (bf16[48,512]{1,0:T(8,128)(2,1)S(1)}, bf16[48,512]{1,0:T(8,128)(2,1)S(1)}, u32[]{:S(2)}, u32[]{:S(2)}) collective-permute-start(bf16[48,512]{1,0:T(8,128)(2,1)S(1)} %pad_maximum_fusion), channel_id=1, source_target_pairs={{0,3},{1,2},{2,1},{3,0},{4,7},{5,6},{6,5},{7,4},{8,11},{9,10},{10,... | collective-permute-start | bytes 147464 | tf_op jit(solution)/shard_map/ppermute | solution.py:282
  10.4 0.0 collective-permute-done.1
  10.4 0.6 %collective-permute-start.3 = (bf16[56,512]{1,0:T(8,128)(2,1)S(1)}, bf16[56,512]{1,0:T(8,128)(2,1)S(1)}, u32[]{:S(2)}, u32[]{:S(2)}) collective-permute-start(bf16[56,512]{1,0:T(8,128)(2,1)S(1)} %concatenate.6.refs_0_), channel_id=1, source_target_pairs={{0,2},{1,3},{2,0},{3,1},{4,6},{5,7},{6,4},{7,5},{8,10},{9,11},{10,... | collective-permute-start | bytes 172040 | tf_op jit(solution)/shard_map/ppermute | solution.py:282
  11.0 1.1 %collective-permute-start.2 = (bf16[56,512]{1,0:T(8,128)(2,1)S(1)}, bf16[56,512]{1,0:T(8,128)(2,1)S(1)}, u32[]{:S(2)}, u32[]{:S(2)}) collective-permute-start(bf16[56,512]{1,0:T(8,128)(2,1)S(1)} %concatenate.6.refs_0_), channel_id=1, source_target_pairs={{0,1},{1,0},{2,3},{3,2},{4,5},{5,4},{6,7},{7,6},{8,9},{9,8},{10,11... | collective-permute-start | bytes 172040 | tf_op jit(solution)/shard_map/ppermute | solution.py:282
  12.1 0.8 %collective-permute-done.4.refs_3_ = bf16[48,512]{1,0:T(8,128)(2,1)S(1)} collective-permute-done((bf16[48,512]{1,0:T(8,128)(2,1)S(1)}, bf16[48,512]{1,0:T(8,128)(2,1)S(1)}, u32[]{:S(2)}, u32[]{:S(2)}) %collective-permute-start.4) | collective-permute-done | bytes 49184 | tf_op jit(solution)/shard_map/ppermute | solution.py:282
  12.9 0.0 collective-permute-start.5
  12.9 1.7 %collective-permute-done.3.refs_2_ = bf16[56,512]{1,0:T(8,128)(2,1)S(1)} collective-permute-done((bf16[56,512]{1,0:T(8,128)(2,1)S(1)}, bf16[56,512]{1,0:T(8,128)(2,1)S(1)}, u32[]{:S(2)}, u32[]{:S(2)}) %collective-permute-start.3) | collective-permute-done | bytes 57376 | tf_op jit(solution)/shard_map/ppermute | solution.py:282
  14.7 0.5 %collective-permute-done.2.refs_1_ = bf16[56,512]{1,0:T(8,128)(2,1)S(1)} collective-permute-done((bf16[56,512]{1,0:T(8,128)(2,1)S(1)}, bf16[56,512]{1,0:T(8,128)(2,1)S(1)}, u32[]{:S(2)}, u32[]{:S(2)}) %collective-permute-start.2) | collective-permute-done | bytes 57376 | tf_op jit(solution)/shard_map/ppermute | solution.py:282
  15.2 0.0 collective-permute-done.5.refs_4_
  15.2 0.3 %meet.1 = (bf16[136,512]{1,0:T(8,128)(2,1)S(1)}, bf16[16,512]{1,0:T(8,128)(2,1)S(1)}) custom-call(bf16[56,512]{1,0:T(8,128)(2,1)S(1)} %concatenate.6.refs_0_, bf16[56,512]{1,0:T(8,128)(2,1)S(1)} %collective-permute-done.2.refs_1_, bf16[56,512]{1,0:T(8,128)(2,1)S(1)} %collective-permute-done.3.refs_2_, bf16[48,512]{1,0:T(8,128)(2,1)S(1)} %collective-permute-done.4.refs_3_, ...), custom_call_target="tpu_custom_call" | custom-call | tf_op jit(solution)/shard_map/meet/pallas_call | solution.py:22
  15.4 1.6 %collective-permute-start.6 = (bf16[136,512]{1,0:T(8,128)(2,1)S(1)}, bf16[136,512]{1,0:T(8,128)(2,1)S(1)}, u32[]{:S(2)}, u32[]{:S(2)}) collective-permute-start(bf16[136,512]{1,0:T(8,128)(2,1)S(1)} %get-tuple-element.22.docs_ref), channel_id=1, source_target_pairs={{0,8},{1,9},{2,10},{3,11},{4,12},{5,13},{6,14},{7,15},{8,0},{9,1},... | collective-permute-start | bytes 417800 | tf_op jit(solution)/shard_map/ppermute | solution.py:282
  17.0 0.1 collective-permute-start.9
  17.1 1.5 %collective-permute-start.8 = (bf16[16,512]{1,0:T(8,128)(2,1)S(1)}, bf16[16,512]{1,0:T(8,128)(2,1)S(1)}, u32[]{:S(2)}, u32[]{:S(2)}) collective-permute-start(bf16[16,512]{1,0:T(8,128)(2,1)S(1)} %get-tuple-element.21.both_ref.refs_0_), channel_id=1, source_target_pairs={{0,20},{1,21},{2,22},{3,23},{4,16},{5,17},{6,18},{7,19},{8,28},{9,... | collective-permute-start | bytes 49160 | tf_op jit(solution)/shard_map/ppermute | solution.py:282
  18.7 0.3 %first_docs.1 = (f32[16,128]{1,0:T(8,128)S(1)}, f32[16,512]{1,0:T(8,128)S(1)}) custom-call(s32[16,128]{1,0:T(8,128)S(1)} %get-tuple-element.18.place_ref, bf16[16,512]{1,0:T(8,128)(2,1)S(1)} %get-tuple-element.21.both_ref.refs_0_, bf16[136,512]{1,0:T(8,128)(2,1)S(1)} %get-tuple-element.22.docs_ref), custom_call_target="tpu_custom_call" | custom-call | tf_op jit(solution)/shard_map/first_docs/pallas_call | solution.py:22
  19.0 1.5 %collective-permute-done.6.refs_0_ = bf16[136,512]{1,0:T(8,128)(2,1)S(1)} collective-permute-done((bf16[136,512]{1,0:T(8,128)(2,1)S(1)}, bf16[136,512]{1,0:T(8,128)(2,1)S(1)}, u32[]{:S(2)}, u32[]{:S(2)}) %collective-permute-start.6) | collective-permute-done | bytes 139296 | tf_op jit(solution)/shard_map/ppermute | solution.py:282
  20.5 0.3 %share.1 = (f32[4,128]{1,0:T(4,128)S(1)}, f32[4,512]{1,0:T(4,128)S(1)}, bf16[16,512]{1,0:T(8,128)(2,1)S(1)}) custom-call(s32[16,128]{1,0:T(8,128)S(1)} %get-tuple-element.18.place_ref, bf16[16,512]{1,0:T(8,128)(2,1)S(1)} %get-tuple-element.21.both_ref.refs_0_, f32[16,128]{1,0:T(8,128)S(1)} %get-tuple-element.23.loss_ref, ...), custom_call_target="tpu_custom_call" | custom-call | tf_op jit(solution)/shard_map/share/pallas_call | solution.py:22
  20.8 0.1 collective-permute-start.7
  20.9 1.1 %collective-permute-done.9.refs_3_ = bf16[16,512]{1,0:T(8,128)(2,1)S(1)} collective-permute-done((bf16[16,512]{1,0:T(8,128)(2,1)S(1)}, bf16[16,512]{1,0:T(8,128)(2,1)S(1)}, u32[]{:S(2)}, u32[]{:S(2)}) %collective-permute-start.9) | collective-permute-done | bytes 16416 | tf_op jit(solution)/shard_map/ppermute | solution.py:282
  22.0 0.0 collective-permute-done.8.refs_2_
  22.0 0.1 collective-permute-done.7.back_ref
  22.1 0.0 copy-done
  22.1 0.9 %last.1 = (f32[1,4]{1,0:T(1,128)}, f32[4,512]{1,0:T(4,128)}, f32[16,512]{1,0:T(8,128)}) custom-call(s32[8,128]{1,0:T(8,128)S(1)} %get-tuple-element.17.at_ref, bf16[16,512]{1,0:T(8,128)(2,1)S(1)} %copy-done, f32[4,128]{1,0:T(4,128)S(1)} %get-tuple-element.25.loss_ref, f32[4,512]{1,0:T(4,128)S(1)} %get-tuple-element.26.grad_ref, ...), custom_call_target="tpu_custom_call" | custom-call | tf_op jit(solution)/shard_map/last/pallas_call | solution.py:22
  (8 shorter events, 0.1 us)
Async XLA Ops:
  0.6 21.5 %copy-start = (bf16[16,512]{1,0:T(8,128)(2,1)S(1)}, bf16[16,512]{1,0:T(8,128)(2,1)}, u32[]{:S(2)}) copy-start(bf16[16,512]{1,0:T(8,128)(2,1)} %docs_ref.1) | copy-start | bytes 49156
  0.6 7.2 %collective-permute-start = (bf16[16,512]{1,0:T(8,128)(2,1)}, bf16[16,512]{1,0:T(8,128)(2,1)S(1)}, u32[]{:S(2)}, u32[]{:S(2)}) collective-permute-start(bf16[16,512]{1,0:T(8,128)(2,1)} %docs_ref.1), channel_id=1, source_target_pairs={{0,16},{1,17},{2,18},{3,19},{4,20},{5,21},{6,22},{7,23},{8,24},{9,... | collective-permute-start | bytes 49160 | tf_op jit(solution)/shard_map/ppermute | solution.py:282
  7.8 2.6 %collective-permute-start.1 = (bf16[16,512]{1,0:T(8,128)(2,1)S(1)}, bf16[16,512]{1,0:T(8,128)(2,1)S(1)}, u32[]{:S(2)}, u32[]{:S(2)}) collective-permute-start(bf16[16,512]{1,0:T(8,128)(2,1)S(1)} %get-tuple-element.20), channel_id=1, source_target_pairs={{0,4},{4,0},{8,12},{12,8},{16,20},{20,16},{24,28},{28,24},{1,5},{5... | collective-permute-start | bytes 49160 | tf_op jit(solution)/shard_map/ppermute | solution.py:276
  7.9 5.1 %collective-permute-start.4 = (bf16[48,512]{1,0:T(8,128)(2,1)S(1)}, bf16[48,512]{1,0:T(8,128)(2,1)S(1)}, u32[]{:S(2)}, u32[]{:S(2)}) collective-permute-start(bf16[48,512]{1,0:T(8,128)(2,1)S(1)} %pad_maximum_fusion), channel_id=1, source_target_pairs={{0,3},{1,2},{2,1},{3,0},{4,7},{5,6},{6,5},{7,4},{8,11},{9,10},{10,... | collective-permute-start | bytes 147464 | tf_op jit(solution)/shard_map/ppermute | solution.py:282
  10.4 4.2 %collective-permute-start.3 = (bf16[56,512]{1,0:T(8,128)(2,1)S(1)}, bf16[56,512]{1,0:T(8,128)(2,1)S(1)}, u32[]{:S(2)}, u32[]{:S(2)}) collective-permute-start(bf16[56,512]{1,0:T(8,128)(2,1)S(1)} %concatenate.6.refs_0_), channel_id=1, source_target_pairs={{0,2},{1,3},{2,0},{3,1},{4,6},{5,7},{6,4},{7,5},{8,10},{9,11},{10,... | collective-permute-start | bytes 172040 | tf_op jit(solution)/shard_map/ppermute | solution.py:282
  11.0 4.2 %collective-permute-start.2 = (bf16[56,512]{1,0:T(8,128)(2,1)S(1)}, bf16[56,512]{1,0:T(8,128)(2,1)S(1)}, u32[]{:S(2)}, u32[]{:S(2)}) collective-permute-start(bf16[56,512]{1,0:T(8,128)(2,1)S(1)} %concatenate.6.refs_0_), channel_id=1, source_target_pairs={{0,1},{1,0},{2,3},{3,2},{4,5},{5,4},{6,7},{7,6},{8,9},{9,8},{10,11... | collective-permute-start | bytes 172040 | tf_op jit(solution)/shard_map/ppermute | solution.py:282
  12.9 2.2 %collective-permute-start.5 = (bf16[16,512]{1,0:T(8,128)(2,1)S(1)}, bf16[16,512]{1,0:T(8,128)(2,1)S(1)}, u32[]{:S(2)}, u32[]{:S(2)}) collective-permute-start(bf16[16,512]{1,0:T(8,128)(2,1)S(1)} %slice.26), channel_id=1, source_target_pairs={{0,4},{4,0},{8,12},{12,8},{16,20},{20,16},{24,28},{28,24},{1,5},{5... | collective-permute-start | bytes 49160 | tf_op jit(solution)/shard_map/ppermute | solution.py:276
  15.4 5.1 %collective-permute-start.6 = (bf16[136,512]{1,0:T(8,128)(2,1)S(1)}, bf16[136,512]{1,0:T(8,128)(2,1)S(1)}, u32[]{:S(2)}, u32[]{:S(2)}) collective-permute-start(bf16[136,512]{1,0:T(8,128)(2,1)S(1)} %get-tuple-element.22.docs_ref), channel_id=1, source_target_pairs={{0,8},{1,9},{2,10},{3,11},{4,12},{5,13},{6,14},{7,15},{8,0},{9,1},... | collective-permute-start | bytes 417800 | tf_op jit(solution)/shard_map/ppermute | solution.py:282
  17.0 5.0 %collective-permute-start.9 = (bf16[16,512]{1,0:T(8,128)(2,1)S(1)}, bf16[16,512]{1,0:T(8,128)(2,1)S(1)}, u32[]{:S(2)}, u32[]{:S(2)}) collective-permute-start(bf16[16,512]{1,0:T(8,128)(2,1)S(1)} %get-tuple-element.21.both_ref.refs_0_), channel_id=1, source_target_pairs={{0,28},{1,29},{2,30},{3,31},{4,24},{5,25},{6,26},{7,27},{8,20},{9,... | collective-permute-start | bytes 49160 | tf_op jit(solution)/shard_map/ppermute | solution.py:282
  17.1 4.9 %collective-permute-start.8 = (bf16[16,512]{1,0:T(8,128)(2,1)S(1)}, bf16[16,512]{1,0:T(8,128)(2,1)S(1)}, u32[]{:S(2)}, u32[]{:S(2)}) collective-permute-start(bf16[16,512]{1,0:T(8,128)(2,1)S(1)} %get-tuple-element.21.both_ref.refs_0_), channel_id=1, source_target_pairs={{0,20},{1,21},{2,22},{3,23},{4,16},{5,17},{6,18},{7,19},{8,28},{9,... | collective-permute-start | bytes 49160 | tf_op jit(solution)/shard_map/ppermute | solution.py:282
  20.8 1.2 %collective-permute-start.7 = (bf16[16,512]{1,0:T(8,128)(2,1)S(1)}, bf16[16,512]{1,0:T(8,128)(2,1)S(1)}, u32[]{:S(2)}, u32[]{:S(2)}) collective-permute-start(bf16[16,512]{1,0:T(8,128)(2,1)S(1)} %get-tuple-element.27), channel_id=1, source_target_pairs={{0,4},{4,0},{8,12},{12,8},{16,20},{20,16},{24,28},{28,24},{1,5},{5... | collective-permute-start | bytes 49160 | tf_op jit(solution)/shard_map/ppermute | solution.py:276

commit v8 on v7

--- a/solution.py
+++ b/solution.py
@@ -82,16 +82,19 @@
         of_group, rest = target // (tm * docs_dev), target % (tm * docs_dev)
         of_layer = of_group // 2
         at = (rest // docs_dev) ^ (column if by_column else 0)
+        crossed = of_group + core
+        if by_column:
+            crossed = crossed + jnp.where(at == tm - 1, 1, 0)
         if by_layer:
             steps = of_layer ^ layer
             far = steps // 2
             at = (at * 2 + far) * docs_dev + rest % docs_dev
             chunk = steps % 2
-            mine = (of_group + core) % 2 == 0
+            crossed = crossed + far
         else:
             at = (of_layer * tm + at) * docs_dev + rest % docs_dev
             chunk = 0
-            mine = (of_group + core) % 2 == 0
+        mine = crossed % 2 == 0
         chunk = jnp.where(mine, chunk, -1)
         place = jnp.where((row == r) & (spot == chunk), at, place)
     place_ref[...] = place
@@ -168,7 +171,7 @@
         peaks.append(pool[4 * recs :, :128])
         totals.append(pool[4 * recs :, 128:256] + pool[4 * recs :, 256:384])
     if apart:
-        pools = [part[...].astype(f32)[part.shape[0] - 4 * recs :] for part in last]
+        pools = [part[...].astype(f32)[part.shape[0] - 4 * recs :] for part in last[::-1]]
         sums.append([pool[:recs] + pool[recs : 2 * recs] for pool in pools])
         stats = jnp.concatenate([pool[2 * recs : 3 * recs] for pool in pools], 0)
         peaks.append(stats[:, :128])
@@ -298,7 +301,7 @@
     if direct:
         blocks = [(0, 0), (0, 1), None, None, (1, 0), (1, 1)]
         blocks += [(steps, flip) for steps in order for flip in (1, 0)]
-        far = across(doc_embed, 2, 0)
+        far = across(doc_embed, 2, 0, 1)
     docs, pools, place, at = pl.pallas_call(
         lambda *refs: pool_kernel((docs_dev, is_direct(columns), direct), blocks, *refs),
         out_shape=(
@@ -333,7 +336,7 @@
     doc_rows = columns * (payload.shape[0] - 6 * recs)
     if is_direct(columns):
         parts += [across(payload, 0, steps) for steps in range(1, columns - 1)]
-        parts.append(across(jnp.concatenate([*docs, pools]), 0, columns - 1))
+        parts.append(across(jnp.concatenate([*docs, pools]), 0, columns - 1, 1))
         parts.append(to_other_core(parts[-1][doc_rows // columns :]))
     else:
         parts = list(lax.all_gather(payload, "tm"))

time: 23.4 us -> 22.9 us (0.979)
    ppermute x7, starting transfers between devices: 11.5 us -> 10.6 us  [across(): lax.ppermute(value, ('grp', 'tm'), swap_pairs(lax.axis_size('grp') * colu...]
    ppermute x3, starting transfers between devices: 0.14 us -> 0.93 us  [to_other_core(): return lax.ppermute(value, 'grp', swap_pairs(lax.axis_size('grp'), 1, 1))]
where the time goes in v8:
time: 22.9 us; the launch traced here: 22.7 us
  starting transfers between devices  11.6 us (51%)
  waiting for transfers between devices  5.59 us (24%)
  Pallas kernels  4.81 us (21%)
  between operations  0.7 us (3%)
    ppermute x7, starting transfers between devices, across(): lax.ppermute(value, ('grp', 'tm'), swap_pairs(lax.axis_size('grp') * colu...  10.6 us
    ppermute x7, waiting for transfers between devices, across(): lax.ppermute(value, ('grp', 'tm'), swap_pairs(lax.axis_size('grp') * colu...  5.5 us
    pallas_call x1, Pallas kernels, body(): pl.pallas_call(lambda *refs: pool_kernel((docs_dev, is_direct(columns), d...  3 us
    pallas_call x4, Pallas kernels, call(): pl.pallas_call(kernel, out_shape=outs, in_specs=[VMEM] * len(operands), o...  1.8 us
    ppermute x3, starting transfers between devices, to_other_core(): return lax.ppermute(value, 'grp', swap_pairs(lax.axis_size('grp'), 1, 1))  0.93 us
  transfers between devices with their start and end apart: 10, of which 6 were waited for; matrix products, arithmetic and copies ran while one was open for 0% of the time, Pallas kernels for 16%

profile of v8, /device:TPU:0, one launch (start us, length us, event | category | flops | bytes accessed | tf_op | source)
XLA Modules:
  0.0 22.7 jit_solution(14296199409747018300)
XLA Ops:
  0.6 0.0 copy-start
  0.6 3.5 %collective-permute-start = (bf16[16,512]{1,0:T(8,128)(2,1)}, bf16[16,512]{1,0:T(8,128)(2,1)S(1)}, u32[]{:S(2)}, u32[]{:S(2)}) collective-permute-start(bf16[16,512]{1,0:T(8,128)(2,1)} %docs_ref.1), channel_id=1, source_target_pairs={{0,20},{1,21},{2,22},{3,23},{4,16},{5,17},{6,18},{7,19},{8,28},{9,... | collective-permute-start | bytes 49160 | tf_op jit(solution)/shard_map/ppermute | solution.py:285
  4.2 3.0 %pool.1 = (bf16[16,512]{1,0:T(8,128)(2,1)S(1)}, bf16[16,512]{1,0:T(8,128)(2,1)S(1)}, s32[16,128]{1,0:T(8,128)S(1)}, s32[8,128]{1,0:T(8,128)S(1)}) custom-call(s32[4]{0:T(128)} %refs_0_.1, s32[32]{0:T(128)} %refs_1_.1, bf16[8,1024]{1,0:T(8,128)(2,1)} %refs_2_.1, bf16[4,256,1024]{2,1,0:T(8,128)(2,1)} %refs_3_.1, bf16[1024,512]{1,0:T(8,128)(2,1)} %refs_4_.1, ...), custom_call_target="tpu_custom_call" | custom-call | tf_op jit(solution)/shard_map/pool/pallas_call | solution.py:305
  7.2 0.7 %collective-permute-start.1 = (bf16[16,512]{1,0:T(8,128)(2,1)S(1)}, bf16[16,512]{1,0:T(8,128)(2,1)S(1)}, u32[]{:S(2)}, u32[]{:S(2)}) collective-permute-start(bf16[16,512]{1,0:T(8,128)(2,1)S(1)} %get-tuple-element.20), channel_id=1, source_target_pairs={{0,4},{4,0},{8,12},{12,8},{16,20},{20,16},{24,28},{28,24},{1,5},{5... | collective-permute-start | bytes 49160 | tf_op jit(solution)/shard_map/ppermute | solution.py:279
  7.9 0.0 collective-permute-done
  7.9 2.1 %collective-permute-start.4 = (bf16[48,512]{1,0:T(8,128)(2,1)S(1)}, bf16[48,512]{1,0:T(8,128)(2,1)S(1)}, u32[]{:S(2)}, u32[]{:S(2)}) collective-permute-start(bf16[48,512]{1,0:T(8,128)(2,1)S(1)} %pad_maximum_fusion), channel_id=1, source_target_pairs={{0,7},{1,6},{2,5},{3,4},{4,3},{5,2},{6,1},{7,0},{8,15},{9,14},{10,... | collective-permute-start | bytes 147464 | tf_op jit(solution)/shard_map/ppermute | solution.py:285
  10.1 0.0 collective-permute-done.1
  10.2 0.6 %collective-permute-start.3 = (bf16[56,512]{1,0:T(8,128)(2,1)S(1)}, bf16[56,512]{1,0:T(8,128)(2,1)S(1)}, u32[]{:S(2)}, u32[]{:S(2)}) collective-permute-start(bf16[56,512]{1,0:T(8,128)(2,1)S(1)} %concatenate.6.refs_0_), channel_id=1, source_target_pairs={{0,2},{1,3},{2,0},{3,1},{4,6},{5,7},{6,4},{7,5},{8,10},{9,11},{10,... | collective-permute-start | bytes 172040 | tf_op jit(solution)/shard_map/ppermute | solution.py:285
  10.7 1.2 %collective-permute-start.2 = (bf16[56,512]{1,0:T(8,128)(2,1)S(1)}, bf16[56,512]{1,0:T(8,128)(2,1)S(1)}, u32[]{:S(2)}, u32[]{:S(2)}) collective-permute-start(bf16[56,512]{1,0:T(8,128)(2,1)S(1)} %concatenate.6.refs_0_), channel_id=1, source_target_pairs={{0,1},{1,0},{2,3},{3,2},{4,5},{5,4},{6,7},{7,6},{8,9},{9,8},{10,11... | collective-permute-start | bytes 172040 | tf_op jit(solution)/shard_map/ppermute | solution.py:285
  11.9 0.9 %collective-permute-done.4.refs_3_ = bf16[48,512]{1,0:T(8,128)(2,1)S(1)} collective-permute-done((bf16[48,512]{1,0:T(8,128)(2,1)S(1)}, bf16[48,512]{1,0:T(8,128)(2,1)S(1)}, u32[]{:S(2)}, u32[]{:S(2)}) %collective-permute-start.4) | collective-permute-done | bytes 49184 | tf_op jit(solution)/shard_map/ppermute | solution.py:285
  12.7 0.1 collective-permute-start.5
  12.9 1.7 %collective-permute-done.3.refs_2_ = bf16[56,512]{1,0:T(8,128)(2,1)S(1)} collective-permute-done((bf16[56,512]{1,0:T(8,128)(2,1)S(1)}, bf16[56,512]{1,0:T(8,128)(2,1)S(1)}, u32[]{:S(2)}, u32[]{:S(2)}) %collective-permute-start.3) | collective-permute-done | bytes 57376 | tf_op jit(solution)/shard_map/ppermute | solution.py:285
  14.5 0.4 %collective-permute-done.2.refs_1_ = bf16[56,512]{1,0:T(8,128)(2,1)S(1)} collective-permute-done((bf16[56,512]{1,0:T(8,128)(2,1)S(1)}, bf16[56,512]{1,0:T(8,128)(2,1)S(1)}, u32[]{:S(2)}, u32[]{:S(2)}) %collective-permute-start.2) | collective-permute-done | bytes 57376 | tf_op jit(solution)/shard_map/ppermute | solution.py:285
  14.9 0.0 collective-permute-done.5.refs_4_
  14.9 0.3 %meet.1 = (bf16[136,512]{1,0:T(8,128)(2,1)S(1)}, bf16[16,512]{1,0:T(8,128)(2,1)S(1)}) custom-call(bf16[56,512]{1,0:T(8,128)(2,1)S(1)} %concatenate.6.refs_0_, bf16[56,512]{1,0:T(8,128)(2,1)S(1)} %collective-permute-done.2.refs_1_, bf16[56,512]{1,0:T(8,128)(2,1)S(1)} %collective-permute-done.3.refs_2_, bf16[48,512]{1,0:T(8,128)(2,1)S(1)} %collective-permute-done.4.refs_3_, ...), custom_call_target="tpu_custom_call" | custom-call | tf_op jit(solution)/shard_map/meet/pallas_call | solution.py:22
  15.2 1.6 %collective-permute-start.6 = (bf16[136,512]{1,0:T(8,128)(2,1)S(1)}, bf16[136,512]{1,0:T(8,128)(2,1)S(1)}, u32[]{:S(2)}, u32[]{:S(2)}) collective-permute-start(bf16[136,512]{1,0:T(8,128)(2,1)S(1)} %get-tuple-element.22.docs_ref), channel_id=1, source_target_pairs={{0,8},{1,9},{2,10},{3,11},{4,12},{5,13},{6,14},{7,15},{8,0},{9,1},... | collective-permute-start | bytes 417800 | tf_op jit(solution)/shard_map/ppermute | solution.py:285
  16.8 0.0 collective-permute-start.9
  16.8 1.6 %collective-permute-start.8 = (bf16[16,512]{1,0:T(8,128)(2,1)S(1)}, bf16[16,512]{1,0:T(8,128)(2,1)S(1)}, u32[]{:S(2)}, u32[]{:S(2)}) collective-permute-start(bf16[16,512]{1,0:T(8,128)(2,1)S(1)} %get-tuple-element.21.both_ref.refs_0_), channel_id=1, source_target_pairs={{0,20},{1,21},{2,22},{3,23},{4,16},{5,17},{6,18},{7,19},{8,28},{9,... | collective-permute-start | bytes 49160 | tf_op jit(solution)/shard_map/ppermute | solution.py:285
  18.4 0.3 %first_docs.1 = (f32[16,128]{1,0:T(8,128)S(1)}, f32[16,512]{1,0:T(8,128)S(1)}) custom-call(s32[16,128]{1,0:T(8,128)S(1)} %get-tuple-element.18.place_ref, bf16[16,512]{1,0:T(8,128)(2,1)S(1)} %get-tuple-element.21.both_ref.refs_0_, bf16[136,512]{1,0:T(8,128)(2,1)S(1)} %get-tuple-element.22.docs_ref), custom_call_target="tpu_custom_call" | custom-call | tf_op jit(solution)/shard_map/first_docs/pallas_call | solution.py:22
  18.7 1.5 %collective-permute-done.6.refs_0_ = bf16[136,512]{1,0:T(8,128)(2,1)S(1)} collective-permute-done((bf16[136,512]{1,0:T(8,128)(2,1)S(1)}, bf16[136,512]{1,0:T(8,128)(2,1)S(1)}, u32[]{:S(2)}, u32[]{:S(2)}) %collective-permute-start.6) | collective-permute-done | bytes 139296 | tf_op jit(solution)/shard_map/ppermute | solution.py:285
  20.2 0.3 %share.1 = (f32[4,128]{1,0:T(4,128)S(1)}, f32[4,512]{1,0:T(4,128)S(1)}, bf16[16,512]{1,0:T(8,128)(2,1)S(1)}) custom-call(s32[16,128]{1,0:T(8,128)S(1)} %get-tuple-element.18.place_ref, bf16[16,512]{1,0:T(8,128)(2,1)S(1)} %get-tuple-element.21.both_ref.refs_0_, f32[16,128]{1,0:T(8,128)S(1)} %get-tuple-element.23.loss_ref, ...), custom_call_target="tpu_custom_call" | custom-call | tf_op jit(solution)/shard_map/share/pallas_call | solution.py:22
  20.6 0.1 collective-permute-start.7
  20.7 1.1 %collective-permute-done.9.refs_3_ = bf16[16,512]{1,0:T(8,128)(2,1)S(1)} collective-permute-done((bf16[16,512]{1,0:T(8,128)(2,1)S(1)}, bf16[16,512]{1,0:T(8,128)(2,1)S(1)}, u32[]{:S(2)}, u32[]{:S(2)}) %collective-permute-start.9) | collective-permute-done | bytes 16416 | tf_op jit(solution)/shard_map/ppermute | solution.py:285
  21.7 0.0 collective-permute-done.8.refs_2_
  21.7 0.1 collective-permute-done.7.back_ref
  21.8 0.0 copy-done
  21.8 0.9 %last.1 = (f32[1,4]{1,0:T(1,128)}, f32[4,512]{1,0:T(4,128)}, f32[16,512]{1,0:T(8,128)}) custom-call(s32[8,128]{1,0:T(8,128)S(1)} %get-tuple-element.17.at_ref, bf16[16,512]{1,0:T(8,128)(2,1)S(1)} %copy-done, f32[4,128]{1,0:T(4,128)S(1)} %get-tuple-element.25.loss_ref, f32[4,512]{1,0:T(4,128)S(1)} %get-tuple-element.26.grad_ref, ...), custom_call_target="tpu_custom_call" | custom-call | tf_op jit(solution)/shard_map/last/pallas_call | solution.py:22
  (8 shorter events, 0.1 us)
Async XLA Ops:
  0.6 21.2 %copy-start = (bf16[16,512]{1,0:T(8,128)(2,1)S(1)}, bf16[16,512]{1,0:T(8,128)(2,1)}, u32[]{:S(2)}) copy-start(bf16[16,512]{1,0:T(8,128)(2,1)} %docs_ref.1) | copy-start | bytes 49156
  0.6 7.3 %collective-permute-start = (bf16[16,512]{1,0:T(8,128)(2,1)}, bf16[16,512]{1,0:T(8,128)(2,1)S(1)}, u32[]{:S(2)}, u32[]{:S(2)}) collective-permute-start(bf16[16,512]{1,0:T(8,128)(2,1)} %docs_ref.1), channel_id=1, source_target_pairs={{0,20},{1,21},{2,22},{3,23},{4,16},{5,17},{6,18},{7,19},{8,28},{9,... | collective-permute-start | bytes 49160 | tf_op jit(solution)/shard_map/ppermute | solution.py:285
  7.2 2.9 %collective-permute-start.1 = (bf16[16,512]{1,0:T(8,128)(2,1)S(1)}, bf16[16,512]{1,0:T(8,128)(2,1)S(1)}, u32[]{:S(2)}, u32[]{:S(2)}) collective-permute-start(bf16[16,512]{1,0:T(8,128)(2,1)S(1)} %get-tuple-element.20), channel_id=1, source_target_pairs={{0,4},{4,0},{8,12},{12,8},{16,20},{20,16},{24,28},{28,24},{1,5},{5... | collective-permute-start | bytes 49160 | tf_op jit(solution)/shard_map/ppermute | solution.py:279
  7.9 4.8 %collective-permute-start.4 = (bf16[48,512]{1,0:T(8,128)(2,1)S(1)}, bf16[48,512]{1,0:T(8,128)(2,1)S(1)}, u32[]{:S(2)}, u32[]{:S(2)}) collective-permute-start(bf16[48,512]{1,0:T(8,128)(2,1)S(1)} %pad_maximum_fusion), channel_id=1, source_target_pairs={{0,7},{1,6},{2,5},{3,4},{4,3},{5,2},{6,1},{7,0},{8,15},{9,14},{10,... | collective-permute-start | bytes 147464 | tf_op jit(solution)/shard_map/ppermute | solution.py:285
  10.2 4.4 %collective-permute-start.3 = (bf16[56,512]{1,0:T(8,128)(2,1)S(1)}, bf16[56,512]{1,0:T(8,128)(2,1)S(1)}, u32[]{:S(2)}, u32[]{:S(2)}) collective-permute-start(bf16[56,512]{1,0:T(8,128)(2,1)S(1)} %concatenate.6.refs_0_), channel_id=1, source_target_pairs={{0,2},{1,3},{2,0},{3,1},{4,6},{5,7},{6,4},{7,5},{8,10},{9,11},{10,... | collective-permute-start | bytes 172040 | tf_op jit(solution)/shard_map/ppermute | solution.py:285
  10.7 4.2 %collective-permute-start.2 = (bf16[56,512]{1,0:T(8,128)(2,1)S(1)}, bf16[56,512]{1,0:T(8,128)(2,1)S(1)}, u32[]{:S(2)}, u32[]{:S(2)}) collective-permute-start(bf16[56,512]{1,0:T(8,128)(2,1)S(1)} %concatenate.6.refs_0_), channel_id=1, source_target_pairs={{0,1},{1,0},{2,3},{3,2},{4,5},{5,4},{6,7},{7,6},{8,9},{9,8},{10,11... | collective-permute-start | bytes 172040 | tf_op jit(solution)/shard_map/ppermute | solution.py:285
  12.7 2.2 %collective-permute-start.5 = (bf16[16,512]{1,0:T(8,128)(2,1)S(1)}, bf16[16,512]{1,0:T(8,128)(2,1)S(1)}, u32[]{:S(2)}, u32[]{:S(2)}) collective-permute-start(bf16[16,512]{1,0:T(8,128)(2,1)S(1)} %slice.26), channel_id=1, source_target_pairs={{0,4},{4,0},{8,12},{12,8},{16,20},{20,16},{24,28},{28,24},{1,5},{5... | collective-permute-start | bytes 49160 | tf_op jit(solution)/shard_map/ppermute | solution.py:279
  15.2 5.1 %collective-permute-start.6 = (bf16[136,512]{1,0:T(8,128)(2,1)S(1)}, bf16[136,512]{1,0:T(8,128)(2,1)S(1)}, u32[]{:S(2)}, u32[]{:S(2)}) collective-permute-start(bf16[136,512]{1,0:T(8,128)(2,1)S(1)} %get-tuple-element.22.docs_ref), channel_id=1, source_target_pairs={{0,8},{1,9},{2,10},{3,11},{4,12},{5,13},{6,14},{7,15},{8,0},{9,1},... | collective-permute-start | bytes 417800 | tf_op jit(solution)/shard_map/ppermute | solution.py:285
  16.8 5.0 %collective-permute-start.9 = (bf16[16,512]{1,0:T(8,128)(2,1)S(1)}, bf16[16,512]{1,0:T(8,128)(2,1)S(1)}, u32[]{:S(2)}, u32[]{:S(2)}) collective-permute-start(bf16[16,512]{1,0:T(8,128)(2,1)S(1)} %get-tuple-element.21.both_ref.refs_0_), channel_id=1, source_target_pairs={{0,28},{1,29},{2,30},{3,31},{4,24},{5,25},{6,26},{7,27},{8,20},{9,... | collective-permute-start | bytes 49160 | tf_op jit(solution)/shard_map/ppermute | solution.py:285
  16.8 5.0 %collective-permute-start.8 = (bf16[16,512]{1,0:T(8,128)(2,1)S(1)}, bf16[16,512]{1,0:T(8,128)(2,1)S(1)}, u32[]{:S(2)}, u32[]{:S(2)}) collective-permute-start(bf16[16,512]{1,0:T(8,128)(2,1)S(1)} %get-tuple-element.21.both_ref.refs_0_), channel_id=1, source_target_pairs={{0,20},{1,21},{2,22},{3,23},{4,16},{5,17},{6,18},{7,19},{8,28},{9,... | collective-permute-start | bytes 49160 | tf_op jit(solution)/shard_map/ppermute | solution.py:285
  20.6 1.2 %collective-permute-start.7 = (bf16[16,512]{1,0:T(8,128)(2,1)S(1)}, bf16[16,512]{1,0:T(8,128)(2,1)S(1)}, u32[]{:S(2)}, u32[]{:S(2)}) collective-permute-start(bf16[16,512]{1,0:T(8,128)(2,1)S(1)} %get-tuple-element.27), channel_id=1, source_target_pairs={{0,4},{4,0},{8,12},{12,8},{16,20},{20,16},{24,28},{28,24},{1,5},{5... | collective-permute-start | bytes 49160 | tf_op jit(solution)/shard_map/ppermute | solution.py:279

commit v9 on v8

--- a/solution.py
+++ b/solution.py
@@ -188,11 +188,10 @@
     used = lax.broadcasted_iota(jnp.int32, whole.shape, 1) < heads
     inverse = jnp.where(used, 1.0 / jnp.where(used, whole, 1.0), 0.0)
     high, low = two_terms(jnp.concatenate([share * inverse for share in shares], 0))
-    spread = lax.broadcasted_iota(jnp.int32, (128, width), 1) // (width // heads)
-    spread = (spread == lax.broadcasted_iota(jnp.int32, (128, width), 0)).astype(f32).astype(bf16)
-    scales = jnp.dot(high, spread, preferred_element_type=f32) + jnp.dot(
-        low, spread, preferred_element_type=f32
-    )
+    spread = lax.broadcasted_iota(jnp.int32, (16, width), 1) // (width // heads)
+    spread = (spread == lax.broadcasted_iota(jnp.int32, (16, width), 0)).astype(f32).astype(bf16)
+    scales = jnp.dot(jnp.concatenate([high, low], 0)[:, :16], spread, preferred_element_type=f32)
+    scales = scales[: high.shape[0]] + scales[high.shape[0] :]
     pooled = jnp.zeros((2 * recs, width), f32)
     for n, part in enumerate(sums):
         pooled = pooled + part * scales[2 * n * recs : 2 * (n + 1) * recs]

time: 22.9 us -> 22.9 us (level)
  no operation moved by 1% of the time
where the time goes in v9:
time: 22.9 us; the launch traced here: 22.7 us
  starting transfers between devices  11.6 us (51%)
  waiting for transfers between devices  5.59 us (24%)
  Pallas kernels  4.78 us (21%)
  between operations  0.7 us (3%)
    ppermute x7, starting transfers between devices, across(): lax.ppermute(value, ('grp', 'tm'), swap_pairs(lax.axis_size('grp') * colu...  10.6 us
    ppermute x7, waiting for transfers between devices, across(): lax.ppermute(value, ('grp', 'tm'), swap_pairs(lax.axis_size('grp') * colu...  5.5 us
    pallas_call x1, Pallas kernels, body(): pl.pallas_call(lambda *refs: pool_kernel((docs_dev, is_direct(columns), d...  3 us
    pallas_call x4, Pallas kernels, call(): pl.pallas_call(kernel, out_shape=outs, in_specs=[VMEM] * len(operands), o...  1.78 us
    ppermute x3, starting transfers between devices, to_other_core(): return lax.ppermute(value, 'grp', swap_pairs(lax.axis_size('grp'), 1, 1))  0.93 us
  transfers between devices with their start and end apart: 10, of which 6 were waited for; matrix products, arithmetic and copies ran while one was open for 0% of the time, Pallas kernels for 16%

profile of v9, /device:TPU:0, one launch (start us, length us, event | category | flops | bytes accessed | tf_op | source)
XLA Modules:
  0.0 22.7 jit_solution(5250941084688817961)
XLA Ops:
  0.6 0.0 copy-start
  0.6 3.5 %collective-permute-start = (bf16[16,512]{1,0:T(8,128)(2,1)}, bf16[16,512]{1,0:T(8,128)(2,1)S(1)}, u32[]{:S(2)}, u32[]{:S(2)}) collective-permute-start(bf16[16,512]{1,0:T(8,128)(2,1)} %docs_ref.1), channel_id=1, source_target_pairs={{0,20},{1,21},{2,22},{3,23},{4,16},{5,17},{6,18},{7,19},{8,28},{9,... | collective-permute-start | bytes 49160 | tf_op jit(solution)/shard_map/ppermute | solution.py:284
  4.2 3.0 %pool.1 = (bf16[16,512]{1,0:T(8,128)(2,1)S(1)}, bf16[16,512]{1,0:T(8,128)(2,1)S(1)}, s32[16,128]{1,0:T(8,128)S(1)}, s32[8,128]{1,0:T(8,128)S(1)}) custom-call(s32[4]{0:T(128)} %refs_0_.1, s32[32]{0:T(128)} %refs_1_.1, bf16[8,1024]{1,0:T(8,128)(2,1)} %refs_2_.1, bf16[4,256,1024]{2,1,0:T(8,128)(2,1)} %refs_3_.1, bf16[1024,512]{1,0:T(8,128)(2,1)} %refs_4_.1, ...), custom_call_target="tpu_custom_call" | custom-call | tf_op jit(solution)/shard_map/pool/pallas_call | solution.py:304
  7.2 0.7 %collective-permute-start.1 = (bf16[16,512]{1,0:T(8,128)(2,1)S(1)}, bf16[16,512]{1,0:T(8,128)(2,1)S(1)}, u32[]{:S(2)}, u32[]{:S(2)}) collective-permute-start(bf16[16,512]{1,0:T(8,128)(2,1)S(1)} %get-tuple-element.20), channel_id=1, source_target_pairs={{0,4},{4,0},{8,12},{12,8},{16,20},{20,16},{24,28},{28,24},{1,5},{5... | collective-permute-start | bytes 49160 | tf_op jit(solution)/shard_map/ppermute | solution.py:278
  7.9 0.0 collective-permute-done
  7.9 2.1 %collective-permute-start.4 = (bf16[48,512]{1,0:T(8,128)(2,1)S(1)}, bf16[48,512]{1,0:T(8,128)(2,1)S(1)}, u32[]{:S(2)}, u32[]{:S(2)}) collective-permute-start(bf16[48,512]{1,0:T(8,128)(2,1)S(1)} %pad_maximum_fusion), channel_id=1, source_target_pairs={{0,7},{1,6},{2,5},{3,4},{4,3},{5,2},{6,1},{7,0},{8,15},{9,14},{10,... | collective-permute-start | bytes 147464 | tf_op jit(solution)/shard_map/ppermute | solution.py:284
  10.1 0.0 collective-permute-done.1
  10.2 0.6 %collective-permute-start.3 = (bf16[56,512]{1,0:T(8,128)(2,1)S(1)}, bf16[56,512]{1,0:T(8,128)(2,1)S(1)}, u32[]{:S(2)}, u32[]{:S(2)}) collective-permute-start(bf16[56,512]{1,0:T(8,128)(2,1)S(1)} %concatenate.6.refs_0_), channel_id=1, source_target_pairs={{0,2},{1,3},{2,0},{3,1},{4,6},{5,7},{6,4},{7,5},{8,10},{9,11},{10,... | collective-permute-start | bytes 172040 | tf_op jit(solution)/shard_map/ppermute | solution.py:284
  10.7 1.2 %collective-permute-start.2 = (bf16[56,512]{1,0:T(8,128)(2,1)S(1)}, bf16[56,512]{1,0:T(8,128)(2,1)S(1)}, u32[]{:S(2)}, u32[]{:S(2)}) collective-permute-start(bf16[56,512]{1,0:T(8,128)(2,1)S(1)} %concatenate.6.refs_0_), channel_id=1, source_target_pairs={{0,1},{1,0},{2,3},{3,2},{4,5},{5,4},{6,7},{7,6},{8,9},{9,8},{10,11... | collective-permute-start | bytes 172040 | tf_op jit(solution)/shard_map/ppermute | solution.py:284
  11.9 0.9 %collective-permute-done.4.refs_3_ = bf16[48,512]{1,0:T(8,128)(2,1)S(1)} collective-permute-done((bf16[48,512]{1,0:T(8,128)(2,1)S(1)}, bf16[48,512]{1,0:T(8,128)(2,1)S(1)}, u32[]{:S(2)}, u32[]{:S(2)}) %collective-permute-start.4) | collective-permute-done | bytes 49184 | tf_op jit(solution)/shard_map/ppermute | solution.py:284
  12.7 0.1 collective-permute-start.5
  12.9 1.7 %collective-permute-done.3.refs_2_ = bf16[56,512]{1,0:T(8,128)(2,1)S(1)} collective-permute-done((bf16[56,512]{1,0:T(8,128)(2,1)S(1)}, bf16[56,512]{1,0:T(8,128)(2,1)S(1)}, u32[]{:S(2)}, u32[]{:S(2)}) %collective-permute-start.3) | collective-permute-done | bytes 57376 | tf_op jit(solution)/shard_map/ppermute | solution.py:284
  14.5 0.4 %collective-permute-done.2.refs_1_ = bf16[56,512]{1,0:T(8,128)(2,1)S(1)} collective-permute-done((bf16[56,512]{1,0:T(8,128)(2,1)S(1)}, bf16[56,512]{1,0:T(8,128)(2,1)S(1)}, u32[]{:S(2)}, u32[]{:S(2)}) %collective-permute-start.2) | collective-permute-done | bytes 57376 | tf_op jit(solution)/shard_map/ppermute | solution.py:284
  14.9 0.0 collective-permute-done.5.refs_4_
  14.9 0.2 %meet.1 = (bf16[136,512]{1,0:T(8,128)(2,1)S(1)}, bf16[16,512]{1,0:T(8,128)(2,1)S(1)}) custom-call(bf16[56,512]{1,0:T(8,128)(2,1)S(1)} %concatenate.6.refs_0_, bf16[56,512]{1,0:T(8,128)(2,1)S(1)} %collective-permute-done.2.refs_1_, bf16[56,512]{1,0:T(8,128)(2,1)S(1)} %collective-permute-done.3.refs_2_, bf16[48,512]{1,0:T(8,128)(2,1)S(1)} %collective-permute-done.4.refs_3_, ...), custom_call_target="tpu_custom_call" | custom-call | tf_op jit(solution)/shard_map/meet/pallas_call | solution.py:22
  15.1 1.6 %collective-permute-start.6 = (bf16[136,512]{1,0:T(8,128)(2,1)S(1)}, bf16[136,512]{1,0:T(8,128)(2,1)S(1)}, u32[]{:S(2)}, u32[]{:S(2)}) collective-permute-start(bf16[136,512]{1,0:T(8,128)(2,1)S(1)} %get-tuple-element.22.docs_ref), channel_id=1, source_target_pairs={{0,8},{1,9},{2,10},{3,11},{4,12},{5,13},{6,14},{7,15},{8,0},{9,1},... | collective-permute-start | bytes 417800 | tf_op jit(solution)/shard_map/ppermute | solution.py:284
  16.7 0.0 collective-permute-start.9
  16.8 1.6 %collective-permute-start.8 = (bf16[16,512]{1,0:T(8,128)(2,1)S(1)}, bf16[16,512]{1,0:T(8,128)(2,1)S(1)}, u32[]{:S(2)}, u32[]{:S(2)}) collective-permute-start(bf16[16,512]{1,0:T(8,128)(2,1)S(1)} %get-tuple-element.21.both_ref.refs_0_), channel_id=1, source_target_pairs={{0,20},{1,21},{2,22},{3,23},{4,16},{5,17},{6,18},{7,19},{8,28},{9,... | collective-permute-start | bytes 49160 | tf_op jit(solution)/shard_map/ppermute | solution.py:284
  18.4 0.3 %first_docs.1 = (f32[16,128]{1,0:T(8,128)S(1)}, f32[16,512]{1,0:T(8,128)S(1)}) custom-call(s32[16,128]{1,0:T(8,128)S(1)} %get-tuple-element.18.place_ref, bf16[16,512]{1,0:T(8,128)(2,1)S(1)} %get-tuple-element.21.both_ref.refs_0_, bf16[136,512]{1,0:T(8,128)(2,1)S(1)} %get-tuple-element.22.docs_ref), custom_call_target="tpu_custom_call" | custom-call | tf_op jit(solution)/shard_map/first_docs/pallas_call | solution.py:22
  18.7 1.5 %collective-permute-done.6.refs_0_ = bf16[136,512]{1,0:T(8,128)(2,1)S(1)} collective-permute-done((bf16[136,512]{1,0:T(8,128)(2,1)S(1)}, bf16[136,512]{1,0:T(8,128)(2,1)S(1)}, u32[]{:S(2)}, u32[]{:S(2)}) %collective-permute-start.6) | collective-permute-done | bytes 139296 | tf_op jit(solution)/shard_map/ppermute | solution.py:284
  20.2 0.3 %share.1 = (f32[4,128]{1,0:T(4,128)S(1)}, f32[4,512]{1,0:T(4,128)S(1)}, bf16[16,512]{1,0:T(8,128)(2,1)S(1)}) custom-call(s32[16,128]{1,0:T(8,128)S(1)} %get-tuple-element.18.place_ref, bf16[16,512]{1,0:T(8,128)(2,1)S(1)} %get-tuple-element.21.both_ref.refs_0_, f32[16,128]{1,0:T(8,128)S(1)} %get-tuple-element.23.loss_ref, ...), custom_call_target="tpu_custom_call" | custom-call | tf_op jit(solution)/shard_map/share/pallas_call | solution.py:22
  20.6 0.1 collective-permute-start.7
  20.6 1.1 %collective-permute-done.9.refs_3_ = bf16[16,512]{1,0:T(8,128)(2,1)S(1)} collective-permute-done((bf16[16,512]{1,0:T(8,128)(2,1)S(1)}, bf16[16,512]{1,0:T(8,128)(2,1)S(1)}, u32[]{:S(2)}, u32[]{:S(2)}) %collective-permute-start.9) | collective-permute-done | bytes 16416 | tf_op jit(solution)/shard_map/ppermute | solution.py:284
  21.7 0.0 collective-permute-done.8.refs_2_
  21.7 0.1 collective-permute-done.7.back_ref
  21.8 0.0 copy-done
  21.8 0.9 %last.1 = (f32[1,4]{1,0:T(1,128)}, f32[4,512]{1,0:T(4,128)}, f32[16,512]{1,0:T(8,128)}) custom-call(s32[8,128]{1,0:T(8,128)S(1)} %get-tuple-element.17.at_ref, bf16[16,512]{1,0:T(8,128)(2,1)S(1)} %copy-done, f32[4,128]{1,0:T(4,128)S(1)} %get-tuple-element.25.loss_ref, f32[4,512]{1,0:T(4,128)S(1)} %get-tuple-element.26.grad_ref, ...), custom_call_target="tpu_custom_call" | custom-call | tf_op jit(solution)/shard_map/last/pallas_call | solution.py:22
  (8 shorter events, 0.1 us)
Async XLA Ops:
  0.6 21.2 %copy-start = (bf16[16,512]{1,0:T(8,128)(2,1)S(1)}, bf16[16,512]{1,0:T(8,128)(2,1)}, u32[]{:S(2)}) copy-start(bf16[16,512]{1,0:T(8,128)(2,1)} %docs_ref.1) | copy-start | bytes 49156
  0.6 7.3 %collective-permute-start = (bf16[16,512]{1,0:T(8,128)(2,1)}, bf16[16,512]{1,0:T(8,128)(2,1)S(1)}, u32[]{:S(2)}, u32[]{:S(2)}) collective-permute-start(bf16[16,512]{1,0:T(8,128)(2,1)} %docs_ref.1), channel_id=1, source_target_pairs={{0,20},{1,21},{2,22},{3,23},{4,16},{5,17},{6,18},{7,19},{8,28},{9,... | collective-permute-start | bytes 49160 | tf_op jit(solution)/shard_map/ppermute | solution.py:284
  7.2 2.9 %collective-permute-start.1 = (bf16[16,512]{1,0:T(8,128)(2,1)S(1)}, bf16[16,512]{1,0:T(8,128)(2,1)S(1)}, u32[]{:S(2)}, u32[]{:S(2)}) collective-permute-start(bf16[16,512]{1,0:T(8,128)(2,1)S(1)} %get-tuple-element.20), channel_id=1, source_target_pairs={{0,4},{4,0},{8,12},{12,8},{16,20},{20,16},{24,28},{28,24},{1,5},{5... | collective-permute-start | bytes 49160 | tf_op jit(solution)/shard_map/ppermute | solution.py:278
  7.9 4.8 %collective-permute-start.4 = (bf16[48,512]{1,0:T(8,128)(2,1)S(1)}, bf16[48,512]{1,0:T(8,128)(2,1)S(1)}, u32[]{:S(2)}, u32[]{:S(2)}) collective-permute-start(bf16[48,512]{1,0:T(8,128)(2,1)S(1)} %pad_maximum_fusion), channel_id=1, source_target_pairs={{0,7},{1,6},{2,5},{3,4},{4,3},{5,2},{6,1},{7,0},{8,15},{9,14},{10,... | collective-permute-start | bytes 147464 | tf_op jit(solution)/shard_map/ppermute | solution.py:284
  10.2 4.4 %collective-permute-start.3 = (bf16[56,512]{1,0:T(8,128)(2,1)S(1)}, bf16[56,512]{1,0:T(8,128)(2,1)S(1)}, u32[]{:S(2)}, u32[]{:S(2)}) collective-permute-start(bf16[56,512]{1,0:T(8,128)(2,1)S(1)} %concatenate.6.refs_0_), channel_id=1, source_target_pairs={{0,2},{1,3},{2,0},{3,1},{4,6},{5,7},{6,4},{7,5},{8,10},{9,11},{10,... | collective-permute-start | bytes 172040 | tf_op jit(solution)/shard_map/ppermute | solution.py:284
  10.7 4.2 %collective-permute-start.2 = (bf16[56,512]{1,0:T(8,128)(2,1)S(1)}, bf16[56,512]{1,0:T(8,128)(2,1)S(1)}, u32[]{:S(2)}, u32[]{:S(2)}) collective-permute-start(bf16[56,512]{1,0:T(8,128)(2,1)S(1)} %concatenate.6.refs_0_), channel_id=1, source_target_pairs={{0,1},{1,0},{2,3},{3,2},{4,5},{5,4},{6,7},{7,6},{8,9},{9,8},{10,11... | collective-permute-start | bytes 172040 | tf_op jit(solution)/shard_map/ppermute | solution.py:284
  12.7 2.2 %collective-permute-start.5 = (bf16[16,512]{1,0:T(8,128)(2,1)S(1)}, bf16[16,512]{1,0:T(8,128)(2,1)S(1)}, u32[]{:S(2)}, u32[]{:S(2)}) collective-permute-start(bf16[16,512]{1,0:T(8,128)(2,1)S(1)} %slice.26), channel_id=1, source_target_pairs={{0,4},{4,0},{8,12},{12,8},{16,20},{20,16},{24,28},{28,24},{1,5},{5... | collective-permute-start | bytes 49160 | tf_op jit(solution)/shard_map/ppermute | solution.py:278
  15.1 5.1 %collective-permute-start.6 = (bf16[136,512]{1,0:T(8,128)(2,1)S(1)}, bf16[136,512]{1,0:T(8,128)(2,1)S(1)}, u32[]{:S(2)}, u32[]{:S(2)}) collective-permute-start(bf16[136,512]{1,0:T(8,128)(2,1)S(1)} %get-tuple-element.22.docs_ref), channel_id=1, source_target_pairs={{0,8},{1,9},{2,10},{3,11},{4,12},{5,13},{6,14},{7,15},{8,0},{9,1},... | collective-permute-start | bytes 417800 | tf_op jit(solution)/shard_map/ppermute | solution.py:284
  16.7 5.0 %collective-permute-start.9 = (bf16[16,512]{1,0:T(8,128)(2,1)S(1)}, bf16[16,512]{1,0:T(8,128)(2,1)S(1)}, u32[]{:S(2)}, u32[]{:S(2)}) collective-permute-start(bf16[16,512]{1,0:T(8,128)(2,1)S(1)} %get-tuple-element.21.both_ref.refs_0_), channel_id=1, source_target_pairs={{0,28},{1,29},{2,30},{3,31},{4,24},{5,25},{6,26},{7,27},{8,20},{9,... | collective-permute-start | bytes 49160 | tf_op jit(solution)/shard_map/ppermute | solution.py:284
  16.8 5.0 %collective-permute-start.8 = (bf16[16,512]{1,0:T(8,128)(2,1)S(1)}, bf16[16,512]{1,0:T(8,128)(2,1)S(1)}, u32[]{:S(2)}, u32[]{:S(2)}) collective-permute-start(bf16[16,512]{1,0:T(8,128)(2,1)S(1)} %get-tuple-element.21.both_ref.refs_0_), channel_id=1, source_target_pairs={{0,20},{1,21},{2,22},{3,23},{4,16},{5,17},{6,18},{7,19},{8,28},{9,... | collective-permute-start | bytes 49160 | tf_op jit(solution)/shard_map/ppermute | solution.py:284
  20.6 1.2 %collective-permute-start.7 = (bf16[16,512]{1,0:T(8,128)(2,1)S(1)}, bf16[16,512]{1,0:T(8,128)(2,1)S(1)}, u32[]{:S(2)}, u32[]{:S(2)}) collective-permute-start(bf16[16,512]{1,0:T(8,128)(2,1)S(1)} %get-tuple-element.27), channel_id=1, source_target_pairs={{0,4},{4,0},{8,12},{12,8},{16,20},{20,16},{24,28},{28,24},{1,5},{5... | collective-permute-start | bytes 49160 | tf_op jit(solution)/shard_map/ppermute | solution.py:278

commit v10 on v9

--- a/solution.py
+++ b/solution.py
@@ -203,8 +203,9 @@
 def pair_terms(logits, positive):
     logits = logit_scale * logits + logit_shift
     signed = jnp.where(positive, -logits, logits)
-    losses = jnp.maximum(signed, 0.0) + jnp.log1p(jnp.exp(-jnp.abs(signed)))
-    slopes = jax.nn.sigmoid(signed)
+    decay = jnp.exp(-jnp.abs(signed))
+    losses = jnp.maximum(signed, 0.0) + jnp.log1p(decay)
+    slopes = jnp.where(signed < 0.0, decay, 1.0) / (1.0 + decay)
     return losses, jnp.where(positive, -slopes, slopes).astype(bf16)
 
 
@@ -240,7 +241,7 @@
     terms = [loss_high, loss_low, loss - loss_high - loss_low]
     terms.append(jnp.zeros((recs, grad.shape[1] - 384), f32))
     send_ref[...] = jnp.concatenate(
-        [grad_high, grad - grad_high, jnp.concatenate(terms, 1), jnp.zeros_like(grad)], 0
+        [grad_high, grad - grad_high, jnp.concatenate(terms, 1)], 0
     ).astype(bf16)
 
 
@@ -362,7 +363,7 @@
     )(place, both, docs)
     loss, grad, send = in_vmem(
         share_kernel,
-        (shape(recs, 128), shape(recs, width), shape(4 * recs, width, bf16)),
+        (shape(recs, 128), shape(recs, width), shape(3 * recs, width, bf16)),
         8,
         "share",
     )(place, both, loss, grad, *near)

time: 22.9 us -> 22.9 us (level)
  no operation moved by 1% of the time
where the time goes in v10:
time: 22.9 us; the launch traced here: 22.7 us
  starting transfers between devices  11.6 us (51%)
  waiting for transfers between devices  5.59 us (24%)
  Pallas kernels  4.81 us (21%)
  between operations  0.7 us (3%)
    ppermute x7, starting transfers between devices, across(): lax.ppermute(value, ('grp', 'tm'), swap_pairs(lax.axis_size('grp') * colu...  10.6 us
    ppermute x7, waiting for transfers between devices, across(): lax.ppermute(value, ('grp', 'tm'), swap_pairs(lax.axis_size('grp') * colu...  5.48 us
    pallas_call x1, Pallas kernels, body(): pl.pallas_call(lambda *refs: pool_kernel((docs_dev, is_direct(columns), d...  3 us
    pallas_call x4, Pallas kernels, call(): pl.pallas_call(kernel, out_shape=outs, in_specs=[VMEM] * len(operands), o...  1.8 us
    ppermute x3, starting transfers between devices, to_other_core(): return lax.ppermute(value, 'grp', swap_pairs(lax.axis_size('grp'), 1, 1))  0.93 us
  transfers between devices with their start and end apart: 10, of which 6 were waited for; matrix products, arithmetic and copies ran while one was open for 0% of the time, Pallas kernels for 16%

profile of v10, /device:TPU:0, one launch (start us, length us, event | category | flops | bytes accessed | tf_op | source)
XLA Modules:
  0.0 22.7 jit_solution(8582974472570321120)
XLA Ops:
  0.6 0.0 copy-start
  0.6 3.5 %collective-permute-start = (bf16[16,512]{1,0:T(8,128)(2,1)}, bf16[16,512]{1,0:T(8,128)(2,1)S(1)}, u32[]{:S(2)}, u32[]{:S(2)}) collective-permute-start(bf16[16,512]{1,0:T(8,128)(2,1)} %docs_ref.1), channel_id=1, source_target_pairs={{0,20},{1,21},{2,22},{3,23},{4,16},{5,17},{6,18},{7,19},{8,28},{9,... | collective-permute-start | bytes 49160 | tf_op jit(solution)/shard_map/ppermute | solution.py:285
  4.2 3.0 %pool.1 = (bf16[16,512]{1,0:T(8,128)(2,1)S(1)}, bf16[16,512]{1,0:T(8,128)(2,1)S(1)}, s32[16,128]{1,0:T(8,128)S(1)}, s32[8,128]{1,0:T(8,128)S(1)}) custom-call(s32[4]{0:T(128)} %refs_0_.1, s32[32]{0:T(128)} %refs_1_.1, bf16[8,1024]{1,0:T(8,128)(2,1)} %refs_2_.1, bf16[4,256,1024]{2,1,0:T(8,128)(2,1)} %refs_3_.1, bf16[1024,512]{1,0:T(8,128)(2,1)} %refs_4_.1, ...), custom_call_target="tpu_custom_call" | custom-call | tf_op jit(solution)/shard_map/pool/pallas_call | solution.py:305
  7.2 0.7 %collective-permute-start.1 = (bf16[16,512]{1,0:T(8,128)(2,1)S(1)}, bf16[16,512]{1,0:T(8,128)(2,1)S(1)}, u32[]{:S(2)}, u32[]{:S(2)}) collective-permute-start(bf16[16,512]{1,0:T(8,128)(2,1)S(1)} %get-tuple-element.20), channel_id=1, source_target_pairs={{0,4},{4,0},{8,12},{12,8},{16,20},{20,16},{24,28},{28,24},{1,5},{5... | collective-permute-start | bytes 49160 | tf_op jit(solution)/shard_map/ppermute | solution.py:279
  7.9 0.0 collective-permute-done
  7.9 2.1 %collective-permute-start.4 = (bf16[48,512]{1,0:T(8,128)(2,1)S(1)}, bf16[48,512]{1,0:T(8,128)(2,1)S(1)}, u32[]{:S(2)}, u32[]{:S(2)}) collective-permute-start(bf16[48,512]{1,0:T(8,128)(2,1)S(1)} %pad_maximum_fusion), channel_id=1, source_target_pairs={{0,7},{1,6},{2,5},{3,4},{4,3},{5,2},{6,1},{7,0},{8,15},{9,14},{10,... | collective-permute-start | bytes 147464 | tf_op jit(solution)/shard_map/ppermute | solution.py:285
  10.1 0.0 collective-permute-done.1
  10.2 0.6 %collective-permute-start.3 = (bf16[56,512]{1,0:T(8,128)(2,1)S(1)}, bf16[56,512]{1,0:T(8,128)(2,1)S(1)}, u32[]{:S(2)}, u32[]{:S(2)}) collective-permute-start(bf16[56,512]{1,0:T(8,128)(2,1)S(1)} %concatenate.6.refs_0_), channel_id=1, source_target_pairs={{0,2},{1,3},{2,0},{3,1},{4,6},{5,7},{6,4},{7,5},{8,10},{9,11},{10,... | collective-permute-start | bytes 172040 | tf_op jit(solution)/shard_map/ppermute | solution.py:285
  10.7 1.2 %collective-permute-start.2 = (bf16[56,512]{1,0:T(8,128)(2,1)S(1)}, bf16[56,512]{1,0:T(8,128)(2,1)S(1)}, u32[]{:S(2)}, u32[]{:S(2)}) collective-permute-start(bf16[56,512]{1,0:T(8,128)(2,1)S(1)} %concatenate.6.refs_0_), channel_id=1, source_target_pairs={{0,1},{1,0},{2,3},{3,2},{4,5},{5,4},{6,7},{7,6},{8,9},{9,8},{10,11... | collective-permute-start | bytes 172040 | tf_op jit(solution)/shard_map/ppermute | solution.py:285
  11.9 0.9 %collective-permute-done.4.refs_3_ = bf16[48,512]{1,0:T(8,128)(2,1)S(1)} collective-permute-done((bf16[48,512]{1,0:T(8,128)(2,1)S(1)}, bf16[48,512]{1,0:T(8,128)(2,1)S(1)}, u32[]{:S(2)}, u32[]{:S(2)}) %collective-permute-start.4) | collective-permute-done | bytes 49184 | tf_op jit(solution)/shard_map/ppermute | solution.py:285
  12.7 0.1 collective-permute-start.5
  12.9 1.7 %collective-permute-done.3.refs_2_ = bf16[56,512]{1,0:T(8,128)(2,1)S(1)} collective-permute-done((bf16[56,512]{1,0:T(8,128)(2,1)S(1)}, bf16[56,512]{1,0:T(8,128)(2,1)S(1)}, u32[]{:S(2)}, u32[]{:S(2)}) %collective-permute-start.3) | collective-permute-done | bytes 57376 | tf_op jit(solution)/shard_map/ppermute | solution.py:285
  14.5 0.4 %collective-permute-done.2.refs_1_ = bf16[56,512]{1,0:T(8,128)(2,1)S(1)} collective-permute-done((bf16[56,512]{1,0:T(8,128)(2,1)S(1)}, bf16[56,512]{1,0:T(8,128)(2,1)S(1)}, u32[]{:S(2)}, u32[]{:S(2)}) %collective-permute-start.2) | collective-permute-done | bytes 57376 | tf_op jit(solution)/shard_map/ppermute | solution.py:285
  14.9 0.0 collective-permute-done.5.refs_4_
  14.9 0.2 %meet.1 = (bf16[136,512]{1,0:T(8,128)(2,1)S(1)}, bf16[16,512]{1,0:T(8,128)(2,1)S(1)}) custom-call(bf16[56,512]{1,0:T(8,128)(2,1)S(1)} %concatenate.6.refs_0_, bf16[56,512]{1,0:T(8,128)(2,1)S(1)} %collective-permute-done.2.refs_1_, bf16[56,512]{1,0:T(8,128)(2,1)S(1)} %collective-permute-done.3.refs_2_, bf16[48,512]{1,0:T(8,128)(2,1)S(1)} %collective-permute-done.4.refs_3_, ...), custom_call_target="tpu_custom_call" | custom-call | tf_op jit(solution)/shard_map/meet/pallas_call | solution.py:22
  15.1 1.6 %collective-permute-start.6 = (bf16[136,512]{1,0:T(8,128)(2,1)S(1)}, bf16[136,512]{1,0:T(8,128)(2,1)S(1)}, u32[]{:S(2)}, u32[]{:S(2)}) collective-permute-start(bf16[136,512]{1,0:T(8,128)(2,1)S(1)} %get-tuple-element.22.docs_ref), channel_id=1, source_target_pairs={{0,8},{1,9},{2,10},{3,11},{4,12},{5,13},{6,14},{7,15},{8,0},{9,1},... | collective-permute-start | bytes 417800 | tf_op jit(solution)/shard_map/ppermute | solution.py:285
  16.7 0.0 collective-permute-start.9
  16.8 1.6 %collective-permute-start.8 = (bf16[16,512]{1,0:T(8,128)(2,1)S(1)}, bf16[16,512]{1,0:T(8,128)(2,1)S(1)}, u32[]{:S(2)}, u32[]{:S(2)}) collective-permute-start(bf16[16,512]{1,0:T(8,128)(2,1)S(1)} %get-tuple-element.21.both_ref.refs_0_), channel_id=1, source_target_pairs={{0,20},{1,21},{2,22},{3,23},{4,16},{5,17},{6,18},{7,19},{8,28},{9,... | collective-permute-start | bytes 49160 | tf_op jit(solution)/shard_map/ppermute | solution.py:285
  18.4 0.3 %first_docs.1 = (f32[16,128]{1,0:T(8,128)S(1)}, f32[16,512]{1,0:T(8,128)S(1)}) custom-call(s32[16,128]{1,0:T(8,128)S(1)} %get-tuple-element.18.place_ref, bf16[16,512]{1,0:T(8,128)(2,1)S(1)} %get-tuple-element.21.both_ref.refs_0_, bf16[136,512]{1,0:T(8,128)(2,1)S(1)} %get-tuple-element.22.docs_ref), custom_call_target="tpu_custom_call" | custom-call | tf_op jit(solution)/shard_map/first_docs/pallas_call | solution.py:22
  18.7 1.5 %collective-permute-done.6.refs_0_ = bf16[136,512]{1,0:T(8,128)(2,1)S(1)} collective-permute-done((bf16[136,512]{1,0:T(8,128)(2,1)S(1)}, bf16[136,512]{1,0:T(8,128)(2,1)S(1)}, u32[]{:S(2)}, u32[]{:S(2)}) %collective-permute-start.6) | collective-permute-done | bytes 139296 | tf_op jit(solution)/shard_map/ppermute | solution.py:285
  20.2 0.3 %share.1 = (f32[4,128]{1,0:T(4,128)S(1)}, f32[4,512]{1,0:T(4,128)S(1)}, bf16[12,512]{1,0:T(8,128)(2,1)S(1)}) custom-call(s32[16,128]{1,0:T(8,128)S(1)} %get-tuple-element.18.place_ref, bf16[16,512]{1,0:T(8,128)(2,1)S(1)} %get-tuple-element.21.both_ref.refs_0_, f32[16,128]{1,0:T(8,128)S(1)} %get-tuple-element.23.loss_ref, ...), custom_call_target="tpu_custom_call" | custom-call | tf_op jit(solution)/shard_map/share/pallas_call | solution.py:22
  20.6 0.1 collective-permute-start.7
  20.7 1.1 %collective-permute-done.9.refs_3_ = bf16[16,512]{1,0:T(8,128)(2,1)S(1)} collective-permute-done((bf16[16,512]{1,0:T(8,128)(2,1)S(1)}, bf16[16,512]{1,0:T(8,128)(2,1)S(1)}, u32[]{:S(2)}, u32[]{:S(2)}) %collective-permute-start.9) | collective-permute-done | bytes 16416 | tf_op jit(solution)/shard_map/ppermute | solution.py:285
  21.7 0.0 collective-permute-done.8.refs_2_
  21.7 0.1 collective-permute-done.7.back_ref
  21.8 0.0 copy-done
  21.8 0.9 %last.1 = (f32[1,4]{1,0:T(1,128)}, f32[4,512]{1,0:T(4,128)}, f32[16,512]{1,0:T(8,128)}) custom-call(s32[8,128]{1,0:T(8,128)S(1)} %get-tuple-element.17.at_ref, bf16[16,512]{1,0:T(8,128)(2,1)S(1)} %copy-done, f32[4,128]{1,0:T(4,128)S(1)} %get-tuple-element.25.loss_ref, f32[4,512]{1,0:T(4,128)S(1)} %get-tuple-element.26.grad_ref, ...), custom_call_target="tpu_custom_call" | custom-call | tf_op jit(solution)/shard_map/last/pallas_call | solution.py:22
  (8 shorter events, 0.1 us)
Async XLA Ops:
  0.6 21.2 %copy-start = (bf16[16,512]{1,0:T(8,128)(2,1)S(1)}, bf16[16,512]{1,0:T(8,128)(2,1)}, u32[]{:S(2)}) copy-start(bf16[16,512]{1,0:T(8,128)(2,1)} %docs_ref.1) | copy-start | bytes 49156
  0.6 7.3 %collective-permute-start = (bf16[16,512]{1,0:T(8,128)(2,1)}, bf16[16,512]{1,0:T(8,128)(2,1)S(1)}, u32[]{:S(2)}, u32[]{:S(2)}) collective-permute-start(bf16[16,512]{1,0:T(8,128)(2,1)} %docs_ref.1), channel_id=1, source_target_pairs={{0,20},{1,21},{2,22},{3,23},{4,16},{5,17},{6,18},{7,19},{8,28},{9,... | collective-permute-start | bytes 49160 | tf_op jit(solution)/shard_map/ppermute | solution.py:285
  7.2 2.9 %collective-permute-start.1 = (bf16[16,512]{1,0:T(8,128)(2,1)S(1)}, bf16[16,512]{1,0:T(8,128)(2,1)S(1)}, u32[]{:S(2)}, u32[]{:S(2)}) collective-permute-start(bf16[16,512]{1,0:T(8,128)(2,1)S(1)} %get-tuple-element.20), channel_id=1, source_target_pairs={{0,4},{4,0},{8,12},{12,8},{16,20},{20,16},{24,28},{28,24},{1,5},{5... | collective-permute-start | bytes 49160 | tf_op jit(solution)/shard_map/ppermute | solution.py:279
  7.9 4.8 %collective-permute-start.4 = (bf16[48,512]{1,0:T(8,128)(2,1)S(1)}, bf16[48,512]{1,0:T(8,128)(2,1)S(1)}, u32[]{:S(2)}, u32[]{:S(2)}) collective-permute-start(bf16[48,512]{1,0:T(8,128)(2,1)S(1)} %pad_maximum_fusion), channel_id=1, source_target_pairs={{0,7},{1,6},{2,5},{3,4},{4,3},{5,2},{6,1},{7,0},{8,15},{9,14},{10,... | collective-permute-start | bytes 147464 | tf_op jit(solution)/shard_map/ppermute | solution.py:285
  10.2 4.4 %collective-permute-start.3 = (bf16[56,512]{1,0:T(8,128)(2,1)S(1)}, bf16[56,512]{1,0:T(8,128)(2,1)S(1)}, u32[]{:S(2)}, u32[]{:S(2)}) collective-permute-start(bf16[56,512]{1,0:T(8,128)(2,1)S(1)} %concatenate.6.refs_0_), channel_id=1, source_target_pairs={{0,2},{1,3},{2,0},{3,1},{4,6},{5,7},{6,4},{7,5},{8,10},{9,11},{10,... | collective-permute-start | bytes 172040 | tf_op jit(solution)/shard_map/ppermute | solution.py:285
  10.7 4.2 %collective-permute-start.2 = (bf16[56,512]{1,0:T(8,128)(2,1)S(1)}, bf16[56,512]{1,0:T(8,128)(2,1)S(1)}, u32[]{:S(2)}, u32[]{:S(2)}) collective-permute-start(bf16[56,512]{1,0:T(8,128)(2,1)S(1)} %concatenate.6.refs_0_), channel_id=1, source_target_pairs={{0,1},{1,0},{2,3},{3,2},{4,5},{5,4},{6,7},{7,6},{8,9},{9,8},{10,11... | collective-permute-start | bytes 172040 | tf_op jit(solution)/shard_map/ppermute | solution.py:285
  12.7 2.2 %collective-permute-start.5 = (bf16[16,512]{1,0:T(8,128)(2,1)S(1)}, bf16[16,512]{1,0:T(8,128)(2,1)S(1)}, u32[]{:S(2)}, u32[]{:S(2)}) collective-permute-start(bf16[16,512]{1,0:T(8,128)(2,1)S(1)} %slice.26), channel_id=1, source_target_pairs={{0,4},{4,0},{8,12},{12,8},{16,20},{20,16},{24,28},{28,24},{1,5},{5... | collective-permute-start | bytes 49160 | tf_op jit(solution)/shard_map/ppermute | solution.py:279
  15.1 5.1 %collective-permute-start.6 = (bf16[136,512]{1,0:T(8,128)(2,1)S(1)}, bf16[136,512]{1,0:T(8,128)(2,1)S(1)}, u32[]{:S(2)}, u32[]{:S(2)}) collective-permute-start(bf16[136,512]{1,0:T(8,128)(2,1)S(1)} %get-tuple-element.22.docs_ref), channel_id=1, source_target_pairs={{0,8},{1,9},{2,10},{3,11},{4,12},{5,13},{6,14},{7,15},{8,0},{9,1},... | collective-permute-start | bytes 417800 | tf_op jit(solution)/shard_map/ppermute | solution.py:285
  16.7 5.0 %collective-permute-start.9 = (bf16[16,512]{1,0:T(8,128)(2,1)S(1)}, bf16[16,512]{1,0:T(8,128)(2,1)S(1)}, u32[]{:S(2)}, u32[]{:S(2)}) collective-permute-start(bf16[16,512]{1,0:T(8,128)(2,1)S(1)} %get-tuple-element.21.both_ref.refs_0_), channel_id=1, source_target_pairs={{0,28},{1,29},{2,30},{3,31},{4,24},{5,25},{6,26},{7,27},{8,20},{9,... | collective-permute-start | bytes 49160 | tf_op jit(solution)/shard_map/ppermute | solution.py:285
  16.8 5.0 %collective-permute-start.8 = (bf16[16,512]{1,0:T(8,128)(2,1)S(1)}, bf16[16,512]{1,0:T(8,128)(2,1)S(1)}, u32[]{:S(2)}, u32[]{:S(2)}) collective-permute-start(bf16[16,512]{1,0:T(8,128)(2,1)S(1)} %get-tuple-element.21.both_ref.refs_0_), channel_id=1, source_target_pairs={{0,20},{1,21},{2,22},{3,23},{4,16},{5,17},{6,18},{7,19},{8,28},{9,... | collective-permute-start | bytes 49160 | tf_op jit(solution)/shard_map/ppermute | solution.py:285
  20.6 1.2 %collective-permute-start.7 = (bf16[12,512]{1,0:T(8,128)(2,1)S(1)}, bf16[12,512]{1,0:T(8,128)(2,1)S(1)}, u32[]{:S(2)}, u32[]{:S(2)}) collective-permute-start(bf16[12,512]{1,0:T(8,128)(2,1)S(1)} %get-tuple-element.27), channel_id=1, source_target_pairs={{0,4},{4,0},{8,12},{12,8},{16,20},{20,16},{24,28},{28,24},{1,5},{5... | collective-permute-start | bytes 36872 | tf_op jit(solution)/shard_map/ppermute | solution.py:279

commit v11 on v9

--- a/solution.py
+++ b/solution.py
@@ -299,7 +299,7 @@
     blocks = []
     if direct:
         blocks = [(0, 0), (0, 1), None, None, (1, 0), (1, 1)]
-        blocks += [(steps, flip) for steps in order for flip in (1, 0)]
+        blocks += [(steps, flip) for steps in order for flip in (steps % 2, 1 - steps % 2)]
         far = across(doc_embed, 2, 0, 1)
     docs, pools, place, at = pl.pallas_call(
         lambda *refs: pool_kernel((docs_dev, is_direct(columns), direct), blocks, *refs),
@@ -349,7 +349,7 @@
     docs, near = own, []
     if direct:
         near = [across(own, 1, 0)]
-        beyond = [across(both, steps, 0, 1) for steps in order]
+        beyond = [across(both, steps, 0, steps % 2) for steps in order]
     else:
         same_core = [[2 * n + core for n in range(layers)] for core in range(2)]
         docs = lax.all_gather(own[:doc_rows], "grp", axis_index_groups=same_core, tiled=True)

time: 22.9 us -> 22.9 us (level)
  transfers between devices with their start and end apart: 10 -> 10, of which waited for: 6 -> 5; matrix products, arithmetic and copies ran while one was open for 0% -> 0% of each run, Pallas kernels for 16% -> 16%
where the time goes in v11:
time: 22.9 us; the launch traced here: 22.7 us
  starting transfers between devices  11.4 us (50%)
  waiting for transfers between devices  5.72 us (25%)
  Pallas kernels  4.78 us (21%)
  between operations  0.7 us (3%)
    ppermute x7, starting transfers between devices, across(): lax.ppermute(value, ('grp', 'tm'), swap_pairs(lax.axis_size('grp') * colu...  10.5 us
    ppermute x7, waiting for transfers between devices, across(): lax.ppermute(value, ('grp', 'tm'), swap_pairs(lax.axis_size('grp') * colu...  5.67 us
    pallas_call x1, Pallas kernels, body(): pl.pallas_call(lambda *refs: pool_kernel((docs_dev, is_direct(columns), d...  3 us
    pallas_call x4, Pallas kernels, call(): pl.pallas_call(kernel, out_shape=outs, in_specs=[VMEM] * len(operands), o...  1.78 us
    ppermute x3, starting transfers between devices, to_other_core(): return lax.ppermute(value, 'grp', swap_pairs(lax.axis_size('grp'), 1, 1))  0.93 us
  transfers between devices with their start and end apart: 10, of which 5 were waited for; matrix products, arithmetic and copies ran while one was open for 0% of the time, Pallas kernels for 16%

profile of v11, /device:TPU:0, one launch (start us, length us, event | category | flops | bytes accessed | tf_op | source)
XLA Modules:
  0.0 22.7 jit_solution(853601648094763820)
XLA Ops:
  0.6 0.0 copy-start
  0.6 3.5 %collective-permute-start = (bf16[16,512]{1,0:T(8,128)(2,1)}, bf16[16,512]{1,0:T(8,128)(2,1)S(1)}, u32[]{:S(2)}, u32[]{:S(2)}) collective-permute-start(bf16[16,512]{1,0:T(8,128)(2,1)} %docs_ref.1), channel_id=1, source_target_pairs={{0,20},{1,21},{2,22},{3,23},{4,16},{5,17},{6,18},{7,19},{8,28},{9,... | collective-permute-start | bytes 49160 | tf_op jit(solution)/shard_map/ppermute | solution.py:284
  4.2 3.0 %pool.1 = (bf16[16,512]{1,0:T(8,128)(2,1)S(1)}, bf16[16,512]{1,0:T(8,128)(2,1)S(1)}, s32[16,128]{1,0:T(8,128)S(1)}, s32[8,128]{1,0:T(8,128)S(1)}) custom-call(s32[4]{0:T(128)} %refs_0_.1, s32[32]{0:T(128)} %refs_1_.1, bf16[8,1024]{1,0:T(8,128)(2,1)} %refs_2_.1, bf16[4,256,1024]{2,1,0:T(8,128)(2,1)} %refs_3_.1, bf16[1024,512]{1,0:T(8,128)(2,1)} %refs_4_.1, ...), custom_call_target="tpu_custom_call" | custom-call | tf_op jit(solution)/shard_map/pool/pallas_call | solution.py:304
  7.2 0.7 %collective-permute-start.1 = (bf16[16,512]{1,0:T(8,128)(2,1)S(1)}, bf16[16,512]{1,0:T(8,128)(2,1)S(1)}, u32[]{:S(2)}, u32[]{:S(2)}) collective-permute-start(bf16[16,512]{1,0:T(8,128)(2,1)S(1)} %get-tuple-element.20), channel_id=1, source_target_pairs={{0,4},{4,0},{8,12},{12,8},{16,20},{20,16},{24,28},{28,24},{1,5},{5... | collective-permute-start | bytes 49160 | tf_op jit(solution)/shard_map/ppermute | solution.py:278
  7.9 0.0 collective-permute-done
  7.9 2.1 %collective-permute-start.4 = (bf16[48,512]{1,0:T(8,128)(2,1)S(1)}, bf16[48,512]{1,0:T(8,128)(2,1)S(1)}, u32[]{:S(2)}, u32[]{:S(2)}) collective-permute-start(bf16[48,512]{1,0:T(8,128)(2,1)S(1)} %pad_maximum_fusion), channel_id=1, source_target_pairs={{0,7},{1,6},{2,5},{3,4},{4,3},{5,2},{6,1},{7,0},{8,15},{9,14},{10,... | collective-permute-start | bytes 147464 | tf_op jit(solution)/shard_map/ppermute | solution.py:284
  10.1 0.0 collective-permute-done.1
  10.2 0.6 %collective-permute-start.3 = (bf16[56,512]{1,0:T(8,128)(2,1)S(1)}, bf16[56,512]{1,0:T(8,128)(2,1)S(1)}, u32[]{:S(2)}, u32[]{:S(2)}) collective-permute-start(bf16[56,512]{1,0:T(8,128)(2,1)S(1)} %concatenate.6.refs_0_), channel_id=1, source_target_pairs={{0,2},{1,3},{2,0},{3,1},{4,6},{5,7},{6,4},{7,5},{8,10},{9,11},{10,... | collective-permute-start | bytes 172040 | tf_op jit(solution)/shard_map/ppermute | solution.py:284
  10.7 1.2 %collective-permute-start.2 = (bf16[56,512]{1,0:T(8,128)(2,1)S(1)}, bf16[56,512]{1,0:T(8,128)(2,1)S(1)}, u32[]{:S(2)}, u32[]{:S(2)}) collective-permute-start(bf16[56,512]{1,0:T(8,128)(2,1)S(1)} %concatenate.6.refs_0_), channel_id=1, source_target_pairs={{0,1},{1,0},{2,3},{3,2},{4,5},{5,4},{6,7},{7,6},{8,9},{9,8},{10,11... | collective-permute-start | bytes 172040 | tf_op jit(solution)/shard_map/ppermute | solution.py:284
  11.9 0.9 %collective-permute-done.4.refs_3_ = bf16[48,512]{1,0:T(8,128)(2,1)S(1)} collective-permute-done((bf16[48,512]{1,0:T(8,128)(2,1)S(1)}, bf16[48,512]{1,0:T(8,128)(2,1)S(1)}, u32[]{:S(2)}, u32[]{:S(2)}) %collective-permute-start.4) | collective-permute-done | bytes 49184 | tf_op jit(solution)/shard_map/ppermute | solution.py:284
  12.7 0.1 collective-permute-start.5
  12.9 1.7 %collective-permute-done.3.refs_2_ = bf16[56,512]{1,0:T(8,128)(2,1)S(1)} collective-permute-done((bf16[56,512]{1,0:T(8,128)(2,1)S(1)}, bf16[56,512]{1,0:T(8,128)(2,1)S(1)}, u32[]{:S(2)}, u32[]{:S(2)}) %collective-permute-start.3) | collective-permute-done | bytes 57376 | tf_op jit(solution)/shard_map/ppermute | solution.py:284
  14.5 0.4 %collective-permute-done.2.refs_1_ = bf16[56,512]{1,0:T(8,128)(2,1)S(1)} collective-permute-done((bf16[56,512]{1,0:T(8,128)(2,1)S(1)}, bf16[56,512]{1,0:T(8,128)(2,1)S(1)}, u32[]{:S(2)}, u32[]{:S(2)}) %collective-permute-start.2) | collective-permute-done | bytes 57376 | tf_op jit(solution)/shard_map/ppermute | solution.py:284
  14.9 0.0 collective-permute-done.5.refs_4_
  14.9 0.2 %meet.1 = (bf16[136,512]{1,0:T(8,128)(2,1)S(1)}, bf16[16,512]{1,0:T(8,128)(2,1)S(1)}) custom-call(bf16[56,512]{1,0:T(8,128)(2,1)S(1)} %concatenate.6.refs_0_, bf16[56,512]{1,0:T(8,128)(2,1)S(1)} %collective-permute-done.2.refs_1_, bf16[56,512]{1,0:T(8,128)(2,1)S(1)} %collective-permute-done.3.refs_2_, bf16[48,512]{1,0:T(8,128)(2,1)S(1)} %collective-permute-done.4.refs_3_, ...), custom_call_target="tpu_custom_call" | custom-call | tf_op jit(solution)/shard_map/meet/pallas_call | solution.py:22
  15.1 1.6 %collective-permute-start.6 = (bf16[136,512]{1,0:T(8,128)(2,1)S(1)}, bf16[136,512]{1,0:T(8,128)(2,1)S(1)}, u32[]{:S(2)}, u32[]{:S(2)}) collective-permute-start(bf16[136,512]{1,0:T(8,128)(2,1)S(1)} %get-tuple-element.22.docs_ref), channel_id=1, source_target_pairs={{0,8},{1,9},{2,10},{3,11},{4,12},{5,13},{6,14},{7,15},{8,0},{9,1},... | collective-permute-start | bytes 417800 | tf_op jit(solution)/shard_map/ppermute | solution.py:284
  16.7 0.0 collective-permute-start.9
  16.8 1.5 %collective-permute-start.8 = (bf16[16,512]{1,0:T(8,128)(2,1)S(1)}, bf16[16,512]{1,0:T(8,128)(2,1)S(1)}, u32[]{:S(2)}, u32[]{:S(2)}) collective-permute-start(bf16[16,512]{1,0:T(8,128)(2,1)S(1)} %get-tuple-element.21.both_ref.refs_0_), channel_id=1, source_target_pairs={{0,16},{1,17},{2,18},{3,19},{4,20},{5,21},{6,22},{7,23},{8,24},{9,... | collective-permute-start | bytes 49160 | tf_op jit(solution)/shard_map/ppermute | solution.py:284
  18.3 0.3 %first_docs.1 = (f32[16,128]{1,0:T(8,128)S(1)}, f32[16,512]{1,0:T(8,128)S(1)}) custom-call(s32[16,128]{1,0:T(8,128)S(1)} %get-tuple-element.18.place_ref, bf16[16,512]{1,0:T(8,128)(2,1)S(1)} %get-tuple-element.21.both_ref.refs_0_, bf16[136,512]{1,0:T(8,128)(2,1)S(1)} %get-tuple-element.22.docs_ref), custom_call_target="tpu_custom_call" | custom-call | tf_op jit(solution)/shard_map/first_docs/pallas_call | solution.py:22
  18.6 1.6 %collective-permute-done.6.refs_0_ = bf16[136,512]{1,0:T(8,128)(2,1)S(1)} collective-permute-done((bf16[136,512]{1,0:T(8,128)(2,1)S(1)}, bf16[136,512]{1,0:T(8,128)(2,1)S(1)}, u32[]{:S(2)}, u32[]{:S(2)}) %collective-permute-start.6) | collective-permute-done | bytes 139296 | tf_op jit(solution)/shard_map/ppermute | solution.py:284
  20.2 0.3 %share.1 = (f32[4,128]{1,0:T(4,128)S(1)}, f32[4,512]{1,0:T(4,128)S(1)}, bf16[16,512]{1,0:T(8,128)(2,1)S(1)}) custom-call(s32[16,128]{1,0:T(8,128)S(1)} %get-tuple-element.18.place_ref, bf16[16,512]{1,0:T(8,128)(2,1)S(1)} %get-tuple-element.21.both_ref.refs_0_, f32[16,128]{1,0:T(8,128)S(1)} %get-tuple-element.23.loss_ref, ...), custom_call_target="tpu_custom_call" | custom-call | tf_op jit(solution)/shard_map/share/pallas_call | solution.py:22
  20.6 0.1 collective-permute-start.7
  20.6 1.1 %collective-permute-done.9.refs_3_ = bf16[16,512]{1,0:T(8,128)(2,1)S(1)} collective-permute-done((bf16[16,512]{1,0:T(8,128)(2,1)S(1)}, bf16[16,512]{1,0:T(8,128)(2,1)S(1)}, u32[]{:S(2)}, u32[]{:S(2)}) %collective-permute-start.9) | collective-permute-done | bytes 16416 | tf_op jit(solution)/shard_map/ppermute | solution.py:284
  21.8 0.0 collective-permute-done.8.refs_2_
  21.8 0.0 collective-permute-done.7.back_ref
  21.8 0.0 copy-done
  21.8 0.9 %last.1 = (f32[1,4]{1,0:T(1,128)}, f32[4,512]{1,0:T(4,128)}, f32[16,512]{1,0:T(8,128)}) custom-call(s32[8,128]{1,0:T(8,128)S(1)} %get-tuple-element.17.at_ref, bf16[16,512]{1,0:T(8,128)(2,1)S(1)} %copy-done, f32[4,128]{1,0:T(4,128)S(1)} %get-tuple-element.25.loss_ref, f32[4,512]{1,0:T(4,128)S(1)} %get-tuple-element.26.grad_ref, ...), custom_call_target="tpu_custom_call" | custom-call | tf_op jit(solution)/shard_map/last/pallas_call | solution.py:22
  (8 shorter events, 0.1 us)
Async XLA Ops:
  0.6 21.2 %copy-start = (bf16[16,512]{1,0:T(8,128)(2,1)S(1)}, bf16[16,512]{1,0:T(8,128)(2,1)}, u32[]{:S(2)}) copy-start(bf16[16,512]{1,0:T(8,128)(2,1)} %docs_ref.1) | copy-start | bytes 49156
  0.6 7.3 %collective-permute-start = (bf16[16,512]{1,0:T(8,128)(2,1)}, bf16[16,512]{1,0:T(8,128)(2,1)S(1)}, u32[]{:S(2)}, u32[]{:S(2)}) collective-permute-start(bf16[16,512]{1,0:T(8,128)(2,1)} %docs_ref.1), channel_id=1, source_target_pairs={{0,20},{1,21},{2,22},{3,23},{4,16},{5,17},{6,18},{7,19},{8,28},{9,... | collective-permute-start | bytes 49160 | tf_op jit(solution)/shard_map/ppermute | solution.py:284
  7.2 2.9 %collective-permute-start.1 = (bf16[16,512]{1,0:T(8,128)(2,1)S(1)}, bf16[16,512]{1,0:T(8,128)(2,1)S(1)}, u32[]{:S(2)}, u32[]{:S(2)}) collective-permute-start(bf16[16,512]{1,0:T(8,128)(2,1)S(1)} %get-tuple-element.20), channel_id=1, source_target_pairs={{0,4},{4,0},{8,12},{12,8},{16,20},{20,16},{24,28},{28,24},{1,5},{5... | collective-permute-start | bytes 49160 | tf_op jit(solution)/shard_map/ppermute | solution.py:278
  7.9 4.8 %collective-permute-start.4 = (bf16[48,512]{1,0:T(8,128)(2,1)S(1)}, bf16[48,512]{1,0:T(8,128)(2,1)S(1)}, u32[]{:S(2)}, u32[]{:S(2)}) collective-permute-start(bf16[48,512]{1,0:T(8,128)(2,1)S(1)} %pad_maximum_fusion), channel_id=1, source_target_pairs={{0,7},{1,6},{2,5},{3,4},{4,3},{5,2},{6,1},{7,0},{8,15},{9,14},{10,... | collective-permute-start | bytes 147464 | tf_op jit(solution)/shard_map/ppermute | solution.py:284
  10.2 4.4 %collective-permute-start.3 = (bf16[56,512]{1,0:T(8,128)(2,1)S(1)}, bf16[56,512]{1,0:T(8,128)(2,1)S(1)}, u32[]{:S(2)}, u32[]{:S(2)}) collective-permute-start(bf16[56,512]{1,0:T(8,128)(2,1)S(1)} %concatenate.6.refs_0_), channel_id=1, source_target_pairs={{0,2},{1,3},{2,0},{3,1},{4,6},{5,7},{6,4},{7,5},{8,10},{9,11},{10,... | collective-permute-start | bytes 172040 | tf_op jit(solution)/shard_map/ppermute | solution.py:284
  10.7 4.2 %collective-permute-start.2 = (bf16[56,512]{1,0:T(8,128)(2,1)S(1)}, bf16[56,512]{1,0:T(8,128)(2,1)S(1)}, u32[]{:S(2)}, u32[]{:S(2)}) collective-permute-start(bf16[56,512]{1,0:T(8,128)(2,1)S(1)} %concatenate.6.refs_0_), channel_id=1, source_target_pairs={{0,1},{1,0},{2,3},{3,2},{4,5},{5,4},{6,7},{7,6},{8,9},{9,8},{10,11... | collective-permute-start | bytes 172040 | tf_op jit(solution)/shard_map/ppermute | solution.py:284
  12.7 2.2 %collective-permute-start.5 = (bf16[16,512]{1,0:T(8,128)(2,1)S(1)}, bf16[16,512]{1,0:T(8,128)(2,1)S(1)}, u32[]{:S(2)}, u32[]{:S(2)}) collective-permute-start(bf16[16,512]{1,0:T(8,128)(2,1)S(1)} %slice.26), channel_id=1, source_target_pairs={{0,4},{4,0},{8,12},{12,8},{16,20},{20,16},{24,28},{28,24},{1,5},{5... | collective-permute-start | bytes 49160 | tf_op jit(solution)/shard_map/ppermute | solution.py:278
  15.1 5.1 %collective-permute-start.6 = (bf16[136,512]{1,0:T(8,128)(2,1)S(1)}, bf16[136,512]{1,0:T(8,128)(2,1)S(1)}, u32[]{:S(2)}, u32[]{:S(2)}) collective-permute-start(bf16[136,512]{1,0:T(8,128)(2,1)S(1)} %get-tuple-element.22.docs_ref), channel_id=1, source_target_pairs={{0,8},{1,9},{2,10},{3,11},{4,12},{5,13},{6,14},{7,15},{8,0},{9,1},... | collective-permute-start | bytes 417800 | tf_op jit(solution)/shard_map/ppermute | solution.py:284
  16.7 5.0 %collective-permute-start.9 = (bf16[16,512]{1,0:T(8,128)(2,1)S(1)}, bf16[16,512]{1,0:T(8,128)(2,1)S(1)}, u32[]{:S(2)}, u32[]{:S(2)}) collective-permute-start(bf16[16,512]{1,0:T(8,128)(2,1)S(1)} %get-tuple-element.21.both_ref.refs_0_), channel_id=1, source_target_pairs={{0,28},{1,29},{2,30},{3,31},{4,24},{5,25},{6,26},{7,27},{8,20},{9,... | collective-permute-start | bytes 49160 | tf_op jit(solution)/shard_map/ppermute | solution.py:284
  16.8 5.0 %collective-permute-start.8 = (bf16[16,512]{1,0:T(8,128)(2,1)S(1)}, bf16[16,512]{1,0:T(8,128)(2,1)S(1)}, u32[]{:S(2)}, u32[]{:S(2)}) collective-permute-start(bf16[16,512]{1,0:T(8,128)(2,1)S(1)} %get-tuple-element.21.both_ref.refs_0_), channel_id=1, source_target_pairs={{0,16},{1,17},{2,18},{3,19},{4,20},{5,21},{6,22},{7,23},{8,24},{9,... | collective-permute-start | bytes 49160 | tf_op jit(solution)/shard_map/ppermute | solution.py:284
  20.6 1.2 %collective-permute-start.7 = (bf16[16,512]{1,0:T(8,128)(2,1)S(1)}, bf16[16,512]{1,0:T(8,128)(2,1)S(1)}, u32[]{:S(2)}, u32[]{:S(2)}) collective-permute-start(bf16[16,512]{1,0:T(8,128)(2,1)S(1)} %get-tuple-element.27), channel_id=1, source_target_pairs={{0,4},{4,0},{8,12},{12,8},{16,20},{20,16},{24,28},{28,24},{1,5},{5... | collective-permute-start | bytes 49160 | tf_op jit(solution)/shard_map/ppermute | solution.py:278
